TPU v7x, 32 devices: a whole 2x2x4 slice. The times are simulated.
32 devices in a mesh: leaf: 8 (over z, y), rhs: 4 (over x, core).
Axes of the slice: x: 2, y: 2, z: 4, core: 2. Of those that a mesh axis runs over, the one named last changes fastest.
Arguments:
- leaf_rhs: bfloat16 [1024, 8192], P('rhs', 'leaf'), parts along dimension 0, may hold values from -6 to 6
- sep_rhs: bfloat16 [1024, 2048], P('rhs', 'leaf'), parts along dimension 0, may hold values from -6 to 6
- leaf_inverse: bfloat16 [8192, 1024], P('leaf'), may hold values from -1.4 to 1.4, as said below
- leaf_update: bfloat16 [8, 3, 1024, 128], P('leaf'), may hold values from -1 to 1
- leaf_panel: int32 [8, 3], P('leaf'), may hold values from 0 to 1
- sep_inverse: bfloat16 [2048, 256], P('leaf'), may hold values from -1.4 to 1.4, as said below
- sep_update: bfloat16 [8, 3, 256, 128], P('leaf'), may hold values from -1 to 1
- sep_panel: int32 [8, 3], P('leaf'), may hold values from 0 to 1
Outputs:
- leaf_solution: float32 [1024, 8192], P('rhs', 'leaf'), parts along dimension 0
- sep_solution: float32 [1024, 2048], P('rhs', 'leaf'), parts along dimension 0
There are 4 independent parts, one for each index of `rhs`. A program takes and returns all parts, laid end to end along the dimension named above; an argument that names none is the same for every part. Nothing has to cross between parts.
Inputs may be any that keep to these rules, and one draw needn't show every extreme that they name: `leaf_inverse`: each diagonal 1024 x 1024 block is lower triangular with diagonal entries between 0.6 and 1.4. `sep_inverse`: each diagonal 256 x 256 block is lower triangular with diagonal entries between 0.6 and 1.4.
All inputs are finite; a program needn't handle non-finite values.
Results may differ from a plain program's by a relative error of at most 0.0047.
Values may be sent and summed in bfloat16 or wider, within the bound.
No kernel may reach another device: no remote copies, remote signals or barrier semaphores. Data moves between devices by JAX's collectives and lax.ppermute only.
A program may use at most 64 MiB of HBM per device.

v0:
```python
from functools import partial

import jax
import jax.numpy as jnp
from jax import lax
from jax.sharding import PartitionSpec as P

contract_last = (((1,), (1,)), ((), ()))


def partner(block, axis, distance):
    count = lax.axis_size(axis)
    route = []
    for low in range(count):
        high = low | 1 << distance
        if high != low and high < count:
            route += [(low, high), (high, low)]
    return lax.ppermute(block, axis, route)


def for_sending(array):

    def short(part):
        return part.astype(jnp.bfloat16) if part.dtype == jnp.float32 else part

    return jax.tree.map(short, array)


def shifted(block, axis, distance):
    devices = range(lax.axis_size(axis))
    route = [(i - distance, i) for i in devices if i - distance in devices]
    return lax.ppermute(block, axis, route)


def place_panels(updates, panel_ids, sep_rows):
    panel_rows = updates.shape[2]
    panel_count = sep_rows // panel_rows
    selector = (panel_ids[:, None] == jnp.arange(panel_count, dtype=jnp.int32)[None, :]).astype(
        jnp.float32
    )
    spread = updates[:, :, None, :] * selector[:, None, :, None]
    return spread.reshape(updates.shape[0], updates.shape[1], sep_rows)


def pick_panels(vectors, panel_ids, panel_rows):
    panel_count = vectors.shape[2] // panel_rows
    divided = vectors.reshape(vectors.shape[0], vectors.shape[1], panel_count, panel_rows)
    selector = (panel_ids[:, None] == jnp.arange(panel_count, dtype=jnp.int32)[None, :]).astype(
        vectors.dtype
    )
    return jnp.sum(divided * selector[:, None, :, None], axis=2).astype(vectors.dtype)


def solve_upward(tree_level, level_count, factors_now, pending_now):
    residual = factors_now[0].astype(jnp.float32) - pending_now
    solved = lax.dot_general(
        residual.astype(jnp.bfloat16),
        factors_now[1],
        contract_last,
        preferred_element_type=jnp.float32,
    )
    if tree_level + 1 < level_count:
        updates = jnp.einsum(
            "rs,lsp->lrp",
            solved.astype(jnp.bfloat16),
            factors_now[2][tree_level + 1 :],
            preferred_element_type=jnp.float32,
        )
        return (solved, updates)
    return (solved, None)


def skip_upward(tree_level, level_count, row_count, sep_rows, panel_rows):
    solved = jnp.zeros((row_count, sep_rows), jnp.float32)
    if tree_level + 1 < level_count:
        return (
            solved,
            jnp.zeros((level_count - tree_level - 1, row_count, panel_rows), jnp.float32),
        )
    return (solved, None)


def solve_downward(tree_level, factors_now, solved_now, ancestors, panel_rows):
    residual = solved_now
    if ancestors is not None:
        picked = pick_panels(ancestors, factors_now[3][tree_level + 1 :], panel_rows)
        residual = solved_now - jnp.einsum(
            "arp,asp->rs",
            picked,
            factors_now[2][tree_level + 1 :],
            preferred_element_type=jnp.float32,
        )
    return jnp.dot(
        residual.astype(jnp.bfloat16), factors_now[1], preferred_element_type=jnp.float32
    )


def local(
    leaf_rhs, sep_rhs, leaf_inverse, leaf_update, leaf_panel, sep_inverse, sep_update, sep_panel
):
    level_count = lax.axis_size("leaf").bit_length() - 1
    position_id = lax.axis_index("leaf")
    sep_rows = sep_inverse.shape[0]
    panel_rows = leaf_update.shape[3]
    scenarios = leaf_rhs.shape[0]
    leaf_weights = leaf_update[0]
    leaf_panels = leaf_panel[0]
    own_factors = (sep_rhs, sep_inverse, sep_update[0], sep_panel[0])
    leaf_solved = lax.dot_general(
        leaf_rhs, leaf_inverse, contract_last, preferred_element_type=jnp.float32
    )
    leaf_terms = jnp.einsum(
        "rb,lbp->lrp",
        leaf_solved.astype(jnp.bfloat16),
        leaf_weights,
        preferred_element_type=jnp.float32,
    )
    pending = place_panels(leaf_terms, leaf_panels, sep_rows)
    factor_list = []
    owner_flags = []
    last_flags = []
    active_flags = []
    solved_list = []
    for tree_level in range(level_count):
        group_mask = (1 << tree_level + 1) - 1
        position = jnp.bitwise_and(position_id, group_mask)
        is_owner = position == (1 << tree_level) - 1
        is_last = position == group_mask
        current = pending[tree_level]
        for bit_number in range(tree_level + 1):
            current = current + partner(current, "leaf", bit_number)
        solved, updates = lax.cond(
            is_owner,
            partial(solve_upward, tree_level, level_count, own_factors, current),
            partial(skip_upward, tree_level, level_count, scenarios, sep_rows, panel_rows),
        )
        if tree_level + 1 < level_count:
            additions = jnp.where(
                is_owner, place_panels(updates, own_factors[3][tree_level + 1 :], sep_rows), 0.0
            )
            pending = pending.at[tree_level + 1 :].add(additions)
        factor_list.append(own_factors)
        owner_flags.append(is_owner)
        last_flags.append(is_last)
        active_flags.append(is_owner)
        solved_list.append(solved)
    ancestors = None
    sep_out = jnp.zeros((scenarios, sep_rows), jnp.float32)
    for tree_level in reversed(range(level_count)):
        if ancestors is not None:
            fetched_values = shifted(for_sending(ancestors), "leaf", -(1 << tree_level)).astype(
                ancestors.dtype
            )
            ancestors = jnp.where(owner_flags[tree_level], fetched_values, ancestors)
        solution = lax.cond(
            active_flags[tree_level],
            partial(
                solve_downward,
                tree_level,
                factor_list[tree_level],
                solved_list[tree_level],
                ancestors,
                panel_rows,
            ),
            partial(jnp.zeros, (scenarios, sep_rows), jnp.float32),
        )
        rounded = solution.astype(jnp.bfloat16)
        arrived = shifted(rounded, "leaf", 1 << tree_level)
        newest = jnp.where(last_flags[tree_level], arrived, rounded)
        sep_out = jnp.where(owner_flags[tree_level], solution, sep_out)
        if ancestors is None:
            ancestors = newest[None]
        else:
            ancestors = jnp.concatenate([newest[None], ancestors], axis=0)
    picked = pick_panels(ancestors, leaf_panels, panel_rows)
    gathered = jnp.einsum("lrp,lbp->rb", picked, leaf_weights, preferred_element_type=jnp.float32)
    leaf_out = jnp.dot(
        (leaf_solved - gathered).astype(jnp.bfloat16),
        leaf_inverse,
        preferred_element_type=jnp.float32,
    )
    return (leaf_out, sep_out)


def solution(mesh):
    return jax.shard_map(
        local,
        mesh=mesh,
        in_specs=(
            P("rhs", "leaf"),
            P("rhs", "leaf"),
            P("leaf", None),
            P("leaf", None, None, None),
            P("leaf", None),
            P("leaf", None),
            P("leaf", None, None, None),
            P("leaf", None),
        ),
        out_specs=(P("rhs", "leaf"), P("rhs", "leaf")),
        check_vma=False,
    )
```

profile of v0, /device:TPU:18, one launch (start us, length us, event | category | flops | bytes accessed | tf_op | source)
XLA Modules:
  0.0 129.1 jit_solution(4218576449559480648)
XLA Ops:
  0.7 1.6 %copy-done = bf16[1024,1024]{1,0:T(8,128)(2,1)S(1)} copy-done((bf16[1024,1024]{1,0:T(8,128)(2,1)S(1)}, bf16[1024,1024]{1,0:T(8,128)(2,1)}, u32[]{:S(2)}) %copy-start) | copy-done | bytes 2097176
  2.2 1.8 %fusion.49 = f32[256,1024]{1,0:T(8,128)S(1)} fusion(bf16[256,1024]{1,0:T(8,128)(2,1)} %param.24, bf16[1024,1024]{1,0:T(8,128)(2,1)S(1)} %copy-done), kind=kOutput, calls=%fused_computation.73 | convolution fusion | flops 536870912 | bytes 3670016 | tf_op jit(solution)/shard_map/dot_general | solution.py:109
  8.0 2.1 %mul.110 = f32[3,256,2,128]{3,2,1,0:T(2,128)} broadcast(f32[3,256,128]{2,1,0:T(8,128)} %copy-done.4), dimensions={0,1,3} | broadcast | bytes 1179648 | tf_op jit(solution)/shard_map/mul | solution.py:41
  10.1 2.7 %mul.111 = f32[3,256,256]{2,1,0:T(8,128)} reshape(f32[3,256,2,128]{3,2,1,0:T(2,128)} %mul.110) | data formatting | bytes 1572864 | tf_op jit(solution)/shard_map/mul | solution.py:41
  12.9 1.7 %collective-permute-done = f32[256,256]{1,0:T(8,128)} collective-permute-done((f32[256,256]{1,0:T(8,128)}, f32[256,256]{1,0:T(8,128)}, u32[]{:S(2)}, u32[]{:S(2)}) %collective-permute-start) | collective-permute-done | bytes 262176 | tf_op jit(solution)/shard_map/ppermute | solution.py:18
  14.6 3.8 %conditional.6 = (f32[256,256]{1,0:T(8,128)}, f32[2,256,128]{2,1,0:T(8,128)}) conditional(s32[]{:T(128)} %convert_element_type.121, () %tuple.72, (bf16[256,256]{1,0:T(8,128)(2,1)S(1)}, f32[256,256]{1,0:T(8,128)}, bf16[256,256]{1,0:T(8,128)(2,1)S(1)}, bf16[3,256,128]{2,1,0:T(8,128)(2,1)}, f32[256,256]{1,0:T(8,128)}) %tuple.106), branch_computations={%region_0.0_spmd, %region_1.0_spmd} | conditional | flops 67436544 | bytes 1703952 | solution.py:132
  14.6 2.0 %fusion.1 = f32[256,256]{1,0:T(8,128)} fusion(bf16[256,256]{1,0:T(8,128)(2,1)S(1)} %get-tuple-element.81, f32[256,256]{1,0:T(8,128)} %get-tuple-element.124, f32[256,256]{1,0:T(8,128)} %get-tuple-element.125, bf16[256,256]{1,0:T(8,128)(2,1)S(1)} %get-tuple-element.79), kind=kOutput, calls=%fused_computation.3 | convolution fusion | flops 33816576 | bytes 1048576 | tf_op jit(solution)/shard_map/cond/branch_1_fun/dot_general | solution.py:56
  16.6 1.9 %convolution_bitcast_fusion = f32[2,256,128]{2,1,0:T(8,128)} fusion(bf16[3,256,128]{2,1,0:T(8,128)(2,1)} %get-tuple-element.82, f32[256,256]{1,0:T(8,128)} %fusion.1), kind=kOutput, calls=%fused_computation | convolution fusion | flops 33619968 | bytes 655360 | tf_op jit(solution)/shard_map/cond/branch_1_fun/rs,lsp->lrp/dot_general | solution.py:63
  18.4 1.9 %mul.118 = f32[2,256,2,128]{3,2,1,0:T(2,128)} broadcast(f32[2,256,128]{2,1,0:T(8,128)} %get-tuple-element.114), dimensions={0,1,3} | broadcast | bytes 786432 | tf_op jit(solution)/shard_map/mul | solution.py:41
  20.4 2.3 %mul.119 = f32[2,256,256]{2,1,0:T(8,128)} reshape(f32[2,256,2,128]{3,2,1,0:T(2,128)} %mul.118) | data formatting | bytes 1048576 | tf_op jit(solution)/shard_map/mul | solution.py:41
  24.6 6.6 %collective-permute-done.1 = f32[256,256]{1,0:T(8,128)S(1)} collective-permute-done((f32[256,256]{1,0:T(8,128)S(1)}, f32[256,256]{1,0:T(8,128)S(1)}, u32[]{:S(2)}, u32[]{:S(2)}) %collective-permute-start.1) | collective-permute-done | bytes 262176 | tf_op jit(solution)/shard_map/ppermute | solution.py:18
  34.2 4.4 %collective-permute-done.2 = f32[256,256]{1,0:T(8,128)} collective-permute-done((f32[256,256]{1,0:T(8,128)}, f32[256,256]{1,0:T(8,128)}, u32[]{:S(2)}, u32[]{:S(2)}) %collective-permute-start.2) | collective-permute-done | bytes 262176 | tf_op jit(solution)/shard_map/ppermute | solution.py:18
  40.2 1.9 %mul.126 = f32[1,256,256]{2,1,0:T(8,128)} reshape(f32[256,2,128]{2,1,0:T(2,128)} %mul.125) | data formatting | bytes 524288 | tf_op jit(solution)/shard_map/mul | solution.py:41
  43.1 2.9 %collective-permute-start.3 = (f32[256,256]{1,0:T(8,128)S(1)}, f32[256,256]{1,0:T(8,128)S(1)}, u32[]{:S(2)}, u32[]{:S(2)}) collective-permute-start(f32[256,256]{1,0:T(8,128)S(1)} %fusion.38), channel_id=1, source_target_pairs={{0,4},{4,0},{8,12},{12,8},{16,20},{20,16},{24,28},{28,24},{1,5},{5... | collective-permute-start | bytes 786440 | tf_op jit(solution)/shard_map/ppermute | solution.py:18
  45.9 4.4 %collective-permute-done.3 = f32[256,256]{1,0:T(8,128)S(1)} collective-permute-done((f32[256,256]{1,0:T(8,128)S(1)}, f32[256,256]{1,0:T(8,128)S(1)}, u32[]{:S(2)}, u32[]{:S(2)}) %collective-permute-start.3) | collective-permute-done | bytes 262176 | tf_op jit(solution)/shard_map/ppermute | solution.py:18
  51.2 8.1 %collective-permute-done.4 = f32[256,256]{1,0:T(8,128)S(1)} collective-permute-done((f32[256,256]{1,0:T(8,128)S(1)}, f32[256,256]{1,0:T(8,128)S(1)}, u32[]{:S(2)}, u32[]{:S(2)}) %collective-permute-start.4) | collective-permute-done | bytes 262176 | tf_op jit(solution)/shard_map/ppermute | solution.py:18
  60.0 9.1 %collective-permute-done.5 = f32[256,256]{1,0:T(8,128)} collective-permute-done((f32[256,256]{1,0:T(8,128)}, f32[256,256]{1,0:T(8,128)}, u32[]{:S(2)}, u32[]{:S(2)}) %collective-permute-start.5) | collective-permute-done | bytes 262176 | tf_op jit(solution)/shard_map/ppermute | solution.py:18
  71.2 6.5 %collective-permute-done.6 = bf16[256,256]{1,0:T(8,128)(2,1)S(1)} collective-permute-done((bf16[256,256]{1,0:T(8,128)(2,1)S(1)}, bf16[256,256]{1,0:T(8,128)(2,1)S(1)}, u32[]{:S(2)}, u32[]{:S(2)}) %collective-permute-start.6) | collective-permute-done | bytes 131104 | tf_op jit(solution)/shard_map/ppermute | solution.py:32
  77.6 3.0 %collective-permute-start.7 = (bf16[1,256,256]{2,1,0:T(8,128)(2,1)S(1)}, bf16[1,256,256]{2,1,0:T(8,128)(2,1)S(1)}, u32[]{:S(2)}, u32[]{:S(2)}) collective-permute-start(bf16[1,256,256]{2,1,0:T(8,128)(2,1)S(1)} %select_bitcast_fusion.1), channel_id=1, source_target_pairs={{8,0},{12,4},{16,8},{20,12},{24,16},{28,20},{9,1},{13,5},{17,9},{2... | collective-permute-start | bytes 393224 | tf_op jit(solution)/shard_map/ppermute | solution.py:32
  80.7 4.2 %collective-permute-done.7 = bf16[1,256,256]{2,1,0:T(8,128)(2,1)S(1)} collective-permute-done((bf16[1,256,256]{2,1,0:T(8,128)(2,1)S(1)}, bf16[1,256,256]{2,1,0:T(8,128)(2,1)S(1)}, u32[]{:S(2)}, u32[]{:S(2)}) %collective-permute-start.7) | collective-permute-done | bytes 131104 | tf_op jit(solution)/shard_map/ppermute | solution.py:32
  86.3 1.9 %collective-permute-start.8 = (bf16[256,256]{1,0:T(8,128)(2,1)}, bf16[256,256]{1,0:T(8,128)(2,1)S(1)}, u32[]{:S(2)}, u32[]{:S(2)}) collective-permute-start(bf16[256,256]{1,0:T(8,128)(2,1)} %get-tuple-element.118), channel_id=1, source_target_pairs={{0,8},{4,12},{8,16},{12,20},{16,24},{20,28},{1,9},{5,13},{9,17},{1... | collective-permute-start | bytes 393224 | tf_op jit(solution)/shard_map/ppermute | solution.py:32
  88.2 5.1 %collective-permute-done.8 = bf16[256,256]{1,0:T(8,128)(2,1)S(1)} collective-permute-done((bf16[256,256]{1,0:T(8,128)(2,1)}, bf16[256,256]{1,0:T(8,128)(2,1)S(1)}, u32[]{:S(2)}, u32[]{:S(2)}) %collective-permute-start.8) | collective-permute-done | bytes 131104 | tf_op jit(solution)/shard_map/ppermute | solution.py:32
  95.6 5.5 %collective-permute-start.9 = (bf16[2,256,256]{2,1,0:T(8,128)(2,1)}, bf16[2,256,256]{2,1,0:T(8,128)(2,1)}, u32[]{:S(2)}, u32[]{:S(2)}) collective-permute-start(bf16[2,256,256]{2,1,0:T(8,128)(2,1)} %pad_maximum_fusion), channel_id=1, source_target_pairs={{4,0},{8,4},{12,8},{16,12},{20,16},{24,20},{28,24},{5,1},{9,5},{13... | collective-permute-start | bytes 786440 | tf_op jit(solution)/shard_map/ppermute | solution.py:32
  101.1 6.4 %collective-permute-done.9 = bf16[2,256,256]{2,1,0:T(8,128)(2,1)} collective-permute-done((bf16[2,256,256]{2,1,0:T(8,128)(2,1)}, bf16[2,256,256]{2,1,0:T(8,128)(2,1)}, u32[]{:S(2)}, u32[]{:S(2)}) %collective-permute-start.9) | collective-permute-done | bytes 262176 | tf_op jit(solution)/shard_map/ppermute | solution.py:32
  109.4 4.8 %conditional.11 = (f32[256,256]{1,0:T(8,128)}, bf16[256,256]{1,0:T(8,128)(2,1)}) conditional(s32[]{:T(128)} %convert_element_type.121, () %tuple.68, (bf16[2,256,256]{2,1,0:T(8,128)(2,1)S(1)}, s32[3]{0:T(128)S(1)}, bf16[3,256,128]{2,1,0:T(8,128)(2,1)}, f32[256,256]{1,0:T(8,128)}, bf16[256,256]{1,0:T(8,128)(2,1)S(1)}) %tuple.111), branch_computations={%region_11.12_spmd, %region_12.14_spmd} | conditional | flops 67502088 | bytes 1966136 | solution.py:155
  110.3 1.7 %multiply_reduce_fusion.1 = bf16[2,256,128]{2,1,0:T(8,128)(2,1)S(1)} fusion(bf16[2,256,2,128]{3,2,1,0:T(2,128)(2,1)} %reshape.272, bf16[2,2]{1,0:T(2,128)(2,1)S(1)} %compare_convert_fusion.1), kind=kLoop, calls=%fused_computation.30 | loop fusion | flops 196608 | bytes 393224 | tf_op jit(solution)/shard_map/cond/branch_1_fun/reduce_sum | solution.py:51
  112.0 2.1 %fusion.46 = (bf16[256,256]{1,0:T(8,128)(2,1)}, f32[256,256]{1,0:T(8,128)}) fusion(bf16[256,256]{1,0:T(8,128)(2,1)S(1)} %get-tuple-element.101, f32[256,256]{1,0:T(8,128)} %get-tuple-element.97, bf16[2,256,128]{2,1,0:T(8,128)(2,1)S(1)} %multiply_reduce_fusion.1, bf16[3,256,128]{2,1,0:T(8,128)(2,1)} %get-tuple-element.100), kind=kOutput, calls=%fused_computation.72 | convolution fusion | flops 67305472 | bytes 1048576 | tf_op jit(solution)/shard_map/cond/branch_1_fun/dot_general | solution.py:93
  114.2 1.9 %collective-permute-start.10 = (bf16[256,256]{1,0:T(8,128)(2,1)}, bf16[256,256]{1,0:T(8,128)(2,1)S(1)}, u32[]{:S(2)}, u32[]{:S(2)}) collective-permute-start(bf16[256,256]{1,0:T(8,128)(2,1)} %get-tuple-element.120), channel_id=1, source_target_pairs={{0,4},{4,8},{8,12},{12,16},{16,20},{20,24},{24,28},{1,5},{5,9},{9,... | collective-permute-start | bytes 393224 | tf_op jit(solution)/shard_map/ppermute | solution.py:32
  116.1 1.7 %select_select_fusion = f32[256,256]{1,0:T(8,128)} fusion(f32[256,256]{1,0:T(8,128)} %get-tuple-element.121, f32[256,256]{1,0:T(8,128)} %get-tuple-element.122, f32[256,256]{1,0:T(8,128)} %get-tuple-element.123, pred[]{:T(512)S(6)} %eq.120, pred[]{:T(512)S(6)} %eq.118, pred[]{:T(512)S(6)} %eq.116), kind=kLoop, calls=%fused_computation.51 | loop fusion | flops 196608 | bytes 1048579 | tf_op jit(solution)/shard_map/jit(_where)/select_n | solution.py:170
  117.8 4.3 %collective-permute-done.10 = bf16[256,256]{1,0:T(8,128)(2,1)S(1)} collective-permute-done((bf16[256,256]{1,0:T(8,128)(2,1)}, bf16[256,256]{1,0:T(8,128)(2,1)S(1)}, u32[]{:S(2)}, u32[]{:S(2)}) %collective-permute-start.10) | collective-permute-done | bytes 131104 | tf_op jit(solution)/shard_map/ppermute | solution.py:32
  123.7 2.2 %fusion.37 = bf16[3,256,128]{2,1,0:T(8,128)(2,1)S(1)} fusion(bf16[2,256,2,128]{3,2,1,0:T(2,128)(2,1)} %concatenate.17, bf16[1,256,2,128]{3,2,1,0:T(2,128)(2,1)} %concatenate.16, bf16[3,2]{1,0:T(4,128)(2,1)S(1)} %get-tuple-element.136), kind=kLoop, calls=%fused_computation.45 | loop fusion | flops 491520 | bytes 589836 | tf_op jit(solution)/shard_map/reduce_sum | solution.py:51
  126.0 3.1 %fusion.30 = f32[256,1024]{1,0:T(8,128)} fusion(bf16[1024,1024]{1,0:T(8,128)(2,1)S(1)} %copy-done, f32[256,1024]{1,0:T(8,128)S(1)} %fusion.49, bf16[3,256,128]{2,1,0:T(8,128)(2,1)S(1)} %fusion.37, bf16[1,3,1024,128]{3,2,1,0:T(8,128)(2,1)} %param.27), kind=kOutput, calls=%fused_computation.36 | convolution fusion | flops 738721792 | bytes 5177344 | tf_op jit(solution)/shard_map/dot_general | solution.py:177
  (70 shorter events, 26.2 us)
Async XLA Ops:
  0.6 1.6 %copy-start = (bf16[1024,1024]{1,0:T(8,128)(2,1)S(1)}, bf16[1024,1024]{1,0:T(8,128)(2,1)}, u32[]{:S(2)}) copy-start(bf16[1024,1024]{1,0:T(8,128)(2,1)} %param.26) | copy-start | bytes 6291460
  0.6 3.4 %copy-start.3 = (bf16[1,3,1024,128]{3,2,1,0:T(8,128)(2,1)S(1)}, bf16[1,3,1024,128]{3,2,1,0:T(8,128)(2,1)}, u32[]{:S(2)}) copy-start(bf16[1,3,1024,128]{3,2,1,0:T(8,128)(2,1)} %param.27) | copy-start | bytes 2359300
  4.0 1.2 copy-start.8
  4.0 3.8 %copy-start.9 = (s32[1,3]{1,0:T(1,128)S(1)}, s32[1,3]{1,0:T(1,128)}, u32[]{:S(2)}) copy-start(s32[1,3]{1,0:T(1,128)} %param.31) | copy-start | bytes 40
  4.5 0.8 copy-start.4
  5.2 9.4 %copy-start.1 = (bf16[256,256]{1,0:T(8,128)(2,1)S(1)}, bf16[256,256]{1,0:T(8,128)(2,1)}, u32[]{:S(2)}) copy-start(bf16[256,256]{1,0:T(8,128)(2,1)} %param.29) | copy-start | bytes 393220
  5.2 9.4 %copy-start.7 = (bf16[256,256]{1,0:T(8,128)(2,1)S(1)}, bf16[256,256]{1,0:T(8,128)(2,1)}, u32[]{:S(2)}) copy-start(bf16[256,256]{1,0:T(8,128)(2,1)} %param.25) | copy-start | bytes 393220
  6.2 8.4 %collective-permute-start = (f32[256,256]{1,0:T(8,128)}, f32[256,256]{1,0:T(8,128)}, u32[]{:S(2)}, u32[]{:S(2)}) collective-permute-start(f32[256,256]{1,0:T(8,128)} %bitcast.94), channel_id=1, source_target_pairs={{0,4},{4,0},{8,12},{12,8},{16,20},{20,16},{24,28},{28,24},{1,5},{5... | collective-permute-start | bytes 786440 | tf_op jit(solution)/shard_map/ppermute | solution.py:18
  23.9 7.3 %copy-start.2 = (f32[2,256,256]{2,1,0:T(8,128)}, f32[2,256,256]{2,1,0:T(8,128)S(1)}, u32[]{:S(2)}) copy-start(f32[2,256,256]{2,1,0:T(8,128)S(1)} %fusion.34) | copy-start | bytes 1572868
  24.0 7.2 %collective-permute-start.1 = (f32[256,256]{1,0:T(8,128)S(1)}, f32[256,256]{1,0:T(8,128)S(1)}, u32[]{:S(2)}, u32[]{:S(2)}) collective-permute-start(f32[256,256]{1,0:T(8,128)S(1)} %slice_bitcast_fusion), channel_id=1, source_target_pairs={{0,4},{4,0},{8,12},{12,8},{16,20},{20,16},{24,28},{28,24},{1,5},{5... | collective-permute-start | bytes 786440 | tf_op jit(solution)/shard_map/ppermute | solution.py:18
  31.9 6.7 %collective-permute-start.2 = (f32[256,256]{1,0:T(8,128)}, f32[256,256]{1,0:T(8,128)}, u32[]{:S(2)}, u32[]{:S(2)}) collective-permute-start(f32[256,256]{1,0:T(8,128)} %fusion.41), channel_id=1, source_target_pairs={{0,8},{8,0},{4,12},{12,4},{16,24},{24,16},{20,28},{28,20},{1,9},{9... | collective-permute-start | bytes 786440 | tf_op jit(solution)/shard_map/ppermute | solution.py:18
  43.1 7.2 %collective-permute-start.3 = (f32[256,256]{1,0:T(8,128)S(1)}, f32[256,256]{1,0:T(8,128)S(1)}, u32[]{:S(2)}, u32[]{:S(2)}) collective-permute-start(f32[256,256]{1,0:T(8,128)S(1)} %fusion.38), channel_id=1, source_target_pairs={{0,4},{4,0},{8,12},{12,8},{16,20},{20,16},{24,28},{28,24},{1,5},{5... | collective-permute-start | bytes 786440 | tf_op jit(solution)/shard_map/ppermute | solution.py:18
  50.3 8.9 %collective-permute-start.4 = (f32[256,256]{1,0:T(8,128)S(1)}, f32[256,256]{1,0:T(8,128)S(1)}, u32[]{:S(2)}, u32[]{:S(2)}) collective-permute-start(f32[256,256]{1,0:T(8,128)S(1)} %add.37), channel_id=1, source_target_pairs={{0,8},{8,0},{4,12},{12,4},{16,24},{24,16},{20,28},{28,20},{1,9},{9... | collective-permute-start | bytes 786440 | tf_op jit(solution)/shard_map/ppermute | solution.py:18
  60.0 9.1 %collective-permute-start.5 = (f32[256,256]{1,0:T(8,128)}, f32[256,256]{1,0:T(8,128)}, u32[]{:S(2)}, u32[]{:S(2)}) collective-permute-start(f32[256,256]{1,0:T(8,128)} %add.38), channel_id=1, source_target_pairs={{0,16},{16,0},{4,20},{20,4},{8,24},{24,8},{12,28},{28,12},{1,17},{... | collective-permute-start | bytes 786440 | tf_op jit(solution)/shard_map/ppermute | solution.py:18
  69.9 7.8 %collective-permute-start.6 = (bf16[256,256]{1,0:T(8,128)(2,1)S(1)}, bf16[256,256]{1,0:T(8,128)(2,1)S(1)}, u32[]{:S(2)}, u32[]{:S(2)}) collective-permute-start(bf16[256,256]{1,0:T(8,128)(2,1)S(1)} %get-tuple-element.116), channel_id=1, source_target_pairs={{0,16},{4,20},{8,24},{12,28},{1,17},{5,21},{9,25},{13,29},{2,18},{... | collective-permute-start | bytes 393224 | tf_op jit(solution)/shard_map/ppermute | solution.py:32
  77.6 7.2 %collective-permute-start.7 = (bf16[1,256,256]{2,1,0:T(8,128)(2,1)S(1)}, bf16[1,256,256]{2,1,0:T(8,128)(2,1)S(1)}, u32[]{:S(2)}, u32[]{:S(2)}) collective-permute-start(bf16[1,256,256]{2,1,0:T(8,128)(2,1)S(1)} %select_bitcast_fusion.1), channel_id=1, source_target_pairs={{8,0},{12,4},{16,8},{20,12},{24,16},{28,20},{9,1},{13,5},{17,9},{2... | collective-permute-start | bytes 393224 | tf_op jit(solution)/shard_map/ppermute | solution.py:32
  84.9 16.2 %copy-start.5 = (bf16[1,256,256]{2,1,0:T(8,128)(2,1)}, bf16[1,256,256]{2,1,0:T(8,128)(2,1)S(1)}, u32[]{:S(2)}) copy-start(bf16[1,256,256]{2,1,0:T(8,128)(2,1)S(1)} %broadcast_select_fusion.1) | copy-start | bytes 393220
  86.3 7.1 %collective-permute-start.8 = (bf16[256,256]{1,0:T(8,128)(2,1)}, bf16[256,256]{1,0:T(8,128)(2,1)S(1)}, u32[]{:S(2)}, u32[]{:S(2)}) collective-permute-start(bf16[256,256]{1,0:T(8,128)(2,1)} %get-tuple-element.118), channel_id=1, source_target_pairs={{0,8},{4,12},{8,16},{12,20},{16,24},{20,28},{1,9},{5,13},{9,17},{1... | collective-permute-start | bytes 393224 | tf_op jit(solution)/shard_map/ppermute | solution.py:32
  94.3 0.6 copy-start.6
  95.6 11.9 %collective-permute-start.9 = (bf16[2,256,256]{2,1,0:T(8,128)(2,1)}, bf16[2,256,256]{2,1,0:T(8,128)(2,1)}, u32[]{:S(2)}, u32[]{:S(2)}) collective-permute-start(bf16[2,256,256]{2,1,0:T(8,128)(2,1)} %pad_maximum_fusion), channel_id=1, source_target_pairs={{4,0},{8,4},{12,8},{16,12},{20,16},{24,20},{28,24},{5,1},{9,5},{13... | collective-permute-start | bytes 786440 | tf_op jit(solution)/shard_map/ppermute | solution.py:32
  114.2 8.0 %collective-permute-start.10 = (bf16[256,256]{1,0:T(8,128)(2,1)}, bf16[256,256]{1,0:T(8,128)(2,1)S(1)}, u32[]{:S(2)}, u32[]{:S(2)}) collective-permute-start(bf16[256,256]{1,0:T(8,128)(2,1)} %get-tuple-element.120), channel_id=1, source_target_pairs={{0,4},{4,8},{8,12},{12,16},{16,20},{20,24},{24,28},{1,5},{5,9},{9,... | collective-permute-start | bytes 393224 | tf_op jit(solution)/shard_map/ppermute | solution.py:32
where the time goes:
time: 130 us; the launch traced here: 129 us
  waiting for transfers between devices  60.7 us (47%)
  local copies, waits for them, and re-layouts  21.5 us (17%)
  starting transfers between devices  20.4 us (16%)
  other arithmetic  14.2 us (11%)
  matrix products  11.3 us (9%)
    ppermute x6, waiting for transfers between devices, partner(): return lax.ppermute(block, axis, route)  34.2 us
    ppermute x5, waiting for transfers between devices, shifted(): return lax.ppermute(block, axis, route)  26.5 us
    ppermute x5, starting transfers between devices, shifted(): return lax.ppermute(block, axis, route)  13.6 us
    mul x7, local copies, waits for them, and re-layouts, place_panels(): spread = updates[:, :, None, :] * selector[:, None, :, None]  11.7 us
    ppermute x6, starting transfers between devices, partner(): return lax.ppermute(block, axis, route)  6.87 us
    reduce_sum x2, other arithmetic, pick_panels(): jnp.sum(divided * selector[:, None, :, None], axis=2).astype(vectors.dtype)  3.94 us
    unnamed x25, local copies, waits for them, and re-layouts  3.87 us
    dot_general x1, matrix products, local(): jnp.dot((leaf_solved - gathered).astype(jnp.bfloat16), leaf_inverse, pref...  3.12 us
  transfers between devices with their start and end apart: 11, of which 11 were waited for; matrix products, arithmetic and copies ran while one was open for 6% of the time, Pallas kernels for 0%

commit v1 on v0

v1 whole, which is shorter than its diff:
```python
from functools import partial

import jax
import jax.numpy as jnp
from jax import lax
from jax.experimental import pallas as pl
from jax.experimental.pallas import tpu as pltpu
from jax.sharding import PartitionSpec as P

NOTE_ROWS = 16
f32, bf16 = jnp.float32, jnp.bfloat16


def dot(a, b):
    return jnp.dot(a, b, preferred_element_type=f32)


def dot_t(a, b):
    return lax.dot_general(a, b, (((1,), (1,)), ((), ())), preferred_element_type=f32)


def own_level(k, levels):
    level = jnp.int32(0)
    for bit in range(levels):
        low = (2 << bit) - 1
        level = jnp.where((k & low) == low, bit + 1, level)
    return level


def placed(block, panel, count):
    return jnp.concatenate(
        [jnp.where(panel == p, block, jnp.zeros_like(block)) for p in range(count)], axis=1
    )


def picked(vectors, panel, count):
    width = vectors.shape[1] // count
    result = vectors[:, :width]
    for p in range(1, count):
        result = jnp.where(panel == p, vectors[:, p * width : (p + 1) * width], result)
    return result


def call(kernel, outs, args, smem=(), flops=0):
    def bytes_of(arrays):
        return sum(a.size * a.dtype.itemsize for a in arrays)

    outs = [jax.ShapeDtypeStruct(shape, dtype) for shape, dtype in outs]
    return pl.pallas_call(
        kernel,
        out_shape=outs,
        in_specs=[
            pl.BlockSpec(memory_space=pltpu.SMEM if i in smem else pltpu.VMEM)
            for i in range(len(args))
        ],
        out_specs=[pl.BlockSpec(memory_space=pltpu.VMEM) for _ in outs],
        compiler_params=pltpu.CompilerParams(vmem_limit_bytes=40 << 20),
        cost_estimate=pl.CostEstimate(
            flops=flops, bytes_accessed=bytes_of(args) + bytes_of(outs), transcendentals=0
        ),
    )(*args)


def exchange(block, distance):
    count = lax.axis_size("leaf")
    return lax.ppermute(block, "leaf", [(i, i ^ distance) for i in range(count)])


def pack_kernel(levels, panel_ref, inverse_ref, update_ref, out_ref):
    rows, panel_rows = inverse_ref.shape[0], update_ref.shape[2]
    out_ref[:rows, :rows] = inverse_ref[...]
    out_ref[rows:, :rows] = jnp.zeros((NOTE_ROWS, rows), bf16)
    for a in range(1, levels):
        columns = pl.ds(rows + (a - 1) * panel_rows, panel_rows)
        out_ref[:rows, columns] = update_ref[a]
        out_ref[rows:, columns] = jnp.full(
            (NOTE_ROWS, panel_rows), panel_ref[0, a].astype(f32)
        ).astype(bf16)


def leaf_up_kernel(
    levels, panel_ref, rhs_ref, inverse_ref, update_ref, sep_rhs_ref, solved_ref, out_ref
):
    k = lax.axis_index("leaf")
    scenarios, sep_rows = sep_rhs_ref.shape
    size, panel_rows = inverse_ref.shape[0], update_ref.shape[2]
    count = sep_rows // panel_rows
    step = min(256, size)
    for low in range(0, size, step):
        high = low + step
        solved_ref[:, low:high] = dot_t(rhs_ref[:, :high], inverse_ref[low:high, :high])
    rounded = solved_ref[...].astype(bf16)
    terms = [dot(rounded, update_ref[a]) for a in range(levels)]
    level = own_level(k, levels)
    wide_level = jnp.minimum(level, levels - 1)
    wide, panel = terms[0], panel_ref[0, 0]
    for a in range(1, levels):
        wide = jnp.where(wide_level == a, terms[a], wide)
        panel = jnp.where(wide_level == a, panel_ref[0, a], panel)
    rhs = jnp.where(level < levels, sep_rhs_ref[...].astype(f32), 0.0)
    out_ref[:scenarios, :sep_rows] = (placed(wide, panel, count) - rhs).astype(bf16)
    out_ref[scenarios:, :sep_rows] = jnp.zeros((NOTE_ROWS, sep_rows), bf16)
    for a in range(levels - 1):
        columns = pl.ds(sep_rows + a * panel_rows, panel_rows)
        later = wide_level <= a
        out_ref[:scenarios, columns] = jnp.where(later, terms[a + 1], terms[a]).astype(bf16)
        panel = jnp.where(later, panel_ref[0, a + 1], panel_ref[0, a])
        out_ref[scenarios:, columns] = jnp.full((NOTE_ROWS, panel_rows), panel.astype(f32)).astype(
            bf16
        )


def hand_on_kernel(step, own_ref, received_ref, factor_ref, carry_ref):
    lower = ((lax.axis_index("leaf") >> step) & 1) == 0
    own, received = own_ref[...], received_ref[...]
    factor_ref[...] = jnp.where(lower, own, received)
    if carry_ref is not None:
        sep_rows = own.shape[0] - NOTE_ROWS
        skipped = own.shape[1] - carry_ref.shape[1]
        following = jnp.where(lower, received, own)
        carry_ref[:, :sep_rows] = following[:, :sep_rows]
        if carry_ref.shape[1] > sep_rows:
            carry_ref[:, sep_rows:] = following[:, sep_rows + skipped :]


def spread_first(message_ref, wide_level, levels, scenarios, sep_rows, panel_rows):
    count = sep_rows // panel_rows
    wide = message_ref[:scenarios, :sep_rows].astype(f32)
    narrow = []
    for a in range(levels - 1):
        columns = pl.ds(sep_rows + a * panel_rows, panel_rows)
        panel = message_ref[scenarios : scenarios + NOTE_ROWS, columns].astype(f32)[:1]
        narrow.append(placed(message_ref[:scenarios, columns].astype(f32), panel, count))
    sums = []
    for a in range(levels):
        value = wide
        if a > 0:
            value = jnp.where(wide_level < a, narrow[a - 1], value)
        if a < levels - 1:
            value = jnp.where(wide_level > a, narrow[a], value)
        sums.append(value)
    return sums


def solve_up(pending, factor_ref, panel_rows):
    scenarios, sep_rows = pending[0].shape
    count = sep_rows // panel_rows
    residual = (-pending[0]).astype(bf16)
    solved = dot_t(residual, factor_ref[:sep_rows, :sep_rows])
    rounded = solved.astype(bf16)
    others = []
    for a, value in enumerate(pending[1:]):
        columns = pl.ds(sep_rows + a * panel_rows, panel_rows)
        panel = factor_ref[sep_rows : sep_rows + NOTE_ROWS, columns].astype(f32)[:1]
        update = dot(rounded, factor_ref[:sep_rows, columns])
        others.append(value + placed(update, panel, count))
    return solved, others


def first_up_kernel(levels, panel_rows, own_ref, received_ref, factor_ref, solved_ref, out_ref):
    k = lax.axis_index("leaf")
    scenarios = own_ref.shape[0] - NOTE_ROWS
    sep_rows = solved_ref.shape[1]
    pending = [
        own + received
        for own, received in zip(
            *(
                spread_first(
                    ref,
                    jnp.minimum(own_level(who, levels), levels - 1),
                    levels,
                    scenarios,
                    sep_rows,
                    panel_rows,
                )
                for ref, who in ((own_ref, k), (received_ref, k ^ 1))
            )
        )
    ]
    solved, others = solve_up(pending, factor_ref, panel_rows)
    solved_ref[...] = solved
    for a, value in enumerate(others):
        out_ref[:, a * sep_rows : (a + 1) * sep_rows] = value.astype(bf16)


def sums_of(own_ref, received_ref, sep_rows):
    return [
        own_ref[:, low : low + sep_rows].astype(f32)
        + received_ref[:, low : low + sep_rows].astype(f32)
        for low in range(0, own_ref.shape[1], sep_rows)
    ]


def up_kernel(panel_rows, own_ref, received_ref, factor_ref, solved_ref, out_ref):
    sep_rows = solved_ref.shape[1]
    pending = sums_of(own_ref, received_ref, sep_rows)
    solved, others = solve_up(pending, factor_ref, panel_rows)
    solved_ref[...] = solved
    for a, value in enumerate(others):
        out_ref[:, a * sep_rows : (a + 1) * sep_rows] = value.astype(bf16)


def down_kernel(levels, *refs):
    panel_ref, own_ref, received_ref, leaf_solved_ref, update_ref, inverse_ref = refs[:6]
    factor_refs = refs[6 : 6 + levels]
    solved_refs = refs[6 + levels : 5 + 2 * levels]
    leaf_out_ref, sep_out_ref, work_ref = refs[5 + 2 * levels :]
    k = lax.axis_index("leaf")
    sep_rows = own_ref.shape[1]
    panel_rows = update_ref.shape[2]
    count = sep_rows // panel_rows
    level = own_level(k, levels)

    top = levels - 1
    pending = sums_of(own_ref, received_ref, sep_rows)
    solved, _ = solve_up(pending, factor_refs[top], panel_rows)
    ancestors = {}
    sep_out = jnp.zeros(sep_out_ref.shape, f32)
    for now in reversed(range(levels)):
        factor_ref = factor_refs[now]
        residual = solved if now == top else solved_refs[now][...]
        for a in range(now + 1, levels):
            columns = pl.ds(sep_rows + (a - now - 1) * panel_rows, panel_rows)
            panel = factor_ref[sep_rows : sep_rows + NOTE_ROWS, columns].astype(f32)[:1]
            block = picked(ancestors[a], panel, count).astype(bf16)
            residual = residual - dot_t(block, factor_ref[:sep_rows, columns])
        solution_now = dot(residual.astype(bf16), factor_ref[:sep_rows, :sep_rows])
        ancestors[now] = solution_now.astype(bf16).astype(f32)
        sep_out = jnp.where(level == now, solution_now, sep_out)
    sep_out_ref[...] = sep_out

    blocks = [picked(ancestors[a], panel_ref[0, a], count).astype(bf16) for a in range(levels)]
    size = inverse_ref.shape[0]
    step = min(256, size)
    for low in range(0, size, step):
        high = low + step
        value = leaf_solved_ref[:, low:high]
        for a in range(levels):
            value = value - dot_t(blocks[a], update_ref[a, low:high, :])
        work_ref[:, low:high] = value.astype(bf16)
    for low in range(0, size, step):
        high = low + step
        leaf_out_ref[:, low:high] = dot(work_ref[:, low:], inverse_ref[low:, low:high])


def local(
    leaf_rhs, sep_rhs, leaf_inverse, leaf_update, leaf_panel, sep_inverse, sep_update, sep_panel
):
    levels = lax.axis_size("leaf").bit_length() - 1
    sep_rows = sep_inverse.shape[0]
    scenarios, size = leaf_rhs.shape
    panel_rows = leaf_update.shape[3]
    tall = sep_rows + NOTE_ROWS
    leaf_update, sep_update = leaf_update[0], sep_update[0]

    (carry,) = call(
        partial(pack_kernel, levels),
        [((tall, sep_rows + (levels - 1) * panel_rows), bf16)],
        (sep_panel, sep_inverse, sep_update),
        smem=(0,),
    )
    arrived = exchange(carry, 1)
    leaf_solved, message = call(
        partial(leaf_up_kernel, levels),
        [
            ((scenarios, size), f32),
            ((scenarios + NOTE_ROWS, sep_rows + (levels - 1) * panel_rows), bf16),
        ],
        (leaf_panel, leaf_rhs, leaf_inverse, leaf_update, sep_rhs),
        smem=(0,),
        flops=2 * scenarios * size * (size + levels * panel_rows),
    )
    factors, solved = [], []
    for now in range(levels):
        received = exchange(message, 1 << now)
        shapes = [(carry.shape, bf16)]
        if now + 1 < levels:
            shapes.append(((tall, sep_rows + (levels - 2 - now) * panel_rows), bf16))
            factor, carry = call(partial(hand_on_kernel, now), shapes, (carry, arrived))
            arrived = exchange(carry, 2 << now)
        else:
            (factor,) = call(
                lambda a, b, c, step=now: hand_on_kernel(step, a, b, c, None),
                shapes,
                (carry, arrived),
            )
        factors.append(factor)
        if now + 1 < levels:
            kernel = (
                partial(first_up_kernel, levels, panel_rows)
                if now == 0
                else partial(up_kernel, panel_rows)
            )
            z, message = call(
                kernel,
                [
                    ((scenarios, sep_rows), f32),
                    ((scenarios, (levels - 1 - now) * sep_rows), bf16),
                ],
                (message, received, factor),
                flops=2 * scenarios * sep_rows * sep_rows * 2,
            )
            solved.append(z)
    args = (leaf_panel, message, received, leaf_solved, leaf_update, leaf_inverse)
    args += tuple(factors) + tuple(solved)
    kernel_args = args
    leaf_out, sep_out = pl.pallas_call(
        partial(down_kernel, levels),
        out_shape=[
            jax.ShapeDtypeStruct((scenarios, size), f32),
            jax.ShapeDtypeStruct((scenarios, sep_rows), f32),
        ],
        in_specs=[pl.BlockSpec(memory_space=pltpu.SMEM)]
        + [pl.BlockSpec(memory_space=pltpu.VMEM)] * (len(kernel_args) - 1),
        out_specs=[pl.BlockSpec(memory_space=pltpu.VMEM)] * 2,
        scratch_shapes=[pltpu.VMEM((scenarios, size), bf16)],
        compiler_params=pltpu.CompilerParams(vmem_limit_bytes=40 << 20),
    )(*kernel_args)
    return leaf_out, sep_out


def solution(mesh):
    return jax.shard_map(
        local,
        mesh=mesh,
        in_specs=(
            P("rhs", "leaf"),
            P("rhs", "leaf"),
            P("leaf", None),
            P("leaf", None, None, None),
            P("leaf", None),
            P("leaf", None),
            P("leaf", None, None, None),
            P("leaf", None),
        ),
        out_specs=(P("rhs", "leaf"), P("rhs", "leaf")),
        check_vma=False,
    )
```

time: 130 us -> 50.1 us (0.39)
  the two profiles are of different devices: /device:TPU:18 before, /device:TPU:0 now
where the time goes in v1:
time: 50.1 us; the launch traced here: 49.8 us
  waiting for transfers between devices  26.7 us (53%)
  starting transfers between devices  8.26 us (16%)
  local copies, waits for them, and re-layouts  7.82 us (16%)
  Pallas kernels  6.28 us (13%)
  between operations  0.73 us (1%)
    ppermute x6, waiting for transfers between devices, exchange(): lax.ppermute(block, 'leaf', [(i, i ^ distance) for i in range(count)])  26.7 us
    ppermute x6, starting transfers between devices, exchange(): lax.ppermute(block, 'leaf', [(i, i ^ distance) for i in range(count)])  8.26 us
    unnamed x22, local copies, waits for them, and re-layouts  7.82 us
    pallas_call x1, Pallas kernels, local(): pl.pallas_call(partial(down_kernel, levels), out_shape=[jax.ShapeDtypeStr...  3.21 us
    pallas_call x7, Pallas kernels, call(): pl.pallas_call(kernel, out_shape=outs, in_specs=[pl.BlockSpec(memory_spac...  3.07 us
  transfers between devices with their start and end apart: 6, of which 4 were waited for; matrix products, arithmetic and copies ran while one was open for 0% of the time, Pallas kernels for 4%

profile of v1, /device:TPU:0, one launch (start us, length us, event | category | flops | bytes accessed | tf_op | source)
XLA Modules:
  0.0 49.8 jit_solution(4069385188214084185)
XLA Ops:
  0.6 0.0 copy-start.5
  0.6 0.9 %copy-done.5 = bf16[1,3,256,128]{3,2,1,0:T(8,128)(2,1)S(1)} copy-done((bf16[1,3,256,128]{3,2,1,0:T(8,128)(2,1)S(1)}, bf16[1,3,256,128]{3,2,1,0:T(8,128)(2,1)}, u32[]{:S(2)}) %copy-start.5) | copy-done | bytes 196632
  1.6 0.9 %copy-done.6 = bf16[256,256]{1,0:T(8,128)(2,1)S(1)} copy-done((bf16[256,256]{1,0:T(8,128)(2,1)S(1)}, bf16[256,256]{1,0:T(8,128)(2,1)}, u32[]{:S(2)}) %copy-start.6) | copy-done | bytes 131096
  2.5 0.7 %copy-done.10 = s32[1,3]{1,0:T(1,128)S(1)} copy-done((s32[1,3]{1,0:T(1,128)S(1)}, s32[1,3]{1,0:T(1,128)}, u32[]{:S(2)}) %copy-start.10) | copy-done | bytes 36
  3.1 0.6 %shard_map.96.own_ref = bf16[272,512]{1,0:T(8,128)(2,1)S(1)} custom-call(s32[1,3]{1,0:T(1,128)S(1)} %copy-done.10, bf16[256,256]{1,0:T(8,128)(2,1)S(1)} %copy-done.6, bf16[3,256,128]{2,1,0:T(8,128)(2,1)S(1)} %bitcast.4), custom_call_target="tpu_custom_call" | custom-call | bytes 606220 | tf_op jit(solution)/shard_map/pallas_call | solution.py:49
  3.7 3.0 %collective-permute-start.1 = (bf16[272,512]{1,0:T(8,128)(2,1)S(1)}, bf16[272,512]{1,0:T(8,128)(2,1)S(1)}, u32[]{:S(2)}, u32[]{:S(2)}) collective-permute-start(bf16[272,512]{1,0:T(8,128)(2,1)S(1)} %shard_map.96.own_ref), channel_id=1, source_target_pairs={{0,4},{4,0},{8,12},{12,8},{16,20},{20,16},{24,28},{28,24},{1,5},{5... | collective-permute-start | bytes 835592 | tf_op jit(solution)/shard_map/ppermute | solution.py:66
  6.7 1.6 %copy-done = bf16[1024,1024]{1,0:T(8,128)(2,1)S(1)} copy-done((bf16[1024,1024]{1,0:T(8,128)(2,1)S(1)}, bf16[1024,1024]{1,0:T(8,128)(2,1)}, u32[]{:S(2)}) %copy-start) | copy-done | bytes 2097176
  8.3 1.1 %copy-done.2 = bf16[1,3,1024,128]{3,2,1,0:T(8,128)(2,1)S(1)} copy-done((bf16[1,3,1024,128]{3,2,1,0:T(8,128)(2,1)S(1)}, bf16[1,3,1024,128]{3,2,1,0:T(8,128)(2,1)}, u32[]{:S(2)}) %copy-start.2) | copy-done | bytes 786456
  9.5 1.0 %copy-done.4 = bf16[256,1024]{1,0:T(8,128)(2,1)S(1)} copy-done((bf16[256,1024]{1,0:T(8,128)(2,1)S(1)}, bf16[256,1024]{1,0:T(8,128)(2,1)}, u32[]{:S(2)}) %copy-start.4) | copy-done | bytes 524312
  10.5 0.9 %copy-done.7 = bf16[256,256]{1,0:T(8,128)(2,1)S(1)} copy-done((bf16[256,256]{1,0:T(8,128)(2,1)S(1)}, bf16[256,256]{1,0:T(8,128)(2,1)}, u32[]{:S(2)}) %copy-start.7) | copy-done | bytes 131096
  11.4 0.7 %copy-done.8 = s32[1,3]{1,0:T(1,128)S(1)} copy-done((s32[1,3]{1,0:T(1,128)S(1)}, s32[1,3]{1,0:T(1,128)}, u32[]{:S(2)}) %copy-start.8) | copy-done | bytes 36
  12.1 1.6 %shard_map.95 = (f32[256,1024]{1,0:T(8,128)S(1)}, bf16[272,512]{1,0:T(8,128)(2,1)S(1)}) custom-call(s32[1,3]{1,0:T(1,128)S(1)} %copy-done.8, bf16[256,1024]{1,0:T(8,128)(2,1)S(1)} %copy-done.4, bf16[1024,1024]{1,0:T(8,128)(2,1)S(1)} %copy-done, bf16[3,1024,128]{2,1,0:T(8,128)(2,1)S(1)} %bitcast.2, bf16[256,256]{1,0:T(8,128)(2,1)S(1)} %copy-done.7), custom_call_target="tpu_custom_call" | custom-call | flops 738197504 | bytes 4866060 | tf_op jit(solution)/shard_map/pallas_call | solution.py:49
  13.6 0.0 copy-start.1
  13.6 0.0 copy-start.3
  13.6 0.0 copy-start.9
  13.7 0.1 collective-permute-start
  13.7 0.0 collective-permute-done.1.received_ref
  13.7 0.1 shard_map.97
  13.8 8.0 %collective-permute-done.received_ref = bf16[272,512]{1,0:T(8,128)(2,1)S(1)} collective-permute-done((bf16[272,512]{1,0:T(8,128)(2,1)S(1)}, bf16[272,512]{1,0:T(8,128)(2,1)S(1)}, u32[]{:S(2)}, u32[]{:S(2)}) %collective-permute-start) | collective-permute-done | bytes 278560 | tf_op jit(solution)/shard_map/ppermute | solution.py:66
  21.8 0.4 shard_map.98
  22.3 1.6 %collective-permute-start.2 = (bf16[256,512]{1,0:T(8,128)(2,1)S(1)}, bf16[256,512]{1,0:T(8,128)(2,1)S(1)}, u32[]{:S(2)}, u32[]{:S(2)}) collective-permute-start(bf16[256,512]{1,0:T(8,128)(2,1)S(1)} %get-tuple-element.14.own_ref), channel_id=1, source_target_pairs={{0,8},{4,12},{8,0},{12,4},{16,24},{20,28},{24,16},{28,20},{1,9},{5... | collective-permute-start | bytes 786440 | tf_op jit(solution)/shard_map/ppermute | solution.py:66
  23.9 0.4 collective-permute-start.3
  24.4 9.3 %collective-permute-done.3.received_ref = bf16[272,384]{1,0:T(8,128)(2,1)S(1)} collective-permute-done((bf16[272,384]{1,0:T(8,128)(2,1)S(1)}, bf16[272,384]{1,0:T(8,128)(2,1)S(1)}, u32[]{:S(2)}, u32[]{:S(2)}) %collective-permute-start.3) | collective-permute-done | bytes 208928 | tf_op jit(solution)/shard_map/ppermute | solution.py:66
  33.7 2.6 %collective-permute-start.5 = (bf16[272,256]{1,0:T(8,128)(2,1)S(1)}, bf16[272,256]{1,0:T(8,128)(2,1)S(1)}, u32[]{:S(2)}, u32[]{:S(2)}) collective-permute-start(bf16[272,256]{1,0:T(8,128)(2,1)S(1)} %get-tuple-element.19.a), channel_id=1, source_target_pairs={{0,16},{4,20},{8,24},{12,28},{16,0},{20,4},{24,8},{28,12},{1,17},{... | collective-permute-start | bytes 417800 | tf_op jit(solution)/shard_map/ppermute | solution.py:66
  36.4 0.0 collective-permute-done.2.received_ref
  36.4 0.4 shard_map.100
  36.8 0.4 collective-permute-start.4
  37.2 8.0 %collective-permute-done.5.b = bf16[272,256]{1,0:T(8,128)(2,1)S(1)} collective-permute-done((bf16[272,256]{1,0:T(8,128)(2,1)S(1)}, bf16[272,256]{1,0:T(8,128)(2,1)S(1)}, u32[]{:S(2)}, u32[]{:S(2)}) %collective-permute-start.5) | collective-permute-done | bytes 139296 | tf_op jit(solution)/shard_map/ppermute | solution.py:66
  45.2 1.4 %collective-permute-done.4.refs_2_ = bf16[256,256]{1,0:T(8,128)(2,1)S(1)} collective-permute-done((bf16[256,256]{1,0:T(8,128)(2,1)S(1)}, bf16[256,256]{1,0:T(8,128)(2,1)S(1)}, u32[]{:S(2)}, u32[]{:S(2)}) %collective-permute-start.4) | collective-permute-done | bytes 131104 | tf_op jit(solution)/shard_map/ppermute | solution.py:66
  46.6 0.0 copy-done.1
  46.6 0.0 copy-done.9
  46.6 3.2 %shard_map.102 = (f32[256,1024]{1,0:T(8,128)}, f32[256,256]{1,0:T(8,128)}) custom-call(s32[1,3]{1,0:T(1,128)S(1)} %copy-done.9, bf16[256,256]{1,0:T(8,128)(2,1)S(1)} %get-tuple-element.17.refs_1_, bf16[256,256]{1,0:T(8,128)(2,1)S(1)} %collective-permute-done.4.refs_2_, f32[256,1024]{1,0:T(8,128)S(1)} %get-tuple-element.18.refs_3_, ...), custom_call_target="tpu_custom_call" | custom-call | tf_op jit(solution)/shard_map/pallas_call | solution.py:307
  (10 shorter events, 0.1 us)
Async XLA Ops:
  0.6 0.9 %copy-start.5 = (bf16[1,3,256,128]{3,2,1,0:T(8,128)(2,1)S(1)}, bf16[1,3,256,128]{3,2,1,0:T(8,128)(2,1)}, u32[]{:S(2)}) copy-start(bf16[1,3,256,128]{3,2,1,0:T(8,128)(2,1)} %param.14) | copy-start | bytes 589828
  1.6 0.9 %copy-start.6 = (bf16[256,256]{1,0:T(8,128)(2,1)S(1)}, bf16[256,256]{1,0:T(8,128)(2,1)}, u32[]{:S(2)}) copy-start(bf16[256,256]{1,0:T(8,128)(2,1)} %inverse_ref.3) | copy-start | bytes 393220
  2.5 0.7 %copy-start.10 = (s32[1,3]{1,0:T(1,128)S(1)}, s32[1,3]{1,0:T(1,128)}, u32[]{:S(2)}) copy-start(s32[1,3]{1,0:T(1,128)} %panel_ref.3) | copy-start | bytes 40
  3.7 10.0 %collective-permute-start.1 = (bf16[272,512]{1,0:T(8,128)(2,1)S(1)}, bf16[272,512]{1,0:T(8,128)(2,1)S(1)}, u32[]{:S(2)}, u32[]{:S(2)}) collective-permute-start(bf16[272,512]{1,0:T(8,128)(2,1)S(1)} %shard_map.96.own_ref), channel_id=1, source_target_pairs={{0,4},{4,0},{8,12},{12,8},{16,20},{20,16},{24,28},{28,24},{1,5},{5... | collective-permute-start | bytes 835592 | tf_op jit(solution)/shard_map/ppermute | solution.py:66
  6.7 1.6 %copy-start = (bf16[1024,1024]{1,0:T(8,128)(2,1)S(1)}, bf16[1024,1024]{1,0:T(8,128)(2,1)}, u32[]{:S(2)}) copy-start(bf16[1024,1024]{1,0:T(8,128)(2,1)} %refs_5_.1) | copy-start | bytes 6291460
  8.3 1.1 %copy-start.2 = (bf16[1,3,1024,128]{3,2,1,0:T(8,128)(2,1)S(1)}, bf16[1,3,1024,128]{3,2,1,0:T(8,128)(2,1)}, u32[]{:S(2)}) copy-start(bf16[1,3,1024,128]{3,2,1,0:T(8,128)(2,1)} %param.11) | copy-start | bytes 2359300
  9.5 1.0 %copy-start.4 = (bf16[256,1024]{1,0:T(8,128)(2,1)S(1)}, bf16[256,1024]{1,0:T(8,128)(2,1)}, u32[]{:S(2)}) copy-start(bf16[256,1024]{1,0:T(8,128)(2,1)} %rhs_ref.1) | copy-start | bytes 1572868
  10.5 0.9 %copy-start.7 = (bf16[256,256]{1,0:T(8,128)(2,1)S(1)}, bf16[256,256]{1,0:T(8,128)(2,1)}, u32[]{:S(2)}) copy-start(bf16[256,256]{1,0:T(8,128)(2,1)} %sep_rhs_ref.1) | copy-start | bytes 393220
  11.4 0.7 %copy-start.8 = (s32[1,3]{1,0:T(1,128)S(1)}, s32[1,3]{1,0:T(1,128)}, u32[]{:S(2)}) copy-start(s32[1,3]{1,0:T(1,128)} %refs_0_.1) | copy-start | bytes 40
  13.6 33.0 %copy-start.1 = (bf16[1024,1024]{1,0:T(8,128)(2,1)S(1)}, bf16[1024,1024]{1,0:T(8,128)(2,1)}, u32[]{:S(2)}) copy-start(bf16[1024,1024]{1,0:T(8,128)(2,1)} %refs_5_.1) | copy-start | bytes 6291460
  13.6 33.0 %copy-start.3 = (bf16[1,3,1024,128]{3,2,1,0:T(8,128)(2,1)S(1)}, bf16[1,3,1024,128]{3,2,1,0:T(8,128)(2,1)}, u32[]{:S(2)}) copy-start(bf16[1,3,1024,128]{3,2,1,0:T(8,128)(2,1)} %param.11) | copy-start | bytes 2359300
  13.6 33.0 %copy-start.9 = (s32[1,3]{1,0:T(1,128)S(1)}, s32[1,3]{1,0:T(1,128)}, u32[]{:S(2)}) copy-start(s32[1,3]{1,0:T(1,128)} %refs_0_.1) | copy-start | bytes 40
  13.7 8.2 %collective-permute-start = (bf16[272,512]{1,0:T(8,128)(2,1)S(1)}, bf16[272,512]{1,0:T(8,128)(2,1)S(1)}, u32[]{:S(2)}, u32[]{:S(2)}) collective-permute-start(bf16[272,512]{1,0:T(8,128)(2,1)S(1)} %get-tuple-element.12.own_ref), channel_id=1, source_target_pairs={{0,4},{4,0},{8,12},{12,8},{16,20},{20,16},{24,28},{28,24},{1,5},{5... | collective-permute-start | bytes 835592 | tf_op jit(solution)/shard_map/ppermute | solution.py:66
  22.3 14.1 %collective-permute-start.2 = (bf16[256,512]{1,0:T(8,128)(2,1)S(1)}, bf16[256,512]{1,0:T(8,128)(2,1)S(1)}, u32[]{:S(2)}, u32[]{:S(2)}) collective-permute-start(bf16[256,512]{1,0:T(8,128)(2,1)S(1)} %get-tuple-element.14.own_ref), channel_id=1, source_target_pairs={{0,8},{4,12},{8,0},{12,4},{16,24},{20,28},{24,16},{28,20},{1,9},{5... | collective-permute-start | bytes 786440 | tf_op jit(solution)/shard_map/ppermute | solution.py:66
  23.9 9.8 %collective-permute-start.3 = (bf16[272,384]{1,0:T(8,128)(2,1)S(1)}, bf16[272,384]{1,0:T(8,128)(2,1)S(1)}, u32[]{:S(2)}, u32[]{:S(2)}) collective-permute-start(bf16[272,384]{1,0:T(8,128)(2,1)S(1)} %get-tuple-element.15.own_ref), channel_id=1, source_target_pairs={{0,8},{4,12},{8,0},{12,4},{16,24},{20,28},{24,16},{28,20},{1,9},{5... | collective-permute-start | bytes 626696 | tf_op jit(solution)/shard_map/ppermute | solution.py:66
  33.7 11.5 %collective-permute-start.5 = (bf16[272,256]{1,0:T(8,128)(2,1)S(1)}, bf16[272,256]{1,0:T(8,128)(2,1)S(1)}, u32[]{:S(2)}, u32[]{:S(2)}) collective-permute-start(bf16[272,256]{1,0:T(8,128)(2,1)S(1)} %get-tuple-element.19.a), channel_id=1, source_target_pairs={{0,16},{4,20},{8,24},{12,28},{16,0},{20,4},{24,8},{28,12},{1,17},{... | collective-permute-start | bytes 417800 | tf_op jit(solution)/shard_map/ppermute | solution.py:66
  36.8 9.8 %collective-permute-start.4 = (bf16[256,256]{1,0:T(8,128)(2,1)S(1)}, bf16[256,256]{1,0:T(8,128)(2,1)S(1)}, u32[]{:S(2)}, u32[]{:S(2)}) collective-permute-start(bf16[256,256]{1,0:T(8,128)(2,1)S(1)} %get-tuple-element.17.refs_1_), channel_id=1, source_target_pairs={{0,16},{4,20},{8,24},{12,28},{16,0},{20,4},{24,8},{28,12},{1,17},{... | collective-permute-start | bytes 393224 | tf_op jit(solution)/shard_map/ppermute | solution.py:66

commit v2 on v1

--- a/solution.py
+++ b/solution.py
@@ -41,19 +41,24 @@
     return result
 
 
-def call(kernel, outs, args, smem=(), flops=0):
+def call(kernel, outs, args, hbm=(), scratch=(), flops=0):
     def bytes_of(arrays):
         return sum(a.size * a.dtype.itemsize for a in arrays)
 
     outs = [jax.ShapeDtypeStruct(shape, dtype) for shape, dtype in outs]
+    args = [
+        pltpu.with_memory_space_constraint(arg, pltpu.HBM) if i in hbm else arg
+        for i, arg in enumerate(args)
+    ]
     return pl.pallas_call(
         kernel,
         out_shape=outs,
         in_specs=[
-            pl.BlockSpec(memory_space=pltpu.SMEM if i in smem else pltpu.VMEM)
+            pl.BlockSpec(memory_space=pltpu.HBM if i in hbm else pltpu.VMEM)
             for i in range(len(args))
         ],
         out_specs=[pl.BlockSpec(memory_space=pltpu.VMEM) for _ in outs],
+        scratch_shapes=scratch,
         compiler_params=pltpu.CompilerParams(vmem_limit_bytes=40 << 20),
         cost_estimate=pl.CostEstimate(
             flops=flops, bytes_accessed=bytes_of(args) + bytes_of(outs), transcendentals=0
@@ -66,21 +71,69 @@
     return lax.ppermute(block, "leaf", [(i, i ^ distance) for i in range(count)])
 
 
-def pack_kernel(levels, panel_ref, inverse_ref, update_ref, out_ref):
-    rows, panel_rows = inverse_ref.shape[0], update_ref.shape[2]
-    out_ref[:rows, :rows] = inverse_ref[...]
-    out_ref[rows:, :rows] = jnp.zeros((NOTE_ROWS, rows), bf16)
+def load_kernel(
+    levels,
+    panel_hbm,
+    sep_inverse_hbm,
+    sep_update_hbm,
+    leaf_rhs_hbm,
+    leaf_inverse_hbm,
+    leaf_update_hbm,
+    sep_rhs_hbm,
+    carry_ref,
+    leaf_rhs_ref,
+    leaf_inverse_ref,
+    leaf_update_ref,
+    sep_rhs_ref,
+    panel_ref,
+    sems,
+):
+    rows, panel_rows = sep_inverse_hbm.shape[0], sep_update_hbm.shape[2]
+    first = [
+        (panel_hbm, panel_ref),
+        (sep_inverse_hbm, carry_ref.at[pl.ds(0, rows), pl.ds(0, rows)]),
+    ]
     for a in range(1, levels):
         columns = pl.ds(rows + (a - 1) * panel_rows, panel_rows)
-        out_ref[:rows, columns] = update_ref[a]
-        out_ref[rows:, columns] = jnp.full(
+        first.append((sep_update_hbm.at[a], carry_ref.at[pl.ds(0, rows), columns]))
+    second = [(leaf_rhs_hbm, leaf_rhs_ref)]
+    size = leaf_inverse_hbm.shape[0]
+    step = min(256, size)
+    for low in range(0, size, step):
+        block = (pl.ds(low, step), pl.ds(0, low + step))
+        second.append((leaf_inverse_hbm.at[block], leaf_inverse_ref.at[block]))
+    second += [(leaf_update_hbm, leaf_update_ref), (sep_rhs_hbm, sep_rhs_ref)]
+    copies = [
+        pltpu.make_async_copy(src, dst, sems.at[i]) for i, (src, dst) in enumerate(first + second)
+    ]
+    for copy in copies:
+        copy.start()
+    carry_ref[rows:, :rows] = jnp.zeros((NOTE_ROWS, rows), bf16)
+    copies[0].wait()
+    for a in range(1, levels):
+        columns = pl.ds(rows + (a - 1) * panel_rows, panel_rows)
+        carry_ref[rows:, columns] = jnp.full(
             (NOTE_ROWS, panel_rows), panel_ref[0, a].astype(f32)
         ).astype(bf16)
+    for copy in copies[1:]:
+        copy.wait()
 
 
 def leaf_up_kernel(
-    levels, panel_ref, rhs_ref, inverse_ref, update_ref, sep_rhs_ref, solved_ref, out_ref
+    levels,
+    panel_hbm,
+    rhs_ref,
+    inverse_ref,
+    update_ref,
+    sep_rhs_ref,
+    solved_ref,
+    own_ref,
+    out_ref,
+    panel_ref,
+    sem,
 ):
+    copy = pltpu.make_async_copy(panel_hbm, panel_ref, sem)
+    copy.start()
     k = lax.axis_index("leaf")
     scenarios, sep_rows = sep_rhs_ref.shape
     size, panel_rows = inverse_ref.shape[0], update_ref.shape[2]
@@ -93,12 +146,15 @@
     terms = [dot(rounded, update_ref[a]) for a in range(levels)]
     level = own_level(k, levels)
     wide_level = jnp.minimum(level, levels - 1)
-    wide, panel = terms[0], panel_ref[0, 0]
-    for a in range(1, levels):
-        wide = jnp.where(wide_level == a, terms[a], wide)
-        panel = jnp.where(wide_level == a, panel_ref[0, a], panel)
     rhs = jnp.where(level < levels, sep_rhs_ref[...].astype(f32), 0.0)
-    out_ref[:scenarios, :sep_rows] = (placed(wide, panel, count) - rhs).astype(bf16)
+    copy.wait()
+    wide = jnp.zeros((scenarios, sep_rows), f32)
+    for a in range(levels):
+        spread = placed(terms[a], panel_ref[0, a], count)
+        spread = jnp.where(wide_level == a, spread - rhs, spread)
+        wide = jnp.where(wide_level == a, spread, wide)
+        own_ref[:, a * sep_rows : (a + 1) * sep_rows] = spread
+    out_ref[:scenarios, :sep_rows] = wide.astype(bf16)
     out_ref[scenarios:, :sep_rows] = jnp.zeros((NOTE_ROWS, sep_rows), bf16)
     for a in range(levels - 1):
         columns = pl.ds(sep_rows + a * panel_rows, panel_rows)
@@ -110,7 +166,7 @@
         )
 
 
-def hand_on_kernel(step, own_ref, received_ref, factor_ref, carry_ref):
+def hand_on(step, own_ref, received_ref, factor_ref, carry_ref):
     lower = ((lax.axis_index("leaf") >> step) & 1) == 0
     own, received = own_ref[...], received_ref[...]
     factor_ref[...] = jnp.where(lower, own, received)
@@ -157,54 +213,56 @@
     return solved, others
 
 
-def first_up_kernel(levels, panel_rows, own_ref, received_ref, factor_ref, solved_ref, out_ref):
-    k = lax.axis_index("leaf")
-    scenarios = own_ref.shape[0] - NOTE_ROWS
-    sep_rows = solved_ref.shape[1]
-    pending = [
-        own + received
-        for own, received in zip(
-            *(
-                spread_first(
-                    ref,
-                    jnp.minimum(own_level(who, levels), levels - 1),
-                    levels,
-                    scenarios,
-                    sep_rows,
-                    panel_rows,
-                )
-                for ref, who in ((own_ref, k), (received_ref, k ^ 1))
-            )
+def sums_of(own_ref, received, sep_rows):
+    return [
+        own_ref[:, a * sep_rows : (a + 1) * sep_rows] + value for a, value in enumerate(received)
+    ]
+
+
+def parts_of(ref, sep_rows):
+    return [
+        ref[:, low : low + sep_rows].astype(f32) for low in range(0, ref.shape[1], sep_rows)
+    ]
+
+
+def up_kernel(
+    levels,
+    now,
+    panel_rows,
+    own_ref,
+    received_ref,
+    factor_ref,
+    carry_ref,
+    arrived_ref,
+    solved_ref,
+    sums_ref,
+    out_ref,
+    next_factor_ref,
+    next_carry_ref=None,
+):
+    scenarios, sep_rows = solved_ref.shape
+    hand_on(now + 1, carry_ref, arrived_ref, next_factor_ref, next_carry_ref)
+    if now == 0:
+        partner = own_level(lax.axis_index("leaf") ^ 1, levels)
+        received = spread_first(
+            received_ref, jnp.minimum(partner, levels - 1), levels, scenarios, sep_rows, panel_rows
         )
-    ]
-    solved, others = solve_up(pending, factor_ref, panel_rows)
+    else:
+        received = parts_of(received_ref, sep_rows)
+    solved, others = solve_up(sums_of(own_ref, received, sep_rows), factor_ref, panel_rows)
     solved_ref[...] = solved
     for a, value in enumerate(others):
+        sums_ref[:, a * sep_rows : (a + 1) * sep_rows] = value
         out_ref[:, a * sep_rows : (a + 1) * sep_rows] = value.astype(bf16)
 
 
-def sums_of(own_ref, received_ref, sep_rows):
-    return [
-        own_ref[:, low : low + sep_rows].astype(f32)
-        + received_ref[:, low : low + sep_rows].astype(f32)
-        for low in range(0, own_ref.shape[1], sep_rows)
-    ]
-
-
-def up_kernel(panel_rows, own_ref, received_ref, factor_ref, solved_ref, out_ref):
-    sep_rows = solved_ref.shape[1]
-    pending = sums_of(own_ref, received_ref, sep_rows)
-    solved, others = solve_up(pending, factor_ref, panel_rows)
-    solved_ref[...] = solved
-    for a, value in enumerate(others):
-        out_ref[:, a * sep_rows : (a + 1) * sep_rows] = value.astype(bf16)
-
-
 def down_kernel(levels, *refs):
-    panel_ref, own_ref, received_ref, leaf_solved_ref, update_ref, inverse_ref = refs[:6]
+    panel_hbm, own_ref, received_ref, leaf_solved_ref, update_ref, inverse_ref = refs[:6]
     factor_refs = refs[6 : 6 + levels]
     solved_refs = refs[6 + levels : 5 + 2 * levels]
-    leaf_out_ref, sep_out_ref, work_ref = refs[5 + 2 * levels :]
+    leaf_out_ref, sep_out_ref, work_ref, panel_ref, sem = refs[5 + 2 * levels :]
+    copy = pltpu.make_async_copy(panel_hbm, panel_ref, sem)
+    copy.start()
     k = lax.axis_index("leaf")
     sep_rows = own_ref.shape[1]
     panel_rows = update_ref.shape[2]
@@ -212,7 +270,7 @@
     level = own_level(k, levels)
 
     top = levels - 1
-    pending = sums_of(own_ref, received_ref, sep_rows)
+    pending = sums_of(own_ref, parts_of(received_ref, sep_rows), sep_rows)
     solved, _ = solve_up(pending, factor_refs[top], panel_rows)
     ancestors = {}
     sep_out = jnp.zeros(sep_out_ref.shape, f32)
@@ -229,6 +287,7 @@
         sep_out = jnp.where(level == now, solution_now, sep_out)
     sep_out_ref[...] = sep_out
 
+    copy.wait()
     blocks = [picked(ancestors[a], panel_ref[0, a], count).astype(bf16) for a in range(levels)]
     size = inverse_ref.shape[0]
     step = min(256, size)
@@ -253,70 +312,72 @@
     tall = sep_rows + NOTE_ROWS
     leaf_update, sep_update = leaf_update[0], sep_update[0]
 
-    (carry,) = call(
-        partial(pack_kernel, levels),
-        [((tall, sep_rows + (levels - 1) * panel_rows), bf16)],
-        (sep_panel, sep_inverse, sep_update),
-        smem=(0,),
-    )
+    panel_smem = pltpu.SMEM(leaf_panel.shape, jnp.int32)
+    loaded = call(
+        partial(load_kernel, levels),
+        [
+            ((tall, sep_rows + (levels - 1) * panel_rows), bf16),
+            (leaf_rhs.shape, bf16),
+            (leaf_inverse.shape, bf16),
+            (leaf_update.shape, bf16),
+            (sep_rhs.shape, bf16),
+        ],
+        (sep_panel, sep_inverse, sep_update, leaf_rhs, leaf_inverse, leaf_update, sep_rhs),
+        hbm=range(7),
+        scratch=[panel_smem, pltpu.SemaphoreType.DMA((levels + 8 + size // 256,))],
+    )
+    carry, leaf_rhs, leaf_inverse, leaf_update, sep_rhs = loaded
     arrived = exchange(carry, 1)
-    leaf_solved, message = call(
+    leaf_solved, sums, message = call(
         partial(leaf_up_kernel, levels),
         [
             ((scenarios, size), f32),
+            ((scenarios, levels * sep_rows), f32),
             ((scenarios + NOTE_ROWS, sep_rows + (levels - 1) * panel_rows), bf16),
         ],
         (leaf_panel, leaf_rhs, leaf_inverse, leaf_update, sep_rhs),
-        smem=(0,),
+        hbm=(0,),
+        scratch=[panel_smem, pltpu.SemaphoreType.DMA],
         flops=2 * scenarios * size * (size + levels * panel_rows),
     )
-    factors, solved = [], []
-    for now in range(levels):
-        received = exchange(message, 1 << now)
-        shapes = [(carry.shape, bf16)]
-        if now + 1 < levels:
-            shapes.append(((tall, sep_rows + (levels - 2 - now) * panel_rows), bf16))
-            factor, carry = call(partial(hand_on_kernel, now), shapes, (carry, arrived))
-            arrived = exchange(carry, 2 << now)
-        else:
-            (factor,) = call(
-                lambda a, b, c, step=now: hand_on_kernel(step, a, b, c, None),
-                shapes,
-                (carry, arrived),
-            )
+
+    def carry_shape(now):
+        return ((tall, sep_rows + (levels - 1 - now) * panel_rows), bf16)
+
+    received = exchange(message, 1)
+    factor, carry = call(
+        partial(hand_on, 0), [carry_shape(0), carry_shape(1)], (carry, arrived)
+    )
+    factors, solved = [factor], []
+    for now in range(levels - 1):
+        arrived = exchange(carry, 2 << now)
+        shapes = [
+            ((scenarios, sep_rows), f32),
+            ((scenarios, (levels - 1 - now) * sep_rows), f32),
+            ((scenarios, (levels - 1 - now) * sep_rows), bf16),
+            carry_shape(now + 1),
+        ]
+        if now + 2 < levels:
+            shapes.append(carry_shape(now + 2))
+        results = call(
+            partial(up_kernel, levels, now, panel_rows),
+            shapes,
+            (sums, received, factor, carry, arrived),
+            flops=2 * scenarios * sep_rows * sep_rows * 2,
+        )
+        z, sums, message, factor = results[:4]
+        carry = results[4] if now + 2 < levels else None
+        solved.append(z)
         factors.append(factor)
-        if now + 1 < levels:
-            kernel = (
-                partial(first_up_kernel, levels, panel_rows)
-                if now == 0
-                else partial(up_kernel, panel_rows)
-            )
-            z, message = call(
-                kernel,
-                [
-                    ((scenarios, sep_rows), f32),
-                    ((scenarios, (levels - 1 - now) * sep_rows), bf16),
-                ],
-                (message, received, factor),
-                flops=2 * scenarios * sep_rows * sep_rows * 2,
-            )
-            solved.append(z)
-    args = (leaf_panel, message, received, leaf_solved, leaf_update, leaf_inverse)
-    args += tuple(factors) + tuple(solved)
-    kernel_args = args
-    leaf_out, sep_out = pl.pallas_call(
+        received = exchange(message, 2 << now)
+    return call(
         partial(down_kernel, levels),
-        out_shape=[
-            jax.ShapeDtypeStruct((scenarios, size), f32),
-            jax.ShapeDtypeStruct((scenarios, sep_rows), f32),
-        ],
-        in_specs=[pl.BlockSpec(memory_space=pltpu.SMEM)]
-        + [pl.BlockSpec(memory_space=pltpu.VMEM)] * (len(kernel_args) - 1),
-        out_specs=[pl.BlockSpec(memory_space=pltpu.VMEM)] * 2,
-        scratch_shapes=[pltpu.VMEM((scenarios, size), bf16)],
-        compiler_params=pltpu.CompilerParams(vmem_limit_bytes=40 << 20),
-    )(*kernel_args)
-    return leaf_out, sep_out
+        [((scenarios, size), f32), ((scenarios, sep_rows), f32)],
+        (leaf_panel, sums, received, leaf_solved, leaf_update, leaf_inverse, *factors, *solved),
+        hbm=(0,),
+        scratch=[pltpu.VMEM((scenarios, size), bf16), panel_smem, pltpu.SemaphoreType.DMA],
+        flops=2 * scenarios * size * (size + levels * panel_rows),
+    )
 
 
 def solution(mesh):

time: 50.1 us -> 38.8 us (0.77)
  waiting for transfers between devices: 26.7 us -> 18.5 us
  local copies, waits for them, and re-layouts: 7.82 us -> 0 us
  starting transfers between devices: 8.26 us -> 12.4 us
  Pallas kernels: 6.28 us -> 7.09 us
    ppermute x6, waiting for transfers between devices: 26.7 us -> 18.5 us  [exchange(): lax.ppermute(block, 'leaf', [(i, i ^ distance) for i in range(count)])]
    unnamed x22 -> x0, local copies, waits for them, and re-layouts: 7.82 us -> none
    ppermute x6, starting transfers between devices: 8.26 us -> 12.4 us  [exchange(): lax.ppermute(block, 'leaf', [(i, i ^ distance) for i in range(count)])]
    pallas_call x7 -> x6, Pallas kernels: 3.07 us -> 7.09 us  [call(): pl.pallas_call(kernel, out_shape=outs, in_specs=[pl.BlockSpec(memory_spac...]
    pallas_call x1 -> x0, Pallas kernels: 3.21 us -> none  [local(): pl.pallas_call(partial(down_kernel, levels), out_shape=[jax.ShapeDtypeStr...]
  transfers between devices with their start and end apart: 6 -> 6, of which waited for: 4 -> 6; matrix products, arithmetic and copies ran while one was open for 0% -> 0% of each run, Pallas kernels for 4% -> 3%
where the time goes in v2:
time: 38.8 us; the launch traced here: 38.6 us
  waiting for transfers between devices  18.5 us (48%)
  starting transfers between devices  12.4 us (32%)
  Pallas kernels  7.09 us (18%)
  between operations  0.67 us (2%)
    ppermute x6, waiting for transfers between devices, exchange(): lax.ppermute(block, 'leaf', [(i, i ^ distance) for i in range(count)])  18.5 us
    ppermute x6, starting transfers between devices, exchange(): lax.ppermute(block, 'leaf', [(i, i ^ distance) for i in range(count)])  12.4 us
    pallas_call x6, Pallas kernels, call(): pl.pallas_call(kernel, out_shape=outs, in_specs=[pl.BlockSpec(memory_spac...  7.09 us
  transfers between devices with their start and end apart: 6, of which 6 were waited for; matrix products, arithmetic and copies ran while one was open for 0% of the time, Pallas kernels for 3%

profile of v2, /device:TPU:0, one launch (start us, length us, event | category | flops | bytes accessed | tf_op | source)
XLA Modules:
  0.0 38.6 jit_solution(15975834819510106385)
XLA Ops:
  0.6 2.0 %shard_map.95 = (bf16[272,512]{1,0:T(8,128)(2,1)S(1)}, bf16[256,1024]{1,0:T(8,128)(2,1)S(1)}, bf16[1024,1024]{1,0:T(8,128)(2,1)S(1)}, bf16[3,1024,128]{2,1,0:T(8,128)(2,1)S(1)}, bf16[256,256]{1,0:T(8,128)(2,1)S(1)}) custom-call(s32[1,3]{1,0:T(1,128)} %panel_hbm.2, bf16[256,256]{1,0:T(8,128)(2,1)} %sep_inverse_hbm.1, bf16[3,256,128]{2,1,0:T(8,128)(2,1)} %bitcast.3, ...), custom_call_target="tpu_custom_call" | custom-call | bytes 7684108 | tf_op jit(solution)/shard_map/pallas_call | solution.py:53
  2.6 3.0 %collective-permute-start.1 = (bf16[272,512]{1,0:T(8,128)(2,1)S(1)}, bf16[272,512]{1,0:T(8,128)(2,1)S(1)}, u32[]{:S(2)}, u32[]{:S(2)}) collective-permute-start(bf16[272,512]{1,0:T(8,128)(2,1)S(1)} %get-tuple-element.27.own_ref), channel_id=1, source_target_pairs={{0,4},{4,0},{8,12},{12,8},{16,20},{20,16},{24,28},{28,24},{1,5},{5... | collective-permute-start | bytes 835592 | tf_op jit(solution)/shard_map/ppermute | solution.py:71
  5.6 1.2 %shard_map.96 = (f32[256,1024]{1,0:T(8,128)S(1)}, f32[256,768]{1,0:T(8,128)S(1)}, bf16[272,512]{1,0:T(8,128)(2,1)S(1)}) custom-call(s32[1,3]{1,0:T(1,128)} %refs_0_.1, bf16[256,1024]{1,0:T(8,128)(2,1)S(1)} %get-tuple-element.21.rhs_ref, bf16[1024,1024]{1,0:T(8,128)(2,1)S(1)} %get-tuple-element.22.inverse_ref.refs_5_, ...), custom_call_target="tpu_custom_call" | custom-call | flops 738197504 | bytes 5652492 | tf_op jit(solution)/shard_map/pallas_call | solution.py:53
  6.8 0.1 collective-permute-start
  6.9 6.2 %collective-permute-done.1.received_ref = bf16[272,512]{1,0:T(8,128)(2,1)S(1)} collective-permute-done((bf16[272,512]{1,0:T(8,128)(2,1)S(1)}, bf16[272,512]{1,0:T(8,128)(2,1)S(1)}, u32[]{:S(2)}, u32[]{:S(2)}) %collective-permute-start.1) | collective-permute-done | bytes 278560 | tf_op jit(solution)/shard_map/ppermute | solution.py:71
  13.1 0.1 shard_map.97
  13.2 2.2 %collective-permute-start.2 = (bf16[272,384]{1,0:T(8,128)(2,1)S(1)}, bf16[272,384]{1,0:T(8,128)(2,1)S(1)}, u32[]{:S(2)}, u32[]{:S(2)}) collective-permute-start(bf16[272,384]{1,0:T(8,128)(2,1)S(1)} %get-tuple-element.29.carry_ref), channel_id=1, source_target_pairs={{0,8},{4,12},{8,0},{12,4},{16,24},{20,28},{24,16},{28,20},{1,9},{5... | collective-permute-start | bytes 626696 | tf_op jit(solution)/shard_map/ppermute | solution.py:71
  15.4 2.9 %collective-permute-done.received_ref = bf16[272,512]{1,0:T(8,128)(2,1)S(1)} collective-permute-done((bf16[272,512]{1,0:T(8,128)(2,1)S(1)}, bf16[272,512]{1,0:T(8,128)(2,1)S(1)}, u32[]{:S(2)}, u32[]{:S(2)}) %collective-permute-start) | collective-permute-done | bytes 278560 | tf_op jit(solution)/shard_map/ppermute | solution.py:71
  18.3 0.9 %collective-permute-done.2.arrived_ref = bf16[272,384]{1,0:T(8,128)(2,1)S(1)} collective-permute-done((bf16[272,384]{1,0:T(8,128)(2,1)S(1)}, bf16[272,384]{1,0:T(8,128)(2,1)S(1)}, u32[]{:S(2)}, u32[]{:S(2)}) %collective-permute-start.2) | collective-permute-done | bytes 208928 | tf_op jit(solution)/shard_map/ppermute | solution.py:71
  19.2 0.4 %shard_map.98 = (f32[256,256]{1,0:T(8,128)S(1)}, f32[256,512]{1,0:T(8,128)S(1)}, bf16[256,512]{1,0:T(8,128)(2,1)S(1)}, bf16[272,384]{1,0:T(8,128)(2,1)S(1)}, bf16[272,256]{1,0:T(8,128)(2,1)S(1)}) custom-call(f32[256,768]{1,0:T(8,128)S(1)} %get-tuple-element.25.own_ref, bf16[272,512]{1,0:T(8,128)(2,1)S(1)} %collective-permute-done.received_ref, ...), custom_call_target="tpu_custom_call" | custom-call | flops 67108864 | bytes 3158016 | tf_op jit(solution)/shard_map/pallas_call | solution.py:53
  19.6 2.1 %collective-permute-start.3 = (bf16[256,512]{1,0:T(8,128)(2,1)S(1)}, bf16[256,512]{1,0:T(8,128)(2,1)S(1)}, u32[]{:S(2)}, u32[]{:S(2)}) collective-permute-start(bf16[256,512]{1,0:T(8,128)(2,1)S(1)} %get-tuple-element.31), channel_id=1, source_target_pairs={{0,8},{4,12},{8,0},{12,4},{16,24},{20,28},{24,16},{28,20},{1,9},{5... | collective-permute-start | bytes 786440 | tf_op jit(solution)/shard_map/ppermute | solution.py:71
  21.7 2.6 %collective-permute-start.4 = (bf16[272,256]{1,0:T(8,128)(2,1)S(1)}, bf16[272,256]{1,0:T(8,128)(2,1)S(1)}, u32[]{:S(2)}, u32[]{:S(2)}) collective-permute-start(bf16[272,256]{1,0:T(8,128)(2,1)S(1)} %get-tuple-element.33.carry_ref), channel_id=1, source_target_pairs={{0,16},{4,20},{8,24},{12,28},{16,0},{20,4},{24,8},{28,12},{1,17},{... | collective-permute-start | bytes 417800 | tf_op jit(solution)/shard_map/ppermute | solution.py:71
  24.3 4.4 %collective-permute-done.4.arrived_ref = bf16[272,256]{1,0:T(8,128)(2,1)S(1)} collective-permute-done((bf16[272,256]{1,0:T(8,128)(2,1)S(1)}, bf16[272,256]{1,0:T(8,128)(2,1)S(1)}, u32[]{:S(2)}, u32[]{:S(2)}) %collective-permute-start.4) | collective-permute-done | bytes 139296 | tf_op jit(solution)/shard_map/ppermute | solution.py:71
  28.7 0.6 %collective-permute-done.3.received_ref = bf16[256,512]{1,0:T(8,128)(2,1)S(1)} collective-permute-done((bf16[256,512]{1,0:T(8,128)(2,1)S(1)}, bf16[256,512]{1,0:T(8,128)(2,1)S(1)}, u32[]{:S(2)}, u32[]{:S(2)}) %collective-permute-start.3) | collective-permute-done | bytes 262176 | tf_op jit(solution)/shard_map/ppermute | solution.py:71
  29.3 0.4 shard_map.99
  29.7 2.4 %collective-permute-start.5 = (bf16[256,256]{1,0:T(8,128)(2,1)S(1)}, bf16[256,256]{1,0:T(8,128)(2,1)S(1)}, u32[]{:S(2)}, u32[]{:S(2)}) collective-permute-start(bf16[256,256]{1,0:T(8,128)(2,1)S(1)} %get-tuple-element.35), channel_id=1, source_target_pairs={{0,16},{4,20},{8,24},{12,28},{16,0},{20,4},{24,8},{28,12},{1,17},{... | collective-permute-start | bytes 393224 | tf_op jit(solution)/shard_map/ppermute | solution.py:71
  32.1 3.5 %collective-permute-done.5.refs_2_ = bf16[256,256]{1,0:T(8,128)(2,1)S(1)} collective-permute-done((bf16[256,256]{1,0:T(8,128)(2,1)S(1)}, bf16[256,256]{1,0:T(8,128)(2,1)S(1)}, u32[]{:S(2)}, u32[]{:S(2)}) %collective-permute-start.5) | collective-permute-done | bytes 131104 | tf_op jit(solution)/shard_map/ppermute | solution.py:71
  35.6 3.1 %shard_map.100 = (f32[256,1024]{1,0:T(8,128)}, f32[256,256]{1,0:T(8,128)}) custom-call(s32[1,3]{1,0:T(1,128)} %refs_0_.1, f32[256,256]{1,0:T(8,128)S(1)} %get-tuple-element.34.refs_1_, bf16[256,256]{1,0:T(8,128)(2,1)S(1)} %collective-permute-done.5.refs_2_, f32[256,1024]{1,0:T(8,128)S(1)} %get-tuple-element.36.refs_3_, ...), custom_call_target="tpu_custom_call" | custom-call | flops 738197504 | bytes 6787084 | tf_op jit(solution)/shard_map/pallas_call | solution.py:53
Async XLA Ops:
  2.6 10.5 %collective-permute-start.1 = (bf16[272,512]{1,0:T(8,128)(2,1)S(1)}, bf16[272,512]{1,0:T(8,128)(2,1)S(1)}, u32[]{:S(2)}, u32[]{:S(2)}) collective-permute-start(bf16[272,512]{1,0:T(8,128)(2,1)S(1)} %get-tuple-element.27.own_ref), channel_id=1, source_target_pairs={{0,4},{4,0},{8,12},{12,8},{16,20},{20,16},{24,28},{28,24},{1,5},{5... | collective-permute-start | bytes 835592 | tf_op jit(solution)/shard_map/ppermute | solution.py:71
  6.8 11.4 %collective-permute-start = (bf16[272,512]{1,0:T(8,128)(2,1)S(1)}, bf16[272,512]{1,0:T(8,128)(2,1)S(1)}, u32[]{:S(2)}, u32[]{:S(2)}) collective-permute-start(bf16[272,512]{1,0:T(8,128)(2,1)S(1)} %get-tuple-element.26), channel_id=1, source_target_pairs={{0,4},{4,0},{8,12},{12,8},{16,20},{20,16},{24,28},{28,24},{1,5},{5... | collective-permute-start | bytes 835592 | tf_op jit(solution)/shard_map/ppermute | solution.py:71
  13.2 6.0 %collective-permute-start.2 = (bf16[272,384]{1,0:T(8,128)(2,1)S(1)}, bf16[272,384]{1,0:T(8,128)(2,1)S(1)}, u32[]{:S(2)}, u32[]{:S(2)}) collective-permute-start(bf16[272,384]{1,0:T(8,128)(2,1)S(1)} %get-tuple-element.29.carry_ref), channel_id=1, source_target_pairs={{0,8},{4,12},{8,0},{12,4},{16,24},{20,28},{24,16},{28,20},{1,9},{5... | collective-permute-start | bytes 626696 | tf_op jit(solution)/shard_map/ppermute | solution.py:71
  19.6 9.7 %collective-permute-start.3 = (bf16[256,512]{1,0:T(8,128)(2,1)S(1)}, bf16[256,512]{1,0:T(8,128)(2,1)S(1)}, u32[]{:S(2)}, u32[]{:S(2)}) collective-permute-start(bf16[256,512]{1,0:T(8,128)(2,1)S(1)} %get-tuple-element.31), channel_id=1, source_target_pairs={{0,8},{4,12},{8,0},{12,4},{16,24},{20,28},{24,16},{28,20},{1,9},{5... | collective-permute-start | bytes 786440 | tf_op jit(solution)/shard_map/ppermute | solution.py:71
  21.7 7.0 %collective-permute-start.4 = (bf16[272,256]{1,0:T(8,128)(2,1)S(1)}, bf16[272,256]{1,0:T(8,128)(2,1)S(1)}, u32[]{:S(2)}, u32[]{:S(2)}) collective-permute-start(bf16[272,256]{1,0:T(8,128)(2,1)S(1)} %get-tuple-element.33.carry_ref), channel_id=1, source_target_pairs={{0,16},{4,20},{8,24},{12,28},{16,0},{20,4},{24,8},{28,12},{1,17},{... | collective-permute-start | bytes 417800 | tf_op jit(solution)/shard_map/ppermute | solution.py:71
  29.7 5.9 %collective-permute-start.5 = (bf16[256,256]{1,0:T(8,128)(2,1)S(1)}, bf16[256,256]{1,0:T(8,128)(2,1)S(1)}, u32[]{:S(2)}, u32[]{:S(2)}) collective-permute-start(bf16[256,256]{1,0:T(8,128)(2,1)S(1)} %get-tuple-element.35), channel_id=1, source_target_pairs={{0,16},{4,20},{8,24},{12,28},{16,0},{20,4},{24,8},{28,12},{1,17},{... | collective-permute-start | bytes 393224 | tf_op jit(solution)/shard_map/ppermute | solution.py:71

commit v3 on v2

v3 whole, which is shorter than its diff:
```python
from functools import partial

import jax
import jax.numpy as jnp
from jax import lax
from jax.experimental import pallas as pl
from jax.experimental.pallas import tpu as pltpu
from jax.sharding import PartitionSpec as P

NOTE_ROWS = 16
GROUPS = 2
f32, bf16 = jnp.float32, jnp.bfloat16


def dot(a, b):
    return jnp.dot(a, b, preferred_element_type=f32)


def dot_t(a, b):
    return lax.dot_general(a, b, (((1,), (1,)), ((), ())), preferred_element_type=f32)


def own_level(k, levels):
    level = jnp.int32(0)
    for bit in range(levels):
        low = (2 << bit) - 1
        level = jnp.where((k & low) == low, bit + 1, level)
    return level


def placed(block, panel, count):
    return jnp.concatenate(
        [jnp.where(panel == p, block, jnp.zeros_like(block)) for p in range(count)], axis=1
    )


def picked(vectors, panel, count):
    width = vectors.shape[1] // count
    result = vectors[:, :width]
    for p in range(1, count):
        result = jnp.where(panel == p, vectors[:, p * width : (p + 1) * width], result)
    return result


def call(kernel, outs, args, hbm=(), hbm_outs=False, aliases=None, scratch=(), flops=0):
    def bytes_of(arrays):
        return sum(a.size * a.dtype.itemsize for a in arrays)

    outs = [jax.ShapeDtypeStruct(shape, dtype) for shape, dtype in outs]
    args = [
        pltpu.with_memory_space_constraint(arg, pltpu.HBM) if i in hbm else arg
        for i, arg in enumerate(args)
    ]
    return pl.pallas_call(
        kernel,
        out_shape=outs,
        in_specs=[
            pl.BlockSpec(memory_space=pltpu.HBM if i in hbm else pltpu.VMEM)
            for i in range(len(args))
        ],
        out_specs=[pl.BlockSpec(memory_space=pltpu.HBM if hbm_outs else pltpu.VMEM) for _ in outs],
        input_output_aliases=aliases or {},
        scratch_shapes=scratch,
        compiler_params=pltpu.CompilerParams(vmem_limit_bytes=40 << 20),
        cost_estimate=pl.CostEstimate(
            flops=flops, bytes_accessed=bytes_of(args) + bytes_of(outs), transcendentals=0
        ),
    )(*args)


def exchange(block, distance, axis="leaf"):
    count = lax.axis_size(axis)
    return lax.ppermute(block, axis, [(i, i ^ distance) for i in range(count)])


def upper_part():
    return lax.axis_index("rhs") & 1


def leaf_up_kernel(
    levels,
    sep_panel_hbm,
    leaf_panel_hbm,
    sep_inverse_hbm,
    sep_update_hbm,
    leaf_rhs_hbm,
    leaf_inverse_hbm,
    leaf_update_hbm,
    sep_rhs_hbm,
    carry_ref,
    leaf_inverse_ref,
    leaf_update_ref,
    solved_ref,
    own_ref,
    *refs,
):
    out_refs = refs[:GROUPS]
    sep_panel_ref, leaf_panel_ref, leaf_rhs_ref, sep_rhs_ref, sems = refs[GROUPS:]
    k = lax.axis_index("leaf")
    scenarios, sep_rows = sep_rhs_hbm.shape
    size, panel_rows = leaf_inverse_hbm.shape[0], leaf_update_hbm.shape[2]
    count = sep_rows // panel_rows
    half = sep_rows // 2
    step = min(256, size)

    started = []

    def bring(source, target):
        copy = pltpu.make_async_copy(source, target, sems.at[len(started)])
        copy.start()
        started.append(copy)
        return copy

    rhs_copy = bring(leaf_rhs_hbm, leaf_rhs_ref)
    inverse_copies = []
    for low in range(0, size, step):
        block = (pl.ds(low, step), pl.ds(0, low + step))
        inverse_copies.append(bring(leaf_inverse_hbm.at[block], leaf_inverse_ref.at[block]))
    update_copy = bring(leaf_update_hbm, leaf_update_ref)
    leaf_panel_copy = bring(leaf_panel_hbm, leaf_panel_ref)
    sep_rhs_copy = bring(sep_rhs_hbm, sep_rhs_ref)
    sep_panel_copy = bring(sep_panel_hbm, sep_panel_ref)
    first_row = pl.multiple_of(upper_part() * half, half)
    factor_copies = [
        bring(
            sep_inverse_hbm.at[pl.ds(first_row, half)],
            carry_ref.at[pl.ds(0, half), pl.ds(0, sep_rows)],
        )
    ]
    for a in range(1, levels):
        columns = pl.ds(sep_rows + (a - 1) * panel_rows, panel_rows)
        factor_copies.append(
            bring(
                sep_update_hbm.at[a, pl.ds(first_row, half)],
                carry_ref.at[pl.ds(0, half), columns],
            )
        )

    rhs_copy.wait()
    rounded = []
    for low, copy in zip(range(0, size, step), inverse_copies):
        high = low + step
        copy.wait()
        value = dot_t(leaf_rhs_ref[:, :high], leaf_inverse_ref[low:high, :high])
        solved_ref[:, low:high] = value
        rounded.append(value.astype(bf16))
    rounded = jnp.concatenate(rounded, axis=1)
    update_copy.wait()
    together = dot(
        rounded, jnp.concatenate([leaf_update_ref[a] for a in range(levels)], axis=1)
    )
    terms = [together[:, a * panel_rows : (a + 1) * panel_rows] for a in range(levels)]

    level = own_level(k, levels)
    wide_level = jnp.minimum(level, levels - 1)
    sep_rhs_copy.wait()
    leaf_panel_copy.wait()
    rhs = jnp.where(level < levels, sep_rhs_ref[...].astype(f32), 0.0)
    wide = jnp.zeros((scenarios, sep_rows), f32)
    for a in range(levels):
        spread = placed(terms[a], leaf_panel_ref[0, a], count)
        spread = jnp.where(wide_level == a, spread - rhs, spread)
        wide = jnp.where(wide_level == a, spread, wide)
        own_ref[:, a * sep_rows : (a + 1) * sep_rows] = spread
    rows = scenarios // GROUPS
    for group, out_ref in enumerate(out_refs):
        low = group * rows
        out_ref[:rows, :sep_rows] = wide[low : low + rows].astype(bf16)
        out_ref[rows:, :sep_rows] = jnp.zeros((NOTE_ROWS, sep_rows), bf16)
        for a in range(levels - 1):
            columns = pl.ds(sep_rows + a * panel_rows, panel_rows)
            later = wide_level <= a
            narrow = jnp.where(later, terms[a + 1], terms[a])
            out_ref[:rows, columns] = narrow[low : low + rows].astype(bf16)
            panel = jnp.where(later, leaf_panel_ref[0, a + 1], leaf_panel_ref[0, a])
            out_ref[rows:, columns] = jnp.full((NOTE_ROWS, panel_rows), panel.astype(f32)).astype(
                bf16
            )

    sep_panel_copy.wait()
    carry_ref[half:, :sep_rows] = jnp.zeros((NOTE_ROWS, sep_rows), bf16)
    for a in range(1, levels):
        columns = pl.ds(sep_rows + (a - 1) * panel_rows, panel_rows)
        carry_ref[half:, columns] = jnp.full(
            (NOTE_ROWS, panel_rows), sep_panel_ref[0, a].astype(f32)
        ).astype(bf16)
    for copy in factor_copies:
        copy.wait()


def hand_on_kernel(step, sep_rows, own_ref, received_ref, factor_ref, carry_ref=None):
    lower = ((lax.axis_index("leaf") >> step) & 1) == 0
    own, received = own_ref[...], received_ref[...]
    factor_ref[...] = jnp.where(lower, own, received)
    if carry_ref is not None:
        skipped = own.shape[1] - carry_ref.shape[1]
        following = jnp.where(lower, received, own)
        carry_ref[:, :sep_rows] = following[:, :sep_rows]
        if carry_ref.shape[1] > sep_rows:
            carry_ref[:, sep_rows:] = following[:, sep_rows + skipped :]


class Factor:
    def __init__(self, own_ref, other_ref, sep_rows, panel_rows):
        self.refs = own_ref, other_ref
        self.sep_rows, self.panel_rows = sep_rows, panel_rows
        self.half = own_ref.shape[0] - NOTE_ROWS

    def columns(self, start, size):
        own, other = (ref[: self.half, start : start + size] for ref in self.refs)
        upper = upper_part() == 1
        return jnp.concatenate([jnp.where(upper, other, own), jnp.where(upper, own, other)], axis=0)

    def inverse(self):
        return self.columns(0, self.sep_rows)

    def updates(self, count):
        return self.columns(self.sep_rows, count * self.panel_rows)

    def panel(self, index):
        start = self.sep_rows + index * self.panel_rows
        notes = self.refs[0][self.half : self.half + NOTE_ROWS, start : start + self.panel_rows]
        return notes.astype(f32)[:1]


def spread_first(message_ref, wide_level, levels, rows, sep_rows, panel_rows):
    count = sep_rows // panel_rows
    wide = message_ref[:rows, :sep_rows].astype(f32)
    narrow = []
    for a in range(levels - 1):
        columns = pl.ds(sep_rows + a * panel_rows, panel_rows)
        panel = message_ref[rows : rows + NOTE_ROWS, columns].astype(f32)[:1]
        narrow.append(placed(message_ref[:rows, columns].astype(f32), panel, count))
    sums = []
    for a in range(levels):
        value = wide
        if a > 0:
            value = jnp.where(wide_level < a, narrow[a - 1], value)
        if a < levels - 1:
            value = jnp.where(wide_level > a, narrow[a], value)
        sums.append(value)
    return sums


def solve_up(pending, factor):
    count = factor.sep_rows // factor.panel_rows
    solved = dot_t((-pending[0]).astype(bf16), factor.inverse())
    others = []
    if len(pending) > 1:
        updates = dot(solved.astype(bf16), factor.updates(len(pending) - 1))
        for a, value in enumerate(pending[1:]):
            update = updates[:, a * factor.panel_rows : (a + 1) * factor.panel_rows]
            others.append(value + placed(update, factor.panel(a), count))
    return solved, others


def sums_of(own_ref, first, received):
    rows, sep_rows = received[0].shape
    return [
        own_ref[first : first + rows, a * sep_rows : (a + 1) * sep_rows] + value
        for a, value in enumerate(received)
    ]


def parts_of(ref, sep_rows):
    return [ref[:, low : low + sep_rows].astype(f32) for low in range(0, ref.shape[1], sep_rows)]


def up_kernel(
    levels,
    now,
    first,
    panel_rows,
    own_ref,
    received_ref,
    factor_ref,
    other_ref,
    solved_ref,
    sums_ref,
    out_ref,
):
    rows, sep_rows = solved_ref.shape
    if now == 0:
        partner = jnp.minimum(own_level(lax.axis_index("leaf") ^ 1, levels), levels - 1)
        received = spread_first(received_ref, partner, levels, rows, sep_rows, panel_rows)
    else:
        received = parts_of(received_ref, sep_rows)
    factor = Factor(factor_ref, other_ref, sep_rows, panel_rows)
    solved, others = solve_up(sums_of(own_ref, first, received), factor)
    solved_ref[...] = solved
    for a, value in enumerate(others):
        sums_ref[:, a * sep_rows : (a + 1) * sep_rows] = value
        out_ref[:, a * sep_rows : (a + 1) * sep_rows] = value.astype(bf16)


def down_kernel(levels, first, earlier, *refs):
    panel_hbm, own_ref, received_ref, leaf_solved_ref, update_ref, inverse_ref = refs[:6]
    factor_refs = refs[6 : 6 + 2 * levels]
    solved_refs = refs[6 + 2 * levels : 5 + 3 * levels]
    refs = refs[5 + 3 * levels + (2 if earlier else 0) :]
    leaf_out_hbm, sep_out_hbm, work_ref, leaf_out_ref, sep_out_ref, panel_ref, sems = refs
    copy = pltpu.make_async_copy(panel_hbm, panel_ref, sems.at[0])
    copy.start()
    k = lax.axis_index("leaf")
    rows, sep_rows = own_ref.shape
    panel_rows = update_ref.shape[2]
    count = sep_rows // panel_rows
    level = own_level(k, levels)
    factors = [
        Factor(factor_refs[2 * now], factor_refs[2 * now + 1], sep_rows, panel_rows)
        for now in range(levels)
    ]

    top = levels - 1
    pending = sums_of(own_ref, 0, parts_of(received_ref, sep_rows))
    solved, _ = solve_up(pending, factors[top])
    ancestors = {}
    sep_out = jnp.zeros((rows, sep_rows), f32)
    for now in reversed(range(levels)):
        factor = factors[now]
        residual = solved
        if now < top:
            blocks = [
                picked(ancestors[a], factor.panel(a - now - 1), count).astype(bf16)
                for a in range(now + 1, levels)
            ]
            residual = solved_refs[now][...] - dot_t(
                jnp.concatenate(blocks, axis=1), factor.updates(top - now)
            )
        solution_now = dot(residual.astype(bf16), factor.inverse())
        ancestors[now] = solution_now.astype(bf16).astype(f32)
        sep_out = jnp.where(level == now, solution_now, sep_out)
    sep_out_ref[...] = sep_out
    here = pl.ds(first, rows)
    leaving = [pltpu.make_async_copy(sep_out_ref, sep_out_hbm.at[here], sems.at[1])]
    leaving[0].start()

    copy.wait()
    blocks = jnp.concatenate(
        [picked(ancestors[a], panel_ref[0, a], count).astype(bf16) for a in range(levels)], axis=1
    )
    size = inverse_ref.shape[0]
    step = min(256, size)
    for low in range(0, size, step):
        high = low + step
        updates = jnp.concatenate([update_ref[a, low:high, :] for a in range(levels)], axis=1)
        value = leaf_solved_ref[first : first + rows, low:high] - dot_t(blocks, updates)
        work_ref[:, low:high] = value.astype(bf16)
    for low in range(0, size, step):
        high = low + step
        leaf_out_ref[:, low:high] = dot(work_ref[:, low:], inverse_ref[low:, low:high])
        columns = pl.ds(low, step)
        leaving.append(
            pltpu.make_async_copy(
                leaf_out_ref.at[:, columns],
                leaf_out_hbm.at[here, columns],
                sems.at[len(leaving) + 1],
            )
        )
        leaving[-1].start()
    for copy in leaving:
        copy.wait()


def local(
    leaf_rhs, sep_rhs, leaf_inverse, leaf_update, leaf_panel, sep_inverse, sep_update, sep_panel
):
    levels = lax.axis_size("leaf").bit_length() - 1
    sep_rows = sep_inverse.shape[0]
    scenarios, size = leaf_rhs.shape
    panel_rows = leaf_update.shape[3]
    rows = scenarios // GROUPS
    panel_smem = pltpu.SMEM(leaf_panel.shape, jnp.int32)
    sems = pltpu.SemaphoreType.DMA((levels + 8 + size // min(256, size),))

    def carry_shape(now):
        width = sep_rows + (levels - 1 - now) * panel_rows
        return ((sep_rows // 2 + NOTE_ROWS, width), bf16)

    results = call(
        partial(leaf_up_kernel, levels),
        [
            carry_shape(0),
            (leaf_inverse.shape, bf16),
            (leaf_update.shape[1:], bf16),
            ((scenarios, size), f32),
            ((scenarios, levels * sep_rows), f32),
        ]
        + [((rows + NOTE_ROWS, sep_rows + (levels - 1) * panel_rows), bf16)] * GROUPS,
        (
            sep_panel,
            leaf_panel,
            sep_inverse,
            sep_update[0],
            leaf_rhs,
            leaf_inverse,
            leaf_update[0],
            sep_rhs,
        ),
        hbm=range(8),
        scratch=[
            panel_smem,
            panel_smem,
            pltpu.VMEM(leaf_rhs.shape, bf16),
            pltpu.VMEM(sep_rhs.shape, bf16),
            sems,
        ],
        flops=2 * scenarios * size * (size + levels * panel_rows),
    )
    carry, leaf_inverse, leaf_update, leaf_solved, own = results[:5]
    sums, messages = [own] * GROUPS, results[5:]
    arrived = exchange(carry, 1)
    received = [exchange(message, 1) for message in messages]
    factors, solved = [], [[] for _ in range(GROUPS)]
    for now in range(levels):
        shapes = [carry_shape(now)]
        if now + 1 < levels:
            shapes.append(carry_shape(now + 1))
        handed = call(partial(hand_on_kernel, now, sep_rows), shapes, (carry, arrived))
        factors += [handed[0], exchange(handed[0], 1, "rhs")]
        if now + 1 == levels:
            break
        carry = handed[1]
        arrived = exchange(carry, 2 << now)
        for group in range(GROUPS):
            z, sums[group], message = call(
                partial(up_kernel, levels, now, group * rows if now == 0 else 0, panel_rows),
                [
                    ((rows, sep_rows), f32),
                    ((rows, (levels - 1 - now) * sep_rows), f32),
                    ((rows, (levels - 1 - now) * sep_rows), bf16),
                ],
                (sums[group], received[group], *factors[-2:]),
                flops=2 * rows * sep_rows * sep_rows * 2,
            )
            solved[group].append(z)
            received[group] = exchange(message, 2 << now)
    outputs = []
    for group in range(GROUPS):
        args = (leaf_panel, sums[group], received[group], leaf_solved, leaf_update, leaf_inverse)
        args += (*factors, *solved[group])
        count = len(args)
        outputs = call(
            partial(down_kernel, levels, group * rows, group > 0),
            [((scenarios, size), f32), ((scenarios, sep_rows), f32)],
            args + tuple(outputs),
            hbm=(0, count, count + 1),
            hbm_outs=True,
            aliases={count: 0, count + 1: 1} if group else None,
            scratch=[
                pltpu.VMEM((rows, size), bf16),
                pltpu.VMEM((rows, size), f32),
                pltpu.VMEM((rows, sep_rows), f32),
                panel_smem,
                sems,
            ],
            flops=2 * rows * size * (size + levels * panel_rows),
        )
    return tuple(outputs)


def solution(mesh):
    return jax.shard_map(
        local,
        mesh=mesh,
        in_specs=(
            P("rhs", "leaf"),
            P("rhs", "leaf"),
            P("leaf", None),
            P("leaf", None, None, None),
            P("leaf", None),
            P("leaf", None),
            P("leaf", None, None, None),
            P("leaf", None),
        ),
        out_specs=(P("rhs", "leaf"), P("rhs", "leaf")),
        check_vma=False,
    )
```

time: 38.8 us -> 41.2 us (1.062)
  waiting for transfers between devices: 18.5 us -> 15.3 us
  Pallas kernels: 7.09 us -> 9.97 us
  starting transfers between devices: 12.4 us -> 15 us
    ppermute x6 -> x12, waiting for transfers between devices: 18.5 us -> 15.3 us  [exchange(): return lax.ppermute(block, axis, [(i, i ^ distance) for i in range(count)])]
    pallas_call x6 -> x10, Pallas kernels: 7.09 us -> 9.97 us  [call(): pl.pallas_call(kernel, out_shape=outs, in_specs=[pl.BlockSpec(memory_spac...]
    ppermute x6 -> x12, starting transfers between devices: 12.4 us -> 15 us  [exchange(): return lax.ppermute(block, axis, [(i, i ^ distance) for i in range(count)])]
  transfers between devices with their start and end apart: 6 -> 12, of which waited for: 6 -> 5; matrix products, arithmetic and copies ran while one was open for 0% -> 0% of each run, Pallas kernels for 3% -> 10%
where the time goes in v3:
time: 41.2 us; the launch traced here: 41.1 us
  waiting for transfers between devices  15.3 us (37%)
  starting transfers between devices  15 us (36%)
  Pallas kernels  9.97 us (24%)
  between operations  0.75 us (2%)
    ppermute x12, waiting for transfers between devices, exchange(): return lax.ppermute(block, axis, [(i, i ^ distance) for i in range(count)])  15.3 us
    ppermute x12, starting transfers between devices, exchange(): return lax.ppermute(block, axis, [(i, i ^ distance) for i in range(count)])  15 us
    pallas_call x10, Pallas kernels, call(): pl.pallas_call(kernel, out_shape=outs, in_specs=[pl.BlockSpec(memory_spac...  9.97 us
  transfers between devices with their start and end apart: 12, of which 5 were waited for; matrix products, arithmetic and copies ran while one was open for 0% of the time, Pallas kernels for 10%

profile of v3, /device:TPU:0, one launch (start us, length us, event | category | flops | bytes accessed | tf_op | source)
XLA Modules:
  0.0 41.1 jit_solution(8619973743886909332)
XLA Ops:
  0.6 3.3 %shard_map.95 = (bf16[144,512]{1,0:T(8,128)(2,1)S(1)}, bf16[1024,1024]{1,0:T(8,128)(2,1)S(1)}, bf16[3,1024,128]{2,1,0:T(8,128)(2,1)S(1)}, f32[256,1024]{1,0:T(8,...) custom-call(s32[1,3]{1,0:T(1,128)} %sep_panel_hbm.1, ...), custom_call_target="tpu_custom_call" | custom-call | flops 738197504 | bytes 9027608 | tf_op jit(solution)/shard_map/pallas_call | solution.py:54
  3.9 3.0 %collective-permute-start.1 = (bf16[144,512]{1,0:T(8,128)(2,1)S(1)}, bf16[144,512]{1,0:T(8,128)(2,1)S(1)}, u32[]{:S(2)}, u32[]{:S(2)}) collective-permute-start(bf16[144,512]{1,0:T(8,128)(2,1)S(1)} %get-tuple-element.29.own_ref), channel_id=1, source_target_pairs={{0,4},{4,0},{8,12},{12,8},{16,20},{20,16},{24,28},{28,24},{1,5},{5... | collective-permute-start | bytes 442376 | tf_op jit(solution)/shard_map/ppermute | solution.py:73
  7.0 0.1 collective-permute-start.9
  7.1 4.6 %collective-permute-done.1.received_ref = bf16[144,512]{1,0:T(8,128)(2,1)S(1)} collective-permute-done((bf16[144,512]{1,0:T(8,128)(2,1)S(1)}, bf16[144,512]{1,0:T(8,128)(2,1)S(1)}, u32[]{:S(2)}, u32[]{:S(2)}) %collective-permute-start.1) | collective-permute-done | bytes 147488 | tf_op jit(solution)/shard_map/ppermute | solution.py:73
  11.7 0.1 collective-permute-start.2
  11.8 2.1 %collective-permute-start = (bf16[144,512]{1,0:T(8,128)(2,1)S(1)}, bf16[144,512]{1,0:T(8,128)(2,1)S(1)}, u32[]{:S(2)}, u32[]{:S(2)}) collective-permute-start(bf16[144,512]{1,0:T(8,128)(2,1)S(1)} %get-tuple-element.28), channel_id=1, source_target_pairs={{0,4},{4,0},{8,12},{12,8},{16,20},{20,16},{24,28},{28,24},{1,5},{5... | collective-permute-start | bytes 442376 | tf_op jit(solution)/shard_map/ppermute | solution.py:73
  13.9 1.6 %collective-permute-start.4 = (bf16[144,384]{1,0:T(8,128)(2,1)S(1)}, bf16[144,384]{1,0:T(8,128)(2,1)S(1)}, u32[]{:S(2)}, u32[]{:S(2)}) collective-permute-start(bf16[144,384]{1,0:T(8,128)(2,1)S(1)} %get-tuple-element.33.own_ref), channel_id=1, source_target_pairs={{0,8},{4,12},{8,0},{12,4},{16,24},{20,28},{24,16},{28,20},{1,9},{5... | collective-permute-start | bytes 331784 | tf_op jit(solution)/shard_map/ppermute | solution.py:73
  15.5 0.0 collective-permute-done.9.received_ref
  15.5 0.0 collective-permute-done.2.other_ref.refs_7_
  15.5 0.3 shard_map.101
  15.8 0.5 %collective-permute-start.10 = (bf16[128,512]{1,0:T(8,128)(2,1)S(1)}, bf16[128,512]{1,0:T(8,128)(2,1)S(1)}, u32[]{:S(2)}, u32[]{:S(2)}) collective-permute-start(bf16[128,512]{1,0:T(8,128)(2,1)S(1)} %get-tuple-element.45), channel_id=1, source_target_pairs={{0,8},{4,12},{8,0},{12,4},{16,24},{20,28},{24,16},{28,20},{1,9},{5... | collective-permute-start | bytes 393224 | tf_op jit(solution)/shard_map/ppermute | solution.py:73
  16.4 3.3 %collective-permute-done.4.received_ref = bf16[144,384]{1,0:T(8,128)(2,1)S(1)} collective-permute-done((bf16[144,384]{1,0:T(8,128)(2,1)S(1)}, bf16[144,384]{1,0:T(8,128)(2,1)S(1)}, u32[]{:S(2)}, u32[]{:S(2)}) %collective-permute-start.4) | collective-permute-done | bytes 110624 | tf_op jit(solution)/shard_map/ppermute | solution.py:73
  19.7 0.1 collective-permute-start.5
  19.8 0.0 collective-permute-done.received_ref
  19.8 0.3 shard_map.97
  20.2 1.8 %collective-permute-start.3 = (bf16[128,512]{1,0:T(8,128)(2,1)S(1)}, bf16[128,512]{1,0:T(8,128)(2,1)S(1)}, u32[]{:S(2)}, u32[]{:S(2)}) collective-permute-start(bf16[128,512]{1,0:T(8,128)(2,1)S(1)} %get-tuple-element.32), channel_id=1, source_target_pairs={{0,8},{4,12},{8,0},{12,4},{16,24},{20,28},{24,16},{28,20},{1,9},{5... | collective-permute-start | bytes 393224 | tf_op jit(solution)/shard_map/ppermute | solution.py:73
  21.9 2.6 %collective-permute-start.7 = (bf16[144,256]{1,0:T(8,128)(2,1)S(1)}, bf16[144,256]{1,0:T(8,128)(2,1)S(1)}, u32[]{:S(2)}, u32[]{:S(2)}) collective-permute-start(bf16[144,256]{1,0:T(8,128)(2,1)S(1)} %get-tuple-element.40.own_ref), channel_id=1, source_target_pairs={{0,16},{4,20},{8,24},{12,28},{16,0},{20,4},{24,8},{28,12},{1,17},{... | collective-permute-start | bytes 221192 | tf_op jit(solution)/shard_map/ppermute | solution.py:73
  24.5 2.8 %collective-permute-done.7.received_ref = bf16[144,256]{1,0:T(8,128)(2,1)S(1)} collective-permute-done((bf16[144,256]{1,0:T(8,128)(2,1)S(1)}, bf16[144,256]{1,0:T(8,128)(2,1)S(1)}, u32[]{:S(2)}, u32[]{:S(2)}) %collective-permute-start.7) | collective-permute-done | bytes 73760 | tf_op jit(solution)/shard_map/ppermute | solution.py:73
  27.3 0.1 collective-permute-start.8
  27.4 0.0 collective-permute-done.5.other_ref.refs_9_
  27.4 0.0 collective-permute-done.10.received_ref
  27.4 0.3 shard_map.102
  27.8 3.1 %collective-permute-start.11 = (bf16[128,256]{1,0:T(8,128)(2,1)S(1)}, bf16[128,256]{1,0:T(8,128)(2,1)S(1)}, u32[]{:S(2)}, u32[]{:S(2)}) collective-permute-start(bf16[128,256]{1,0:T(8,128)(2,1)S(1)} %get-tuple-element.47), channel_id=1, source_target_pairs={{0,16},{4,20},{8,24},{12,28},{16,0},{20,4},{24,8},{28,12},{1,17},{... | collective-permute-start | bytes 196616 | tf_op jit(solution)/shard_map/ppermute | solution.py:73
  30.9 0.0 collective-permute-done.3.received_ref
  30.9 0.3 shard_map.99
  31.2 0.1 collective-permute-start.6
  31.3 0.0 collective-permute-done.8.refs_11_
  31.3 2.3 %collective-permute-done.11.refs_2_ = bf16[128,256]{1,0:T(8,128)(2,1)S(1)} collective-permute-done((bf16[128,256]{1,0:T(8,128)(2,1)S(1)}, bf16[128,256]{1,0:T(8,128)(2,1)S(1)}, u32[]{:S(2)}, u32[]{:S(2)}) %collective-permute-start.11) | collective-permute-done | bytes 65568 | tf_op jit(solution)/shard_map/ppermute | solution.py:73
  33.6 2.6 %shard_map.103 = (f32[256,1024]{1,0:T(8,128)}, f32[256,256]{1,0:T(8,128)}) custom-call(s32[1,3]{1,0:T(1,128)} %refs_0_.3, f32[128,256]{1,0:T(8,128)S(1)} %get-tuple-element.46.refs_1_, bf16[128,256]{1,0:T(8,128)(2,1)S(1)} %collective-permute-done.11.refs_2_, f32[256,1024]{1,0:T(8,128)S(1)} %get-tuple-element.37.refs_3_, ...), custom_call_target="tpu_custom_call" | custom-call | flops 369098752 | bytes 6365196 | tf_op jit(solution)/shard_map/pallas_call | solution.py:54
  36.2 2.3 %collective-permute-done.6.refs_2_ = bf16[128,256]{1,0:T(8,128)(2,1)S(1)} collective-permute-done((bf16[128,256]{1,0:T(8,128)(2,1)S(1)}, bf16[128,256]{1,0:T(8,128)(2,1)S(1)}, u32[]{:S(2)}, u32[]{:S(2)}) %collective-permute-start.6) | collective-permute-done | bytes 65568 | tf_op jit(solution)/shard_map/ppermute | solution.py:73
  38.5 2.6 %shard_map.104 = (f32[256,1024]{1,0:T(8,128)}, f32[256,256]{1,0:T(8,128)}) custom-call(s32[1,3]{1,0:T(1,128)} %refs_0_.3, f32[128,256]{1,0:T(8,128)S(1)} %get-tuple-element.35.refs_1_, bf16[128,256]{1,0:T(8,128)(2,1)S(1)} %collective-permute-done.6.refs_2_, ...), custom_call_target="tpu_custom_call", output_to_operand_aliasing={{0}: (14, {}), {1}: (15, {})} | custom-call | flops 369098752 | bytes 7675916 | tf_op jit(solution)/shard_map/pallas_call | solution.py:54
  (3 shorter events, 0.1 us)
Async XLA Ops:
  3.9 7.7 %collective-permute-start.1 = (bf16[144,512]{1,0:T(8,128)(2,1)S(1)}, bf16[144,512]{1,0:T(8,128)(2,1)S(1)}, u32[]{:S(2)}, u32[]{:S(2)}) collective-permute-start(bf16[144,512]{1,0:T(8,128)(2,1)S(1)} %get-tuple-element.29.own_ref), channel_id=1, source_target_pairs={{0,4},{4,0},{8,12},{12,8},{16,20},{20,16},{24,28},{28,24},{1,5},{5... | collective-permute-start | bytes 442376 | tf_op jit(solution)/shard_map/ppermute | solution.py:73
  7.0 8.5 %collective-permute-start.9 = (bf16[144,512]{1,0:T(8,128)(2,1)S(1)}, bf16[144,512]{1,0:T(8,128)(2,1)S(1)}, u32[]{:S(2)}, u32[]{:S(2)}) collective-permute-start(bf16[144,512]{1,0:T(8,128)(2,1)S(1)} %get-tuple-element.43), channel_id=1, source_target_pairs={{0,4},{4,0},{8,12},{12,8},{16,20},{20,16},{24,28},{28,24},{1,5},{5... | collective-permute-start | bytes 442376 | tf_op jit(solution)/shard_map/ppermute | solution.py:73
  11.7 3.8 %collective-permute-start.2 = (bf16[144,512]{1,0:T(8,128)(2,1)S(1)}, bf16[144,512]{1,0:T(8,128)(2,1)S(1)}, u32[]{:S(2)}, u32[]{:S(2)}) collective-permute-start(bf16[144,512]{1,0:T(8,128)(2,1)S(1)} %get-tuple-element.30.factor_ref.refs_6_), channel_id=1, source_target_pairs={{0,1},{1,0},{2,3},{3,2},{4,5},{5,4},{6,7},{7,6},{8,9},{9,8},{10,11... | collective-permute-start | bytes 442376 | tf_op jit(solution)/shard_map/ppermute | solution.py:73
  11.8 8.0 %collective-permute-start = (bf16[144,512]{1,0:T(8,128)(2,1)S(1)}, bf16[144,512]{1,0:T(8,128)(2,1)S(1)}, u32[]{:S(2)}, u32[]{:S(2)}) collective-permute-start(bf16[144,512]{1,0:T(8,128)(2,1)S(1)} %get-tuple-element.28), channel_id=1, source_target_pairs={{0,4},{4,0},{8,12},{12,8},{16,20},{20,16},{24,28},{28,24},{1,5},{5... | collective-permute-start | bytes 442376 | tf_op jit(solution)/shard_map/ppermute | solution.py:73
  13.9 5.8 %collective-permute-start.4 = (bf16[144,384]{1,0:T(8,128)(2,1)S(1)}, bf16[144,384]{1,0:T(8,128)(2,1)S(1)}, u32[]{:S(2)}, u32[]{:S(2)}) collective-permute-start(bf16[144,384]{1,0:T(8,128)(2,1)S(1)} %get-tuple-element.33.own_ref), channel_id=1, source_target_pairs={{0,8},{4,12},{8,0},{12,4},{16,24},{20,28},{24,16},{28,20},{1,9},{5... | collective-permute-start | bytes 331784 | tf_op jit(solution)/shard_map/ppermute | solution.py:73
  15.8 11.6 %collective-permute-start.10 = (bf16[128,512]{1,0:T(8,128)(2,1)S(1)}, bf16[128,512]{1,0:T(8,128)(2,1)S(1)}, u32[]{:S(2)}, u32[]{:S(2)}) collective-permute-start(bf16[128,512]{1,0:T(8,128)(2,1)S(1)} %get-tuple-element.45), channel_id=1, source_target_pairs={{0,8},{4,12},{8,0},{12,4},{16,24},{20,28},{24,16},{28,20},{1,9},{5... | collective-permute-start | bytes 393224 | tf_op jit(solution)/shard_map/ppermute | solution.py:73
  19.7 7.7 %collective-permute-start.5 = (bf16[144,384]{1,0:T(8,128)(2,1)S(1)}, bf16[144,384]{1,0:T(8,128)(2,1)S(1)}, u32[]{:S(2)}, u32[]{:S(2)}) collective-permute-start(bf16[144,384]{1,0:T(8,128)(2,1)S(1)} %get-tuple-element.34.factor_ref.refs_8_), channel_id=1, source_target_pairs={{0,1},{1,0},{2,3},{3,2},{4,5},{5,4},{6,7},{7,6},{8,9},{9,8},{10,11... | collective-permute-start | bytes 331784 | tf_op jit(solution)/shard_map/ppermute | solution.py:73
  20.2 10.7 %collective-permute-start.3 = (bf16[128,512]{1,0:T(8,128)(2,1)S(1)}, bf16[128,512]{1,0:T(8,128)(2,1)S(1)}, u32[]{:S(2)}, u32[]{:S(2)}) collective-permute-start(bf16[128,512]{1,0:T(8,128)(2,1)S(1)} %get-tuple-element.32), channel_id=1, source_target_pairs={{0,8},{4,12},{8,0},{12,4},{16,24},{20,28},{24,16},{28,20},{1,9},{5... | collective-permute-start | bytes 393224 | tf_op jit(solution)/shard_map/ppermute | solution.py:73
  21.9 5.4 %collective-permute-start.7 = (bf16[144,256]{1,0:T(8,128)(2,1)S(1)}, bf16[144,256]{1,0:T(8,128)(2,1)S(1)}, u32[]{:S(2)}, u32[]{:S(2)}) collective-permute-start(bf16[144,256]{1,0:T(8,128)(2,1)S(1)} %get-tuple-element.40.own_ref), channel_id=1, source_target_pairs={{0,16},{4,20},{8,24},{12,28},{16,0},{20,4},{24,8},{28,12},{1,17},{... | collective-permute-start | bytes 221192 | tf_op jit(solution)/shard_map/ppermute | solution.py:73
  27.3 4.0 %collective-permute-start.8 = (bf16[144,256]{1,0:T(8,128)(2,1)S(1)}, bf16[144,256]{1,0:T(8,128)(2,1)S(1)}, u32[]{:S(2)}, u32[]{:S(2)}) collective-permute-start(bf16[144,256]{1,0:T(8,128)(2,1)S(1)} %shard_map.100.refs_10_), channel_id=1, source_target_pairs={{0,1},{1,0},{2,3},{3,2},{4,5},{5,4},{6,7},{7,6},{8,9},{9,8},{10,11... | collective-permute-start | bytes 221192 | tf_op jit(solution)/shard_map/ppermute | solution.py:73
  27.8 5.8 %collective-permute-start.11 = (bf16[128,256]{1,0:T(8,128)(2,1)S(1)}, bf16[128,256]{1,0:T(8,128)(2,1)S(1)}, u32[]{:S(2)}, u32[]{:S(2)}) collective-permute-start(bf16[128,256]{1,0:T(8,128)(2,1)S(1)} %get-tuple-element.47), channel_id=1, source_target_pairs={{0,16},{4,20},{8,24},{12,28},{16,0},{20,4},{24,8},{28,12},{1,17},{... | collective-permute-start | bytes 196616 | tf_op jit(solution)/shard_map/ppermute | solution.py:73
  31.2 7.3 %collective-permute-start.6 = (bf16[128,256]{1,0:T(8,128)(2,1)S(1)}, bf16[128,256]{1,0:T(8,128)(2,1)S(1)}, u32[]{:S(2)}, u32[]{:S(2)}) collective-permute-start(bf16[128,256]{1,0:T(8,128)(2,1)S(1)} %get-tuple-element.36), channel_id=1, source_target_pairs={{0,16},{4,20},{8,24},{12,28},{16,0},{20,4},{24,8},{28,12},{1,17},{... | collective-permute-start | bytes 196616 | tf_op jit(solution)/shard_map/ppermute | solution.py:73

commit v4 on v3

v4 whole, which is shorter than its diff:
```python
from functools import partial

import jax
import jax.numpy as jnp
from jax import lax
from jax.experimental import pallas as pl
from jax.experimental.pallas import tpu as pltpu
from jax.sharding import PartitionSpec as P

NOTE_ROWS = 16
f32, bf16 = jnp.float32, jnp.bfloat16


def dot(a, b):
    return jnp.dot(a, b, preferred_element_type=f32)


def dot_t(a, b):
    return lax.dot_general(a, b, (((1,), (1,)), ((), ())), preferred_element_type=f32)


def own_level(k, levels):
    level = jnp.int32(0)
    for bit in range(levels):
        low = (2 << bit) - 1
        level = jnp.where((k & low) == low, bit + 1, level)
    return level


def placed(block, panel, count):
    return jnp.concatenate(
        [jnp.where(panel == p, block, jnp.zeros_like(block)) for p in range(count)], axis=1
    )


def picked(vectors, panel, count):
    width = vectors.shape[1] // count
    result = vectors[:, :width]
    for p in range(1, count):
        result = jnp.where(panel == p, vectors[:, p * width : (p + 1) * width], result)
    return result


def call(kernel, outs, args, hbm=(), hbm_outs=False, scratch=(), flops=0):
    def bytes_of(arrays):
        return sum(a.size * a.dtype.itemsize for a in arrays)

    outs = [jax.ShapeDtypeStruct(shape, dtype) for shape, dtype in outs]
    args = [
        pltpu.with_memory_space_constraint(arg, pltpu.HBM) if i in hbm else arg
        for i, arg in enumerate(args)
    ]
    return pl.pallas_call(
        kernel,
        out_shape=outs,
        in_specs=[
            pl.BlockSpec(memory_space=pltpu.HBM if i in hbm else pltpu.VMEM)
            for i in range(len(args))
        ],
        out_specs=[pl.BlockSpec(memory_space=pltpu.HBM if hbm_outs else pltpu.VMEM) for _ in outs],
        scratch_shapes=scratch,
        compiler_params=pltpu.CompilerParams(vmem_limit_bytes=40 << 20),
        cost_estimate=pl.CostEstimate(
            flops=flops, bytes_accessed=bytes_of(args) + bytes_of(outs), transcendentals=0
        ),
    )(*args)


def exchange(block, distance, axis="leaf", upward=False):
    route = [(i, i ^ distance) for i in range(lax.axis_size(axis))]
    return lax.ppermute(block, axis, [pair for pair in route if not upward or pair[0] < pair[1]])


def upper_part():
    return lax.axis_index("rhs") & 1


def load_kernel(
    levels,
    sep_panel_hbm,
    leaf_panel_hbm,
    sep_inverse_hbm,
    sep_update_hbm,
    leaf_rhs_hbm,
    leaf_inverse_hbm,
    leaf_update_hbm,
    sep_rhs_hbm,
    carry_ref,
    leaf_rhs_ref,
    leaf_inverse_ref,
    leaf_update_ref,
    sep_rhs_ref,
    sep_panel_ref,
    leaf_panel_ref,
    sems,
):
    sep_rows = sep_rhs_hbm.shape[1]
    size, panel_rows = leaf_inverse_hbm.shape[0], leaf_update_hbm.shape[2]
    half = sep_rows // 2
    step = min(256, size)
    copies = []

    def bring(source, target):
        copies.append(pltpu.make_async_copy(source, target, sems.at[len(copies)]))
        copies[-1].start()

    bring(sep_panel_hbm, sep_panel_ref)
    bring(leaf_panel_hbm, leaf_panel_ref)
    rows = pl.ds(pl.multiple_of(upper_part() * half, half), half)
    bring(sep_inverse_hbm.at[rows], carry_ref.at[pl.ds(0, half), pl.ds(0, sep_rows)])
    for a in range(1, levels):
        columns = pl.ds(sep_rows + (a - 1) * panel_rows, panel_rows)
        bring(sep_update_hbm.at[a, rows], carry_ref.at[pl.ds(0, half), columns])
    bring(leaf_rhs_hbm, leaf_rhs_ref)
    for low in range(0, size, step):
        block = (pl.ds(low, step), pl.ds(0, low + step))
        bring(leaf_inverse_hbm.at[block], leaf_inverse_ref.at[block])
    bring(leaf_update_hbm, leaf_update_ref)
    bring(sep_rhs_hbm, sep_rhs_ref)

    copies[0].wait()
    copies[1].wait()
    row = lax.broadcasted_iota(jnp.int32, (NOTE_ROWS, sep_rows), 0)
    notes = jnp.zeros((NOTE_ROWS, sep_rows), f32)
    for a in range(levels):
        notes = jnp.where(row == a, leaf_panel_ref[0, a].astype(f32), notes)
    carry_ref[half:, :sep_rows] = notes.astype(bf16)
    for a in range(1, levels):
        columns = pl.ds(sep_rows + (a - 1) * panel_rows, panel_rows)
        carry_ref[half:, columns] = jnp.full(
            (NOTE_ROWS, panel_rows), sep_panel_ref[0, a].astype(f32)
        ).astype(bf16)
    for copy in copies[2:]:
        copy.wait()


def leaf_up_kernel(
    levels, carry_ref, rhs_ref, inverse_ref, update_ref, sep_rhs_ref, solved_ref, own_ref, out_ref
):
    k = lax.axis_index("leaf")
    scenarios, sep_rows = sep_rhs_ref.shape
    size, panel_rows = inverse_ref.shape[0], update_ref.shape[2]
    count = sep_rows // panel_rows
    step = min(256, size)
    rounded = []
    for low in range(0, size, step):
        high = low + step
        value = dot_t(rhs_ref[:, :high], inverse_ref[low:high, :high])
        solved_ref[:, low:high] = value
        rounded.append(value.astype(bf16))
    updates = jnp.concatenate([update_ref[a] for a in range(levels)], axis=1)
    together = dot(jnp.concatenate(rounded, axis=1), updates)
    terms = [together[:, a * panel_rows : (a + 1) * panel_rows] for a in range(levels)]
    level = own_level(k, levels)
    wide_level = jnp.minimum(level, levels - 1)
    rhs = jnp.where(level < levels, sep_rhs_ref[...].astype(f32), 0.0)
    wide = jnp.zeros((scenarios, sep_rows), f32)
    for a in range(levels):
        spread = placed(terms[a], leaf_panel(carry_ref, a, panel_rows), count)
        spread = jnp.where(wide_level == a, spread - rhs, spread)
        wide = jnp.where(wide_level == a, spread, wide)
        own_ref[:, a * sep_rows : (a + 1) * sep_rows] = spread
    out_ref[:, :sep_rows] = wide.astype(bf16)
    for a in range(levels - 1):
        columns = pl.ds(sep_rows + a * panel_rows, panel_rows)
        out_ref[:, columns] = jnp.where(wide_level <= a, terms[a + 1], terms[a]).astype(bf16)


def leaf_panel(first_carry_ref, level, panel_rows):
    rows = first_carry_ref.shape[0]
    notes = first_carry_ref[rows - NOTE_ROWS :, :panel_rows].astype(f32)
    return notes[level : level + 1]


def hand_on_kernel(step, sep_rows, own_ref, received_ref, factor_ref, carry_ref=None):
    lower = ((lax.axis_index("leaf") >> step) & 1) == 0
    own, received = own_ref[...], received_ref[...]
    factor_ref[...] = jnp.where(lower, own, received)
    if carry_ref is not None:
        skipped = own.shape[1] - carry_ref.shape[1]
        following = jnp.where(lower, received, own)
        carry_ref[:, :sep_rows] = following[:, :sep_rows]
        if carry_ref.shape[1] > sep_rows:
            carry_ref[:, sep_rows:] = following[:, sep_rows + skipped :]


class Factor:
    def __init__(self, own_ref, other_ref, sep_rows, panel_rows):
        self.refs = own_ref, other_ref
        self.sep_rows, self.panel_rows = sep_rows, panel_rows
        self.half = own_ref.shape[0] - NOTE_ROWS

    def columns(self, start, size):
        own, other = (ref[: self.half, start : start + size] for ref in self.refs)
        upper = upper_part() == 1
        return jnp.concatenate([jnp.where(upper, other, own), jnp.where(upper, own, other)], axis=0)

    def inverse(self):
        return self.columns(0, self.sep_rows)

    def updates(self, count):
        return self.columns(self.sep_rows, count * self.panel_rows)

    def panel(self, index):
        start = self.sep_rows + index * self.panel_rows
        notes = self.refs[0][self.half : self.half + NOTE_ROWS, start : start + self.panel_rows]
        return notes.astype(f32)[:1]


def spread_first(message_ref, arrived_ref, wide_level, levels, sep_rows, panel_rows):
    count = sep_rows // panel_rows
    wide = message_ref[:, :sep_rows].astype(f32)
    sums = []
    for level in range(levels):
        value = wide
        panel = leaf_panel(arrived_ref, level, panel_rows)
        for a, here in ((level - 1, wide_level < level), (level, wide_level > level)):
            if 0 <= a < levels - 1:
                columns = pl.ds(sep_rows + a * panel_rows, panel_rows)
                narrow = placed(message_ref[:, columns].astype(f32), panel, count)
                value = jnp.where(here, narrow, value)
        sums.append(value)
    return sums


def solve_up(pending, factor):
    count = factor.sep_rows // factor.panel_rows
    solved = dot_t((-pending[0]).astype(bf16), factor.inverse())
    others = []
    if len(pending) > 1:
        updates = dot(solved.astype(bf16), factor.updates(len(pending) - 1))
        for a, value in enumerate(pending[1:]):
            update = updates[:, a * factor.panel_rows : (a + 1) * factor.panel_rows]
            others.append(value + placed(update, factor.panel(a), count))
    return solved, others


def sums_of(own_ref, received):
    sep_rows = received[0].shape[1]
    return [
        own_ref[:, a * sep_rows : (a + 1) * sep_rows] + value for a, value in enumerate(received)
    ]


def parts_of(ref, sep_rows):
    return [ref[:, low : low + sep_rows].astype(f32) for low in range(0, ref.shape[1], sep_rows)]


def up_kernel(
    levels, now, panel_rows, own_ref, received_ref, factor_ref, other_ref, arrived_ref, *refs
):
    solved_ref, sums_ref, out_ref = refs[-3:]
    sep_rows = solved_ref.shape[1]
    if now == 0:
        partner = jnp.minimum(own_level(lax.axis_index("leaf") ^ 1, levels), levels - 1)
        received = spread_first(received_ref, arrived_ref, partner, levels, sep_rows, panel_rows)
    else:
        received = parts_of(received_ref, sep_rows)
    factor = Factor(factor_ref, other_ref, sep_rows, panel_rows)
    solved, others = solve_up(sums_of(own_ref, received), factor)
    solved_ref[...] = solved
    for a, value in enumerate(others):
        sums_ref[:, a * sep_rows : (a + 1) * sep_rows] = value
        out_ref[:, a * sep_rows : (a + 1) * sep_rows] = value.astype(bf16)


def down_kernel(levels, *refs):
    panel_hbm, own_ref, received_ref, leaf_solved_ref, update_ref, inverse_ref = refs[:6]
    factor_refs = refs[6 : 6 + 2 * levels]
    solved_refs = refs[6 + 2 * levels : 5 + 3 * levels]
    leaf_out_hbm, sep_out_hbm, work_ref, leaf_out_ref, sep_out_ref, panel_ref, sems = refs[
        5 + 3 * levels :
    ]
    copy = pltpu.make_async_copy(panel_hbm, panel_ref, sems.at[0])
    copy.start()
    k = lax.axis_index("leaf")
    rows, sep_rows = own_ref.shape
    panel_rows = update_ref.shape[2]
    count = sep_rows // panel_rows
    level = own_level(k, levels)
    factors = [
        Factor(factor_refs[2 * now], factor_refs[2 * now + 1], sep_rows, panel_rows)
        for now in range(levels)
    ]

    top = levels - 1
    pending = sums_of(own_ref, parts_of(received_ref, sep_rows))
    solved, _ = solve_up(pending, factors[top])
    ancestors = {}
    sep_out = jnp.zeros((rows, sep_rows), f32)
    for now in reversed(range(levels)):
        factor = factors[now]
        residual = solved
        if now < top:
            blocks = [
                picked(ancestors[a], factor.panel(a - now - 1), count).astype(bf16)
                for a in range(now + 1, levels)
            ]
            residual = solved_refs[now][...] - dot_t(
                jnp.concatenate(blocks, axis=1), factor.updates(top - now)
            )
        solution_now = dot(residual.astype(bf16), factor.inverse())
        ancestors[now] = solution_now.astype(bf16).astype(f32)
        sep_out = jnp.where(level == now, solution_now, sep_out)
    sep_out_ref[...] = sep_out
    leaving = [pltpu.make_async_copy(sep_out_ref, sep_out_hbm, sems.at[1])]
    leaving[0].start()

    copy.wait()
    blocks = jnp.concatenate(
        [picked(ancestors[a], panel_ref[0, a], count).astype(bf16) for a in range(levels)], axis=1
    )
    size = inverse_ref.shape[0]
    step = min(256, size)
    for low in range(0, size, step):
        high = low + step
        updates = jnp.concatenate([update_ref[a, low:high, :] for a in range(levels)], axis=1)
        value = leaf_solved_ref[:, low:high] - dot_t(blocks, updates)
        work_ref[:, low:high] = value.astype(bf16)
    for low in range(0, size, step):
        high = low + step
        leaf_out_ref[:, low:high] = dot(work_ref[:, low:], inverse_ref[low:, low:high])
        columns = pl.ds(low, step)
        leaving.append(
            pltpu.make_async_copy(
                leaf_out_ref.at[:, columns],
                leaf_out_hbm.at[:, columns],
                sems.at[len(leaving) + 1],
            )
        )
        leaving[-1].start()
    for copy in leaving:
        copy.wait()


def local(
    leaf_rhs, sep_rhs, leaf_inverse, leaf_update, leaf_panel, sep_inverse, sep_update, sep_panel
):
    levels = lax.axis_size("leaf").bit_length() - 1
    sep_rows = sep_inverse.shape[0]
    scenarios, size = leaf_rhs.shape
    leaf_update, sep_update = leaf_update[0], sep_update[0]
    panel_rows = leaf_update.shape[2]
    panel_smem = pltpu.SMEM(leaf_panel.shape, jnp.int32)
    sems = pltpu.SemaphoreType.DMA((levels + 8 + size // min(256, size),))
    leaf_flops = 2 * scenarios * size * (size + levels * panel_rows)

    def carry_shape(now):
        width = sep_rows + (levels - 1 - now) * panel_rows
        return ((sep_rows // 2 + NOTE_ROWS, width), bf16)

    loaded = (leaf_rhs, leaf_inverse, leaf_update, sep_rhs)
    carry, *loaded = call(
        partial(load_kernel, levels),
        [carry_shape(0)] + [(array.shape, bf16) for array in loaded],
        (sep_panel, leaf_panel, sep_inverse, sep_update, *loaded),
        hbm=range(8),
        scratch=[panel_smem, panel_smem, sems],
    )
    arrived = exchange(carry, 1)
    leaf_solved, sums, message = call(
        partial(leaf_up_kernel, levels),
        [
            ((scenarios, size), f32),
            ((scenarios, levels * sep_rows), f32),
            ((scenarios, sep_rows + (levels - 1) * panel_rows), bf16),
        ],
        (carry, *loaded),
        flops=leaf_flops,
    )
    received = exchange(message, 1)
    first_arrived = arrived
    factors, solved = [], []
    for now in range(levels):
        shapes = [carry_shape(now)]
        if now + 1 < levels:
            shapes.append(carry_shape(now + 1))
        handed = call(partial(hand_on_kernel, now, sep_rows), shapes, (carry, arrived))
        factors += [handed[0], exchange(handed[0], 1, "rhs")]
        if now + 1 == levels:
            break
        carry = handed[1]
        arrived = exchange(carry, 2 << now, upward=now + 2 == levels)
        z, sums, message = call(
            partial(up_kernel, levels, now, panel_rows),
            [
                ((scenarios, sep_rows), f32),
                ((scenarios, (levels - 1 - now) * sep_rows), f32),
                ((scenarios, (levels - 1 - now) * sep_rows), bf16),
            ],
            (sums, received, *factors[-2:], first_arrived, arrived)[: 6 if now + 2 < levels else 5],
            flops=2 * scenarios * sep_rows * sep_rows * 2,
        )
        solved.append(z)
        received = exchange(message, 2 << now)
    _, leaf_inverse, leaf_update, _ = loaded
    return call(
        partial(down_kernel, levels),
        [((scenarios, size), f32), ((scenarios, sep_rows), f32)],
        (leaf_panel, sums, received, leaf_solved, leaf_update, leaf_inverse, *factors, *solved),
        hbm=(0,),
        hbm_outs=True,
        scratch=[
            pltpu.VMEM((scenarios, size), bf16),
            pltpu.VMEM((scenarios, size), f32),
            pltpu.VMEM((scenarios, sep_rows), f32),
            panel_smem,
            sems,
        ],
        flops=leaf_flops,
    )


def solution(mesh):
    return jax.shard_map(
        local,
        mesh=mesh,
        in_specs=(
            P("rhs", "leaf"),
            P("rhs", "leaf"),
            P("leaf", None),
            P("leaf", None, None, None),
            P("leaf", None),
            P("leaf", None),
            P("leaf", None, None, None),
            P("leaf", None),
        ),
        out_specs=(P("rhs", "leaf"), P("rhs", "leaf")),
        check_vma=False,
    )
```

time: 41.2 us -> 36 us (0.87)
  Pallas kernels: 9.97 us -> 6.29 us
  waiting for transfers between devices: 15.3 us -> 14 us
    pallas_call x10 -> x8, Pallas kernels: 9.97 us -> 6.29 us  [call(): pl.pallas_call(kernel, out_shape=outs, in_specs=[pl.BlockSpec(memory_spac...]
    ppermute x12 -> x9, waiting for transfers between devices: 15.3 us -> 14 us  [exchange(): lax.ppermute(block, axis, [pair for pair in route if not upward or pair[0...]
    ppermute x12 -> x9, starting transfers between devices: 15 us -> 14.8 us  [exchange(): lax.ppermute(block, axis, [pair for pair in route if not upward or pair[0...]
  transfers between devices with their start and end apart: 12 -> 9, of which waited for: 5 -> 5; matrix products, arithmetic and copies ran while one was open for 0% -> 0% of each run, Pallas kernels for 10% -> 4%
where the time goes in v4:
time: 36 us; the launch traced here: 35.8 us
  starting transfers between devices  14.8 us (41%)
  waiting for transfers between devices  14 us (39%)
  Pallas kernels  6.29 us (17%)
  between operations  0.73 us (2%)
    ppermute x9, starting transfers between devices, exchange(): lax.ppermute(block, axis, [pair for pair in route if not upward or pair[0...  14.8 us
    ppermute x9, waiting for transfers between devices, exchange(): lax.ppermute(block, axis, [pair for pair in route if not upward or pair[0...  14 us
    pallas_call x8, Pallas kernels, call(): pl.pallas_call(kernel, out_shape=outs, in_specs=[pl.BlockSpec(memory_spac...  6.29 us
  transfers between devices with their start and end apart: 9, of which 5 were waited for; matrix products, arithmetic and copies ran while one was open for 0% of the time, Pallas kernels for 4%

profile of v4, /device:TPU:0, one launch (start us, length us, event | category | flops | bytes accessed | tf_op | source)
XLA Modules:
  0.0 35.8 jit_solution(9202627276687896170)
XLA Ops:
  0.6 1.9 %shard_map.95 = (bf16[144,512]{1,0:T(8,128)(2,1)S(1)}, bf16[256,1024]{1,0:T(8,128)(2,1)S(1)}, bf16[1024,1024]{1,0:T(8,128)(2,1)S(1)}, bf16[3,1024,128]{2,1,0:T(8,128)(2,1)S(1)}, bf16[256,256]{1,0:T(8,128)(2,1)S(1)}) custom-call(s32[1,3]{1,0:T(1,128)} %sep_panel_hbm.1, s32[1,3]{1,0:T(1,128)} %refs_0_.1, bf16[256,256]{1,0:T(8,128)(2,1)} %sep_inverse_hbm.1, ...), custom_call_target="tpu_custom_call" | custom-call | bytes 7553048 | tf_op jit(solution)/shard_map/pallas_call | solution.py:53
  2.6 3.0 %collective-permute-start.1 = (bf16[144,512]{1,0:T(8,128)(2,1)S(1)}, bf16[144,512]{1,0:T(8,128)(2,1)S(1)}, u32[]{:S(2)}, u32[]{:S(2)}) collective-permute-start(bf16[144,512]{1,0:T(8,128)(2,1)S(1)} %get-tuple-element.20.carry_ref.own_ref), channel_id=1, source_target_pairs={{0,4},{4,0},{8,12},{12,8},{16,20},{20,16},{24,28},{28,24},{1,5},{5... | collective-permute-start | bytes 442376 | tf_op jit(solution)/shard_map/ppermute | solution.py:71
  5.6 0.8 %shard_map.96 = (f32[256,1024]{1,0:T(8,128)S(1)}, f32[256,768]{1,0:T(8,128)S(1)}, bf16[256,512]{1,0:T(8,128)(2,1)S(1)}) custom-call(bf16[144,512]{1,0:T(8,128)(2,1)S(1)} %get-tuple-element.20.carry_ref.own_ref, bf16[256,1024]{1,0:T(8,128)(2,1)S(1)} %get-tuple-element.21.rhs_ref, bf16[1024,1024]{1,0:T(8,128)(2,1)S(1)} %get-tuple-element.22.inverse_ref.refs_5_, ...), custom_call_target="tpu_custom_call" | custom-call | flops 738197504 | bytes 5783552 | tf_op jit(solution)/shard_map/pallas_call | solution.py:53
  6.4 0.1 collective-permute-start
  6.5 3.6 %collective-permute-done.1.received_ref.arrived_ref = bf16[144,512]{1,0:T(8,128)(2,1)S(1)} collective-permute-done((bf16[144,512]{1,0:T(8,128)(2,1)S(1)}, bf16[144,512]{1,0:T(8,128)(2,1)S(1)}, u32[]{:S(2)}, u32[]{:S(2)}) %collective-permute-start.1) | collective-permute-done | bytes 147488 | tf_op jit(solution)/shard_map/ppermute | solution.py:71
  10.2 0.1 collective-permute-start.2
  10.3 2.1 %collective-permute-start.3 = (bf16[144,384]{1,0:T(8,128)(2,1)S(1)}, bf16[144,384]{1,0:T(8,128)(2,1)S(1)}, u32[]{:S(2)}, u32[]{:S(2)}) collective-permute-start(bf16[144,384]{1,0:T(8,128)(2,1)S(1)} %get-tuple-element.28.own_ref), channel_id=1, source_target_pairs={{0,8},{4,12},{8,0},{12,4},{16,24},{20,28},{24,16},{28,20},{1,9},{5... | collective-permute-start | bytes 331784 | tf_op jit(solution)/shard_map/ppermute | solution.py:71
  12.4 3.7 %collective-permute-done.3.refs_0_.received_ref = bf16[144,384]{1,0:T(8,128)(2,1)S(1)} collective-permute-done((bf16[144,384]{1,0:T(8,128)(2,1)S(1)}, bf16[144,384]{1,0:T(8,128)(2,1)S(1)}, u32[]{:S(2)}, u32[]{:S(2)}) %collective-permute-start.3) | collective-permute-done | bytes 110624 | tf_op jit(solution)/shard_map/ppermute | solution.py:71
  16.1 0.0 collective-permute-done.received_ref
  16.1 0.0 collective-permute-done.2.other_ref.refs_7_
  16.1 0.4 %shard_map.98 = (f32[256,256]{1,0:T(8,128)S(1)}, f32[256,512]{1,0:T(8,128)S(1)}, bf16[256,512]{1,0:T(8,128)(2,1)S(1)}) custom-call(f32[256,768]{1,0:T(8,128)S(1)} %get-tuple-element.25.own_ref, bf16[256,512]{1,0:T(8,128)(2,1)S(1)} %collective-permute-done.received_ref, bf16[144,512]{1,0:T(8,128)(2,1)S(1)} %get-tuple-element.27.factor_ref.refs_6_, ...), custom_call_target="tpu_custom_call" | custom-call | flops 67108864 | bytes 2650112 | tf_op jit(solution)/shard_map/pallas_call | solution.py:53
  16.5 1.8 %collective-permute-start.4 = (bf16[256,512]{1,0:T(8,128)(2,1)S(1)}, bf16[256,512]{1,0:T(8,128)(2,1)S(1)}, u32[]{:S(2)}, u32[]{:S(2)}) collective-permute-start(bf16[256,512]{1,0:T(8,128)(2,1)S(1)} %get-tuple-element.30), channel_id=1, source_target_pairs={{0,8},{4,12},{8,0},{12,4},{16,24},{20,28},{24,16},{28,20},{1,9},{5... | collective-permute-start | bytes 786440 | tf_op jit(solution)/shard_map/ppermute | solution.py:71
  18.3 0.1 collective-permute-start.5
  18.4 4.5 %collective-permute-start.7 = (bf16[144,256]{1,0:T(8,128)(2,1)S(1)}, bf16[144,256]{1,0:T(8,128)(2,1)S(1)}, u32[]{:S(2)}, u32[]{:S(2)}) collective-permute-start(bf16[144,256]{1,0:T(8,128)(2,1)S(1)} %get-tuple-element.35.own_ref), channel_id=1, source_target_pairs={{0,16},{4,20},{8,24},{12,28},{1,17},{5,21},{9,25},{13,29},{2,18},{... | collective-permute-start | bytes 221192 | tf_op jit(solution)/shard_map/ppermute | solution.py:71
  22.9 0.0 collective-permute-done.5.other_ref.refs_9_
  22.9 1.7 %collective-permute-done.4.received_ref = bf16[256,512]{1,0:T(8,128)(2,1)S(1)} collective-permute-done((bf16[256,512]{1,0:T(8,128)(2,1)S(1)}, bf16[256,512]{1,0:T(8,128)(2,1)S(1)}, u32[]{:S(2)}, u32[]{:S(2)}) %collective-permute-start.4) | collective-permute-done | bytes 262176 | tf_op jit(solution)/shard_map/ppermute | solution.py:71
  24.6 0.4 %shard_map.100 = (f32[256,256]{1,0:T(8,128)S(1)}, f32[256,256]{1,0:T(8,128)S(1)}, bf16[256,256]{1,0:T(8,128)(2,1)S(1)}) custom-call(f32[256,512]{1,0:T(8,128)S(1)} %get-tuple-element.29.own_ref, bf16[256,512]{1,0:T(8,128)(2,1)S(1)} %collective-permute-done.4.received_ref, bf16[144,384]{1,0:T(8,128)(2,1)S(1)} %get-tuple-element.31.factor_ref.refs_8_, ...), custom_call_target="tpu_custom_call" | custom-call | flops 67108864 | bytes 1810432 | tf_op jit(solution)/shard_map/pallas_call | solution.py:53
  25.0 3.0 %collective-permute-start.6 = (bf16[256,256]{1,0:T(8,128)(2,1)S(1)}, bf16[256,256]{1,0:T(8,128)(2,1)S(1)}, u32[]{:S(2)}, u32[]{:S(2)}) collective-permute-start(bf16[256,256]{1,0:T(8,128)(2,1)S(1)} %get-tuple-element.33), channel_id=1, source_target_pairs={{0,16},{4,20},{8,24},{12,28},{16,0},{20,4},{24,8},{28,12},{1,17},{... | collective-permute-start | bytes 393224 | tf_op jit(solution)/shard_map/ppermute | solution.py:71
  28.0 0.0 collective-permute-done.7.received_ref
  28.0 0.1 collective-permute-start.8
  28.1 1.3 %collective-permute-done.8.refs_11_ = bf16[144,256]{1,0:T(8,128)(2,1)S(1)} collective-permute-done((bf16[144,256]{1,0:T(8,128)(2,1)S(1)}, bf16[144,256]{1,0:T(8,128)(2,1)S(1)}, u32[]{:S(2)}, u32[]{:S(2)}) %collective-permute-start.8) | collective-permute-done | bytes 73760 | tf_op jit(solution)/shard_map/ppermute | solution.py:71
  29.3 3.8 %collective-permute-done.6.refs_2_ = bf16[256,256]{1,0:T(8,128)(2,1)S(1)} collective-permute-done((bf16[256,256]{1,0:T(8,128)(2,1)S(1)}, bf16[256,256]{1,0:T(8,128)(2,1)S(1)}, u32[]{:S(2)}, u32[]{:S(2)}) %collective-permute-start.6) | collective-permute-done | bytes 131104 | tf_op jit(solution)/shard_map/ppermute | solution.py:71
  33.1 2.7 %shard_map.102 = (f32[256,1024]{1,0:T(8,128)}, f32[256,256]{1,0:T(8,128)}) custom-call(s32[1,3]{1,0:T(1,128)} %refs_0_.1, f32[256,256]{1,0:T(8,128)S(1)} %get-tuple-element.32.refs_1_, bf16[256,256]{1,0:T(8,128)(2,1)S(1)} %collective-permute-done.6.refs_2_, f32[256,1024]{1,0:T(8,128)S(1)} %get-tuple-element.34.refs_3_, ...), custom_call_target="tpu_custom_call" | custom-call | flops 738197504 | bytes 6823948 | tf_op jit(solution)/shard_map/pallas_call | solution.py:53
  (3 shorter events, 0.1 us)
Async XLA Ops:
  2.6 7.6 %collective-permute-start.1 = (bf16[144,512]{1,0:T(8,128)(2,1)S(1)}, bf16[144,512]{1,0:T(8,128)(2,1)S(1)}, u32[]{:S(2)}, u32[]{:S(2)}) collective-permute-start(bf16[144,512]{1,0:T(8,128)(2,1)S(1)} %get-tuple-element.20.carry_ref.own_ref), channel_id=1, source_target_pairs={{0,4},{4,0},{8,12},{12,8},{16,20},{20,16},{24,28},{28,24},{1,5},{5... | collective-permute-start | bytes 442376 | tf_op jit(solution)/shard_map/ppermute | solution.py:71
  6.4 9.6 %collective-permute-start = (bf16[256,512]{1,0:T(8,128)(2,1)S(1)}, bf16[256,512]{1,0:T(8,128)(2,1)S(1)}, u32[]{:S(2)}, u32[]{:S(2)}) collective-permute-start(bf16[256,512]{1,0:T(8,128)(2,1)S(1)} %get-tuple-element.26), channel_id=1, source_target_pairs={{0,4},{4,0},{8,12},{12,8},{16,20},{20,16},{24,28},{28,24},{1,5},{5... | collective-permute-start | bytes 786440 | tf_op jit(solution)/shard_map/ppermute | solution.py:71
  10.2 5.9 %collective-permute-start.2 = (bf16[144,512]{1,0:T(8,128)(2,1)S(1)}, bf16[144,512]{1,0:T(8,128)(2,1)S(1)}, u32[]{:S(2)}, u32[]{:S(2)}) collective-permute-start(bf16[144,512]{1,0:T(8,128)(2,1)S(1)} %get-tuple-element.27.factor_ref.refs_6_), channel_id=1, source_target_pairs={{0,1},{1,0},{2,3},{3,2},{4,5},{5,4},{6,7},{7,6},{8,9},{9,8},{10,11... | collective-permute-start | bytes 442376 | tf_op jit(solution)/shard_map/ppermute | solution.py:71
  10.3 5.8 %collective-permute-start.3 = (bf16[144,384]{1,0:T(8,128)(2,1)S(1)}, bf16[144,384]{1,0:T(8,128)(2,1)S(1)}, u32[]{:S(2)}, u32[]{:S(2)}) collective-permute-start(bf16[144,384]{1,0:T(8,128)(2,1)S(1)} %get-tuple-element.28.own_ref), channel_id=1, source_target_pairs={{0,8},{4,12},{8,0},{12,4},{16,24},{20,28},{24,16},{28,20},{1,9},{5... | collective-permute-start | bytes 331784 | tf_op jit(solution)/shard_map/ppermute | solution.py:71
  16.5 8.1 %collective-permute-start.4 = (bf16[256,512]{1,0:T(8,128)(2,1)S(1)}, bf16[256,512]{1,0:T(8,128)(2,1)S(1)}, u32[]{:S(2)}, u32[]{:S(2)}) collective-permute-start(bf16[256,512]{1,0:T(8,128)(2,1)S(1)} %get-tuple-element.30), channel_id=1, source_target_pairs={{0,8},{4,12},{8,0},{12,4},{16,24},{20,28},{24,16},{28,20},{1,9},{5... | collective-permute-start | bytes 786440 | tf_op jit(solution)/shard_map/ppermute | solution.py:71
  18.3 4.6 %collective-permute-start.5 = (bf16[144,384]{1,0:T(8,128)(2,1)S(1)}, bf16[144,384]{1,0:T(8,128)(2,1)S(1)}, u32[]{:S(2)}, u32[]{:S(2)}) collective-permute-start(bf16[144,384]{1,0:T(8,128)(2,1)S(1)} %get-tuple-element.31.factor_ref.refs_8_), channel_id=1, source_target_pairs={{0,1},{1,0},{2,3},{3,2},{4,5},{5,4},{6,7},{7,6},{8,9},{9,8},{10,11... | collective-permute-start | bytes 331784 | tf_op jit(solution)/shard_map/ppermute | solution.py:71
  18.4 9.6 %collective-permute-start.7 = (bf16[144,256]{1,0:T(8,128)(2,1)S(1)}, bf16[144,256]{1,0:T(8,128)(2,1)S(1)}, u32[]{:S(2)}, u32[]{:S(2)}) collective-permute-start(bf16[144,256]{1,0:T(8,128)(2,1)S(1)} %get-tuple-element.35.own_ref), channel_id=1, source_target_pairs={{0,16},{4,20},{8,24},{12,28},{1,17},{5,21},{9,25},{13,29},{2,18},{... | collective-permute-start | bytes 221192 | tf_op jit(solution)/shard_map/ppermute | solution.py:71
  25.0 8.2 %collective-permute-start.6 = (bf16[256,256]{1,0:T(8,128)(2,1)S(1)}, bf16[256,256]{1,0:T(8,128)(2,1)S(1)}, u32[]{:S(2)}, u32[]{:S(2)}) collective-permute-start(bf16[256,256]{1,0:T(8,128)(2,1)S(1)} %get-tuple-element.33), channel_id=1, source_target_pairs={{0,16},{4,20},{8,24},{12,28},{16,0},{20,4},{24,8},{28,12},{1,17},{... | collective-permute-start | bytes 393224 | tf_op jit(solution)/shard_map/ppermute | solution.py:71
  28.0 1.3 %collective-permute-start.8 = (bf16[144,256]{1,0:T(8,128)(2,1)S(1)}, bf16[144,256]{1,0:T(8,128)(2,1)S(1)}, u32[]{:S(2)}, u32[]{:S(2)}) collective-permute-start(bf16[144,256]{1,0:T(8,128)(2,1)S(1)} %shard_map.101.refs_10_), channel_id=1, source_target_pairs={{0,1},{1,0},{2,3},{3,2},{4,5},{5,4},{6,7},{7,6},{8,9},{9,8},{10,11... | collective-permute-start | bytes 221192 | tf_op jit(solution)/shard_map/ppermute | solution.py:71

commit v5 on v4

--- a/solution.py
+++ b/solution.py
@@ -75,29 +75,19 @@
     return lax.axis_index("rhs") & 1
 
 
-def load_kernel(
+def pack_kernel(
     levels,
     sep_panel_hbm,
     leaf_panel_hbm,
     sep_inverse_hbm,
     sep_update_hbm,
-    leaf_rhs_hbm,
-    leaf_inverse_hbm,
-    leaf_update_hbm,
-    sep_rhs_hbm,
     carry_ref,
-    leaf_rhs_ref,
-    leaf_inverse_ref,
-    leaf_update_ref,
-    sep_rhs_ref,
     sep_panel_ref,
     leaf_panel_ref,
     sems,
 ):
-    sep_rows = sep_rhs_hbm.shape[1]
-    size, panel_rows = leaf_inverse_hbm.shape[0], leaf_update_hbm.shape[2]
+    sep_rows, panel_rows = sep_inverse_hbm.shape[1], sep_update_hbm.shape[2]
     half = sep_rows // 2
-    step = min(256, size)
     copies = []
 
     def bring(source, target):
@@ -111,12 +101,6 @@
     for a in range(1, levels):
         columns = pl.ds(sep_rows + (a - 1) * panel_rows, panel_rows)
         bring(sep_update_hbm.at[a, rows], carry_ref.at[pl.ds(0, half), columns])
-    bring(leaf_rhs_hbm, leaf_rhs_ref)
-    for low in range(0, size, step):
-        block = (pl.ds(low, step), pl.ds(0, low + step))
-        bring(leaf_inverse_hbm.at[block], leaf_inverse_ref.at[block])
-    bring(leaf_update_hbm, leaf_update_ref)
-    bring(sep_rhs_hbm, sep_rhs_ref)
 
     copies[0].wait()
     copies[1].wait()
@@ -135,26 +119,60 @@
 
 
 def leaf_up_kernel(
-    levels, carry_ref, rhs_ref, inverse_ref, update_ref, sep_rhs_ref, solved_ref, own_ref, out_ref
+    levels,
+    carry_ref,
+    rhs_hbm,
+    inverse_hbm,
+    update_hbm,
+    sep_rhs_hbm,
+    inverse_ref,
+    update_ref,
+    solved_ref,
+    own_ref,
+    out_ref,
+    rhs_ref,
+    sep_rhs_ref,
+    sems,
 ):
     k = lax.axis_index("leaf")
-    scenarios, sep_rows = sep_rhs_ref.shape
+    sep_rows = sep_rhs_ref.shape[1]
     size, panel_rows = inverse_ref.shape[0], update_ref.shape[2]
     count = sep_rows // panel_rows
     step = min(256, size)
-    rounded = []
-    for low in range(0, size, step):
+    lows = range(0, size, step)
+    copies = []
+
+    def bring(source, target):
+        copies.append(pltpu.make_async_copy(source, target, sems.at[len(copies)]))
+        copies[-1].start()
+
+    bring(rhs_hbm, rhs_ref)
+    for low in lows:
+        block = (pl.ds(low, step), pl.ds(0, low + step))
+        bring(inverse_hbm.at[block], inverse_ref.at[block])
+    bring(update_hbm, update_ref)
+    bring(sep_rhs_hbm, sep_rhs_ref)
+
+    def solve(low):
         high = low + step
         value = dot_t(rhs_ref[:, :high], inverse_ref[low:high, :high])
         solved_ref[:, low:high] = value
-        rounded.append(value.astype(bf16))
+        return value.astype(bf16)
+
+    early = len(copies) - 3
+    for copy in copies[:early]:
+        copy.wait()
+    rounded = [solve(low) for low in lows[:-1]]
+    for copy in copies[early:]:
+        copy.wait()
+    rounded.append(solve(lows[-1]))
     updates = jnp.concatenate([update_ref[a] for a in range(levels)], axis=1)
     together = dot(jnp.concatenate(rounded, axis=1), updates)
     terms = [together[:, a * panel_rows : (a + 1) * panel_rows] for a in range(levels)]
     level = own_level(k, levels)
     wide_level = jnp.minimum(level, levels - 1)
     rhs = jnp.where(level < levels, sep_rhs_ref[...].astype(f32), 0.0)
-    wide = jnp.zeros((scenarios, sep_rows), f32)
+    wide = jnp.zeros(rhs.shape, f32)
     for a in range(levels):
         spread = placed(terms[a], leaf_panel(carry_ref, a, panel_rows), count)
         spread = jnp.where(wide_level == a, spread - rhs, spread)
@@ -172,16 +190,18 @@
     return notes[level : level + 1]
 
 
-def hand_on_kernel(step, sep_rows, own_ref, received_ref, factor_ref, carry_ref=None):
+def hand_on_kernel(step, sep_rows, own_ref, received_ref, carry_ref):
     lower = ((lax.axis_index("leaf") >> step) & 1) == 0
-    own, received = own_ref[...], received_ref[...]
-    factor_ref[...] = jnp.where(lower, own, received)
-    if carry_ref is not None:
-        skipped = own.shape[1] - carry_ref.shape[1]
-        following = jnp.where(lower, received, own)
-        carry_ref[:, :sep_rows] = following[:, :sep_rows]
-        if carry_ref.shape[1] > sep_rows:
-            carry_ref[:, sep_rows:] = following[:, sep_rows + skipped :]
+    following = jnp.where(lower, received_ref[...], own_ref[...])
+    skipped = own_ref.shape[1] - carry_ref.shape[1]
+    carry_ref[:, :sep_rows] = following[:, :sep_rows]
+    if carry_ref.shape[1] > sep_rows:
+        carry_ref[:, sep_rows:] = following[:, sep_rows + skipped :]
+
+
+def keep_kernel(step, own_ref, received_ref, *refs):
+    lower = ((lax.axis_index("leaf") >> step) & 1) == 0
+    refs[-1][...] = jnp.where(lower, own_ref[...], received_ref[...])
 
 
 class Factor:
@@ -246,14 +266,12 @@
     return [ref[:, low : low + sep_rows].astype(f32) for low in range(0, ref.shape[1], sep_rows)]
 
 
-def up_kernel(
-    levels, now, panel_rows, own_ref, received_ref, factor_ref, other_ref, arrived_ref, *refs
-):
+def up_kernel(levels, now, panel_rows, own_ref, received_ref, factor_ref, other_ref, *refs):
     solved_ref, sums_ref, out_ref = refs[-3:]
     sep_rows = solved_ref.shape[1]
     if now == 0:
         partner = jnp.minimum(own_level(lax.axis_index("leaf") ^ 1, levels), levels - 1)
-        received = spread_first(received_ref, arrived_ref, partner, levels, sep_rows, panel_rows)
+        received = spread_first(received_ref, refs[0], partner, levels, sep_rows, panel_rows)
     else:
         received = parts_of(received_ref, sep_rows)
     factor = Factor(factor_ref, other_ref, sep_rows, panel_rows)
@@ -342,45 +360,51 @@
     leaf_update, sep_update = leaf_update[0], sep_update[0]
     panel_rows = leaf_update.shape[2]
     panel_smem = pltpu.SMEM(leaf_panel.shape, jnp.int32)
-    sems = pltpu.SemaphoreType.DMA((levels + 8 + size // min(256, size),))
+    sems = pltpu.SemaphoreType.DMA((levels + 8 + 3 * (size // min(256, size)),))
     leaf_flops = 2 * scenarios * size * (size + levels * panel_rows)
 
     def carry_shape(now):
         width = sep_rows + (levels - 1 - now) * panel_rows
         return ((sep_rows // 2 + NOTE_ROWS, width), bf16)
 
-    loaded = (leaf_rhs, leaf_inverse, leaf_update, sep_rhs)
-    carry, *loaded = call(
-        partial(load_kernel, levels),
-        [carry_shape(0)] + [(array.shape, bf16) for array in loaded],
-        (sep_panel, leaf_panel, sep_inverse, sep_update, *loaded),
-        hbm=range(8),
+    (carry,) = call(
+        partial(pack_kernel, levels),
+        [carry_shape(0)],
+        (sep_panel, leaf_panel, sep_inverse, sep_update),
+        hbm=range(4),
         scratch=[panel_smem, panel_smem, sems],
     )
     arrived = exchange(carry, 1)
-    leaf_solved, sums, message = call(
+    leaf_inverse, leaf_update, leaf_solved, sums, message = call(
         partial(leaf_up_kernel, levels),
         [
+            (leaf_inverse.shape, bf16),
+            (leaf_update.shape, bf16),
             ((scenarios, size), f32),
             ((scenarios, levels * sep_rows), f32),
             ((scenarios, sep_rows + (levels - 1) * panel_rows), bf16),
         ],
-        (carry, *loaded),
+        (carry, leaf_rhs, leaf_inverse, leaf_update, sep_rhs),
+        hbm=range(1, 5),
+        scratch=[pltpu.VMEM(leaf_rhs.shape, bf16), pltpu.VMEM(sep_rhs.shape, bf16), sems],
         flops=leaf_flops,
     )
     received = exchange(message, 1)
-    first_arrived = arrived
+    first = (arrived,)
     factors, solved = [], []
     for now in range(levels):
-        shapes = [carry_shape(now)]
+        pair = (carry, arrived)
         if now + 1 < levels:
-            shapes.append(carry_shape(now + 1))
-        handed = call(partial(hand_on_kernel, now, sep_rows), shapes, (carry, arrived))
-        factors += [handed[0], exchange(handed[0], 1, "rhs")]
+            (carry,) = call(
+                partial(hand_on_kernel, now, sep_rows), [carry_shape(now + 1)], pair
+            )
+            arrived = exchange(carry, 2 << now, upward=now + 2 == levels)
+            pair += (carry,)
+        factors += call(partial(keep_kernel, now), [carry_shape(now)], pair)
+        factors.append(exchange(factors[-1], 1, "rhs"))
         if now + 1 == levels:
             break
-        carry = handed[1]
-        arrived = exchange(carry, 2 << now, upward=now + 2 == levels)
+        extra = (first if now == 0 else ()) + ((arrived,) if now + 2 < levels else ())
         z, sums, message = call(
             partial(up_kernel, levels, now, panel_rows),
             [
@@ -388,12 +412,11 @@
                 ((scenarios, (levels - 1 - now) * sep_rows), f32),
                 ((scenarios, (levels - 1 - now) * sep_rows), bf16),
             ],
-            (sums, received, *factors[-2:], first_arrived, arrived)[: 6 if now + 2 < levels else 5],
+            (sums, received, *factors[-2:], *extra),
             flops=2 * scenarios * sep_rows * sep_rows * 2,
         )
         solved.append(z)
         received = exchange(message, 2 << now)
-    _, leaf_inverse, leaf_update, _ = loaded
     return call(
         partial(down_kernel, levels),
         [((scenarios, size), f32), ((scenarios, sep_rows), f32)],

time: 36 us -> 34.5 us (0.958)
  waiting for transfers between devices: 14 us -> 11.9 us
  Pallas kernels: 6.29 us -> 7.34 us
  starting transfers between devices: 14.8 us -> 14.3 us
    ppermute x9, waiting for transfers between devices: 14 us -> 11.9 us  [exchange(): lax.ppermute(block, axis, [pair for pair in route if not upward or pair[0...]
    pallas_call x8 -> x10, Pallas kernels: 6.29 us -> 7.34 us  [call(): pl.pallas_call(kernel, out_shape=outs, in_specs=[pl.BlockSpec(memory_spac...]
    ppermute x9, starting transfers between devices: 14.8 us -> 14.3 us  [exchange(): lax.ppermute(block, axis, [pair for pair in route if not upward or pair[0...]
  transfers between devices with their start and end apart: 9 -> 9, of which waited for: 5 -> 6; matrix products, arithmetic and copies ran while one was open for 0% -> 0% of each run, Pallas kernels for 4% -> 9%
where the time goes in v5:
time: 34.5 us; the launch traced here: 34.3 us
  starting transfers between devices  14.3 us (41%)
  waiting for transfers between devices  11.9 us (34%)
  Pallas kernels  7.34 us (21%)
  between operations  0.74 us (2%)
    ppermute x9, starting transfers between devices, exchange(): lax.ppermute(block, axis, [pair for pair in route if not upward or pair[0...  14.3 us
    ppermute x9, waiting for transfers between devices, exchange(): lax.ppermute(block, axis, [pair for pair in route if not upward or pair[0...  11.9 us
    pallas_call x10, Pallas kernels, call(): pl.pallas_call(kernel, out_shape=outs, in_specs=[pl.BlockSpec(memory_spac...  7.34 us
  transfers between devices with their start and end apart: 9, of which 6 were waited for; matrix products, arithmetic and copies ran while one was open for 0% of the time, Pallas kernels for 9%

profile of v5, /device:TPU:0, one launch (start us, length us, event | category | flops | bytes accessed | tf_op | source)
XLA Modules:
  0.0 34.3 jit_solution(3628597117145759416)
XLA Ops:
  0.6 1.1 %shard_map.95.carry_ref.own_ref = bf16[144,512]{1,0:T(8,128)(2,1)S(1)} custom-call(s32[1,3]{1,0:T(1,128)} %sep_panel_hbm.1, s32[1,3]{1,0:T(1,128)} %refs_0_.1, bf16[256,256]{1,0:T(8,128)(2,1)} %sep_inverse_hbm.1, bf16[3,256,128]{2,1,0:T(8,128)(2,1)} %bitcast.3), custom_call_target="tpu_custom_call" | custom-call | bytes 475160 | tf_op jit(solution)/shard_map/pallas_call | solution.py:53
  1.7 3.0 %collective-permute-start.1 = (bf16[144,512]{1,0:T(8,128)(2,1)S(1)}, bf16[144,512]{1,0:T(8,128)(2,1)S(1)}, u32[]{:S(2)}, u32[]{:S(2)}) collective-permute-start(bf16[144,512]{1,0:T(8,128)(2,1)S(1)} %shard_map.95.carry_ref.own_ref), channel_id=1, source_target_pairs={{0,4},{4,0},{8,12},{12,8},{16,20},{20,16},{24,28},{28,24},{1,5},{5... | collective-permute-start | bytes 442376 | tf_op jit(solution)/shard_map/ppermute | solution.py:71
  4.7 2.6 %shard_map.96 = (bf16[1024,1024]{1,0:T(8,128)(2,1)S(1)}, bf16[3,1024,128]{2,1,0:T(8,128)(2,1)S(1)}, f32[256,1024]{1,0:T(8,128)S(1)}, f32[256,768]{1,0:T(8,128)S(1)}, bf16[256,512]{1,0:T(8,128)(2,1)S(1)}) custom-call(bf16[144,512]{1,0:T(8,128)(2,1)S(1)} %shard_map.95.carry_ref.own_ref, bf16[256,1024]{1,0:T(8,128)(2,1)} %rhs_hbm.1, ...), custom_call_target="tpu_custom_call" | custom-call | flops 738197504 | bytes 8667136 | tf_op jit(solution)/shard_map/pallas_call | solution.py:53
  7.4 0.1 collective-permute-start
  7.5 1.1 %collective-permute-done.1.received_ref.refs_0_ = bf16[144,512]{1,0:T(8,128)(2,1)S(1)} collective-permute-done((bf16[144,512]{1,0:T(8,128)(2,1)S(1)}, bf16[144,512]{1,0:T(8,128)(2,1)S(1)}, u32[]{:S(2)}, u32[]{:S(2)}) %collective-permute-start.1) | collective-permute-done | bytes 147488 | tf_op jit(solution)/shard_map/ppermute | solution.py:71
  8.6 0.1 collective-permute-start.2
  8.7 1.9 %collective-permute-start.3 = (bf16[144,384]{1,0:T(8,128)(2,1)S(1)}, bf16[144,384]{1,0:T(8,128)(2,1)S(1)}, u32[]{:S(2)}, u32[]{:S(2)}) collective-permute-start(bf16[144,384]{1,0:T(8,128)(2,1)S(1)} %shard_map.97.refs_0_.own_ref), channel_id=1, source_target_pairs={{0,8},{4,12},{8,0},{12,4},{16,24},{20,28},{24,16},{28,20},{1,9},{5... | collective-permute-start | bytes 331784 | tf_op jit(solution)/shard_map/ppermute | solution.py:71
  10.6 3.7 %collective-permute-done.3.refs_1_.received_ref = bf16[144,384]{1,0:T(8,128)(2,1)S(1)} collective-permute-done((bf16[144,384]{1,0:T(8,128)(2,1)S(1)}, bf16[144,384]{1,0:T(8,128)(2,1)S(1)}, u32[]{:S(2)}, u32[]{:S(2)}) %collective-permute-start.3) | collective-permute-done | bytes 110624 | tf_op jit(solution)/shard_map/ppermute | solution.py:71
  14.2 1.0 %collective-permute-done.received_ref = bf16[256,512]{1,0:T(8,128)(2,1)S(1)} collective-permute-done((bf16[256,512]{1,0:T(8,128)(2,1)S(1)}, bf16[256,512]{1,0:T(8,128)(2,1)S(1)}, u32[]{:S(2)}, u32[]{:S(2)}) %collective-permute-start) | collective-permute-done | bytes 262176 | tf_op jit(solution)/shard_map/ppermute | solution.py:71
  15.2 0.0 collective-permute-done.2.other_ref.refs_7_
  15.2 0.4 %shard_map.99 = (f32[256,256]{1,0:T(8,128)S(1)}, f32[256,512]{1,0:T(8,128)S(1)}, bf16[256,512]{1,0:T(8,128)(2,1)S(1)}) custom-call(f32[256,768]{1,0:T(8,128)S(1)} %get-tuple-element.13.own_ref, bf16[256,512]{1,0:T(8,128)(2,1)S(1)} %collective-permute-done.received_ref, bf16[144,512]{1,0:T(8,128)(2,1)S(1)} %shard_map.98.factor_ref.refs_6_, ...), custom_call_target="tpu_custom_call" | custom-call | flops 67108864 | bytes 2650112 | tf_op jit(solution)/shard_map/pallas_call | solution.py:53
  15.6 1.6 %collective-permute-start.4 = (bf16[256,512]{1,0:T(8,128)(2,1)S(1)}, bf16[256,512]{1,0:T(8,128)(2,1)S(1)}, u32[]{:S(2)}, u32[]{:S(2)}) collective-permute-start(bf16[256,512]{1,0:T(8,128)(2,1)S(1)} %get-tuple-element.16), channel_id=1, source_target_pairs={{0,8},{4,12},{8,0},{12,4},{16,24},{20,28},{24,16},{28,20},{1,9},{5... | collective-permute-start | bytes 786440 | tf_op jit(solution)/shard_map/ppermute | solution.py:71
  17.3 0.1 collective-permute-start.5
  17.4 4.5 %collective-permute-start.7 = (bf16[144,256]{1,0:T(8,128)(2,1)S(1)}, bf16[144,256]{1,0:T(8,128)(2,1)S(1)}, u32[]{:S(2)}, u32[]{:S(2)}) collective-permute-start(bf16[144,256]{1,0:T(8,128)(2,1)S(1)} %shard_map.100.refs_0_.own_ref), channel_id=1, source_target_pairs={{0,16},{4,20},{8,24},{12,28},{1,17},{5,21},{9,25},{13,29},{2,18},{... | collective-permute-start | bytes 221192 | tf_op jit(solution)/shard_map/ppermute | solution.py:71
  21.9 0.0 collective-permute-done.5.other_ref.refs_9_
  21.9 0.7 %collective-permute-done.4.received_ref = bf16[256,512]{1,0:T(8,128)(2,1)S(1)} collective-permute-done((bf16[256,512]{1,0:T(8,128)(2,1)S(1)}, bf16[256,512]{1,0:T(8,128)(2,1)S(1)}, u32[]{:S(2)}, u32[]{:S(2)}) %collective-permute-start.4) | collective-permute-done | bytes 262176 | tf_op jit(solution)/shard_map/ppermute | solution.py:71
  22.6 0.4 %shard_map.102 = (f32[256,256]{1,0:T(8,128)S(1)}, f32[256,256]{1,0:T(8,128)S(1)}, bf16[256,256]{1,0:T(8,128)(2,1)S(1)}) custom-call(f32[256,512]{1,0:T(8,128)S(1)} %get-tuple-element.15.own_ref, bf16[256,512]{1,0:T(8,128)(2,1)S(1)} %collective-permute-done.4.received_ref, bf16[144,384]{1,0:T(8,128)(2,1)S(1)} %shard_map.101.factor_ref.refs_8_, ...), custom_call_target="tpu_custom_call" | custom-call | flops 67108864 | bytes 1662976 | tf_op jit(solution)/shard_map/pallas_call | solution.py:53
  23.0 3.0 %collective-permute-start.6 = (bf16[256,256]{1,0:T(8,128)(2,1)S(1)}, bf16[256,256]{1,0:T(8,128)(2,1)S(1)}, u32[]{:S(2)}, u32[]{:S(2)}) collective-permute-start(bf16[256,256]{1,0:T(8,128)(2,1)S(1)} %get-tuple-element.18), channel_id=1, source_target_pairs={{0,16},{4,20},{8,24},{12,28},{16,0},{20,4},{24,8},{28,12},{1,17},{... | collective-permute-start | bytes 393224 | tf_op jit(solution)/shard_map/ppermute | solution.py:71
  26.0 0.0 collective-permute-done.7.received_ref
  26.0 0.1 collective-permute-start.8
  26.1 1.3 %collective-permute-done.8.refs_11_ = bf16[144,256]{1,0:T(8,128)(2,1)S(1)} collective-permute-done((bf16[144,256]{1,0:T(8,128)(2,1)S(1)}, bf16[144,256]{1,0:T(8,128)(2,1)S(1)}, u32[]{:S(2)}, u32[]{:S(2)}) %collective-permute-start.8) | collective-permute-done | bytes 73760 | tf_op jit(solution)/shard_map/ppermute | solution.py:71
  27.3 4.2 %collective-permute-done.6.refs_2_ = bf16[256,256]{1,0:T(8,128)(2,1)S(1)} collective-permute-done((bf16[256,256]{1,0:T(8,128)(2,1)S(1)}, bf16[256,256]{1,0:T(8,128)(2,1)S(1)}, u32[]{:S(2)}, u32[]{:S(2)}) %collective-permute-start.6) | collective-permute-done | bytes 131104 | tf_op jit(solution)/shard_map/ppermute | solution.py:71
  31.5 2.8 %shard_map.104 = (f32[256,1024]{1,0:T(8,128)}, f32[256,256]{1,0:T(8,128)}) custom-call(s32[1,3]{1,0:T(1,128)} %refs_0_.1, f32[256,256]{1,0:T(8,128)S(1)} %get-tuple-element.17.refs_1_, bf16[256,256]{1,0:T(8,128)(2,1)S(1)} %collective-permute-done.6.refs_2_, f32[256,1024]{1,0:T(8,128)S(1)} %get-tuple-element.19.refs_3_, ...), custom_call_target="tpu_custom_call" | custom-call | flops 738197504 | bytes 6823948 | tf_op jit(solution)/shard_map/pallas_call | solution.py:53
  (5 shorter events, 0.1 us)
Async XLA Ops:
  1.7 6.9 %collective-permute-start.1 = (bf16[144,512]{1,0:T(8,128)(2,1)S(1)}, bf16[144,512]{1,0:T(8,128)(2,1)S(1)}, u32[]{:S(2)}, u32[]{:S(2)}) collective-permute-start(bf16[144,512]{1,0:T(8,128)(2,1)S(1)} %shard_map.95.carry_ref.own_ref), channel_id=1, source_target_pairs={{0,4},{4,0},{8,12},{12,8},{16,20},{20,16},{24,28},{28,24},{1,5},{5... | collective-permute-start | bytes 442376 | tf_op jit(solution)/shard_map/ppermute | solution.py:71
  7.4 7.8 %collective-permute-start = (bf16[256,512]{1,0:T(8,128)(2,1)S(1)}, bf16[256,512]{1,0:T(8,128)(2,1)S(1)}, u32[]{:S(2)}, u32[]{:S(2)}) collective-permute-start(bf16[256,512]{1,0:T(8,128)(2,1)S(1)} %get-tuple-element.14), channel_id=1, source_target_pairs={{0,4},{4,0},{8,12},{12,8},{16,20},{20,16},{24,28},{28,24},{1,5},{5... | collective-permute-start | bytes 786440 | tf_op jit(solution)/shard_map/ppermute | solution.py:71
  8.6 6.6 %collective-permute-start.2 = (bf16[144,512]{1,0:T(8,128)(2,1)S(1)}, bf16[144,512]{1,0:T(8,128)(2,1)S(1)}, u32[]{:S(2)}, u32[]{:S(2)}) collective-permute-start(bf16[144,512]{1,0:T(8,128)(2,1)S(1)} %shard_map.98.factor_ref.refs_6_), channel_id=1, source_target_pairs={{0,1},{1,0},{2,3},{3,2},{4,5},{5,4},{6,7},{7,6},{8,9},{9,8},{10,11... | collective-permute-start | bytes 442376 | tf_op jit(solution)/shard_map/ppermute | solution.py:71
  8.7 5.5 %collective-permute-start.3 = (bf16[144,384]{1,0:T(8,128)(2,1)S(1)}, bf16[144,384]{1,0:T(8,128)(2,1)S(1)}, u32[]{:S(2)}, u32[]{:S(2)}) collective-permute-start(bf16[144,384]{1,0:T(8,128)(2,1)S(1)} %shard_map.97.refs_0_.own_ref), channel_id=1, source_target_pairs={{0,8},{4,12},{8,0},{12,4},{16,24},{20,28},{24,16},{28,20},{1,9},{5... | collective-permute-start | bytes 331784 | tf_op jit(solution)/shard_map/ppermute | solution.py:71
  15.6 7.0 %collective-permute-start.4 = (bf16[256,512]{1,0:T(8,128)(2,1)S(1)}, bf16[256,512]{1,0:T(8,128)(2,1)S(1)}, u32[]{:S(2)}, u32[]{:S(2)}) collective-permute-start(bf16[256,512]{1,0:T(8,128)(2,1)S(1)} %get-tuple-element.16), channel_id=1, source_target_pairs={{0,8},{4,12},{8,0},{12,4},{16,24},{20,28},{24,16},{28,20},{1,9},{5... | collective-permute-start | bytes 786440 | tf_op jit(solution)/shard_map/ppermute | solution.py:71
  17.3 4.6 %collective-permute-start.5 = (bf16[144,384]{1,0:T(8,128)(2,1)S(1)}, bf16[144,384]{1,0:T(8,128)(2,1)S(1)}, u32[]{:S(2)}, u32[]{:S(2)}) collective-permute-start(bf16[144,384]{1,0:T(8,128)(2,1)S(1)} %shard_map.101.factor_ref.refs_8_), channel_id=1, source_target_pairs={{0,1},{1,0},{2,3},{3,2},{4,5},{5,4},{6,7},{7,6},{8,9},{9,8},{10,11... | collective-permute-start | bytes 331784 | tf_op jit(solution)/shard_map/ppermute | solution.py:71
  17.4 8.6 %collective-permute-start.7 = (bf16[144,256]{1,0:T(8,128)(2,1)S(1)}, bf16[144,256]{1,0:T(8,128)(2,1)S(1)}, u32[]{:S(2)}, u32[]{:S(2)}) collective-permute-start(bf16[144,256]{1,0:T(8,128)(2,1)S(1)} %shard_map.100.refs_0_.own_ref), channel_id=1, source_target_pairs={{0,16},{4,20},{8,24},{12,28},{1,17},{5,21},{9,25},{13,29},{2,18},{... | collective-permute-start | bytes 221192 | tf_op jit(solution)/shard_map/ppermute | solution.py:71
  23.0 8.6 %collective-permute-start.6 = (bf16[256,256]{1,0:T(8,128)(2,1)S(1)}, bf16[256,256]{1,0:T(8,128)(2,1)S(1)}, u32[]{:S(2)}, u32[]{:S(2)}) collective-permute-start(bf16[256,256]{1,0:T(8,128)(2,1)S(1)} %get-tuple-element.18), channel_id=1, source_target_pairs={{0,16},{4,20},{8,24},{12,28},{16,0},{20,4},{24,8},{28,12},{1,17},{... | collective-permute-start | bytes 393224 | tf_op jit(solution)/shard_map/ppermute | solution.py:71
  26.0 1.3 %collective-permute-start.8 = (bf16[144,256]{1,0:T(8,128)(2,1)S(1)}, bf16[144,256]{1,0:T(8,128)(2,1)S(1)}, u32[]{:S(2)}, u32[]{:S(2)}) collective-permute-start(bf16[144,256]{1,0:T(8,128)(2,1)S(1)} %shard_map.103.refs_10_), channel_id=1, source_target_pairs={{0,1},{1,0},{2,3},{3,2},{4,5},{5,4},{6,7},{7,6},{8,9},{9,8},{10,11... | collective-permute-start | bytes 221192 | tf_op jit(solution)/shard_map/ppermute | solution.py:71

commit v6 on v5

--- a/solution.py
+++ b/solution.py
@@ -282,18 +282,35 @@
         out_ref[:, a * sep_rows : (a + 1) * sep_rows] = value.astype(bf16)
 
 
+def prepare_kernel(levels, solved_ref, update_ref, inverse_ref, base_ref, folded_ref):
+    size, panel_rows = inverse_ref.shape[0], update_ref.shape[2]
+    step = min(256, size)
+    for low in range(0, size, step):
+        high = low + step
+        solved = solved_ref[:, low:]
+        coarse = solved.astype(bf16)
+        fine = (solved - coarse.astype(f32)).astype(bf16)
+        block = inverse_ref[low:, low:high]
+        base_ref[:, low:high] = dot(coarse, block) + dot(fine, block)
+        for a in range(levels):
+            folded_ref[a * panel_rows : (a + 1) * panel_rows, low:high] = lax.dot_general(
+                update_ref[a, low:, :],
+                block,
+                (((0,), (0,)), ((), ())),
+                preferred_element_type=f32,
+            ).astype(bf16)
+
+
 def down_kernel(levels, *refs):
-    panel_hbm, own_ref, received_ref, leaf_solved_ref, update_ref, inverse_ref = refs[:6]
-    factor_refs = refs[6 : 6 + 2 * levels]
-    solved_refs = refs[6 + 2 * levels : 5 + 3 * levels]
-    leaf_out_hbm, sep_out_hbm, work_ref, leaf_out_ref, sep_out_ref, panel_ref, sems = refs[
-        5 + 3 * levels :
-    ]
+    panel_hbm, own_ref, received_ref, base_ref, folded_ref = refs[:5]
+    factor_refs = refs[5 : 5 + 2 * levels]
+    solved_refs = refs[5 + 2 * levels : 4 + 3 * levels]
+    leaf_out_hbm, sep_out_hbm, leaf_out_ref, sep_out_ref, panel_ref, sems = refs[4 + 3 * levels :]
     copy = pltpu.make_async_copy(panel_hbm, panel_ref, sems.at[0])
     copy.start()
     k = lax.axis_index("leaf")
     rows, sep_rows = own_ref.shape
-    panel_rows = update_ref.shape[2]
+    panel_rows = folded_ref.shape[0] // levels
     count = sep_rows // panel_rows
     level = own_level(k, levels)
     factors = [
@@ -328,16 +345,11 @@
     blocks = jnp.concatenate(
         [picked(ancestors[a], panel_ref[0, a], count).astype(bf16) for a in range(levels)], axis=1
     )
-    size = inverse_ref.shape[0]
+    size = folded_ref.shape[1]
     step = min(256, size)
     for low in range(0, size, step):
         high = low + step
-        updates = jnp.concatenate([update_ref[a, low:high, :] for a in range(levels)], axis=1)
-        value = leaf_solved_ref[:, low:high] - dot_t(blocks, updates)
-        work_ref[:, low:high] = value.astype(bf16)
-    for low in range(0, size, step):
-        high = low + step
-        leaf_out_ref[:, low:high] = dot(work_ref[:, low:], inverse_ref[low:, low:high])
+        leaf_out_ref[:, low:high] = base_ref[:, low:high] - dot(blocks, folded_ref[:, low:high])
         columns = pl.ds(low, step)
         leaving.append(
             pltpu.make_async_copy(
@@ -390,6 +402,12 @@
         flops=leaf_flops,
     )
     received = exchange(message, 1)
+    base, folded = call(
+        partial(prepare_kernel, levels),
+        [((scenarios, size), f32), ((levels * panel_rows, size), bf16)],
+        (leaf_solved, leaf_update, leaf_inverse),
+        flops=2 * leaf_flops,
+    )
     first = (arrived,)
     factors, solved = [], []
     for now in range(levels):
@@ -404,7 +422,8 @@
         factors.append(exchange(factors[-1], 1, "rhs"))
         if now + 1 == levels:
             break
-        extra = (first if now == 0 else ()) + ((arrived,) if now + 2 < levels else ())
+        extra = (*first, folded) if now == 0 else ()
+        extra += (arrived,) if now + 2 < levels else ()
         z, sums, message = call(
             partial(up_kernel, levels, now, panel_rows),
             [
@@ -420,11 +439,10 @@
     return call(
         partial(down_kernel, levels),
         [((scenarios, size), f32), ((scenarios, sep_rows), f32)],
-        (leaf_panel, sums, received, leaf_solved, leaf_update, leaf_inverse, *factors, *solved),
+        (leaf_panel, sums, received, base, folded, *factors, *solved),
         hbm=(0,),
         hbm_outs=True,
         scratch=[
-            pltpu.VMEM((scenarios, size), bf16),
             pltpu.VMEM((scenarios, size), f32),
             pltpu.VMEM((scenarios, sep_rows), f32),
             panel_smem,

time: 34.5 us -> 34.1 us (0.988)
  waiting for transfers between devices: 11.9 us -> 10.5 us
  Pallas kernels: 7.34 us -> 8.3 us
    ppermute x9, waiting for transfers between devices: 11.9 us -> 10.5 us  [exchange(): lax.ppermute(block, axis, [pair for pair in route if not upward or pair[0...]
    pallas_call x10 -> x11, Pallas kernels: 7.34 us -> 8.3 us  [call(): pl.pallas_call(kernel, out_shape=outs, in_specs=[pl.BlockSpec(memory_spac...]
  transfers between devices with their start and end apart: 9 -> 9, of which waited for: 6 -> 6; matrix products, arithmetic and copies ran while one was open for 0% -> 0% of each run, Pallas kernels for 9% -> 13%
where the time goes in v6:
time: 34.1 us; the launch traced here: 33.9 us
  starting transfers between devices  14.3 us (42%)
  waiting for transfers between devices  10.5 us (31%)
  Pallas kernels  8.3 us (24%)
  between operations  0.75 us (2%)
    ppermute x9, starting transfers between devices, exchange(): lax.ppermute(block, axis, [pair for pair in route if not upward or pair[0...  14.3 us
    ppermute x9, waiting for transfers between devices, exchange(): lax.ppermute(block, axis, [pair for pair in route if not upward or pair[0...  10.5 us
    pallas_call x11, Pallas kernels, call(): pl.pallas_call(kernel, out_shape=outs, in_specs=[pl.BlockSpec(memory_spac...  8.3 us
  transfers between devices with their start and end apart: 9, of which 6 were waited for; matrix products, arithmetic and copies ran while one was open for 0% of the time, Pallas kernels for 13%

profile of v6, /device:TPU:0, one launch (start us, length us, event | category | flops | bytes accessed | tf_op | source)
XLA Modules:
  0.0 33.9 jit_solution(17065521446701442934)
XLA Ops:
  0.6 1.1 %shard_map.95.carry_ref.own_ref = bf16[144,512]{1,0:T(8,128)(2,1)S(1)} custom-call(s32[1,3]{1,0:T(1,128)} %sep_panel_hbm.1, s32[1,3]{1,0:T(1,128)} %refs_0_.1, bf16[256,256]{1,0:T(8,128)(2,1)} %sep_inverse_hbm.1, bf16[3,256,128]{2,1,0:T(8,128)(2,1)} %bitcast.3), custom_call_target="tpu_custom_call" | custom-call | bytes 475160 | tf_op jit(solution)/shard_map/pallas_call | solution.py:53
  1.7 3.0 %collective-permute-start.1 = (bf16[144,512]{1,0:T(8,128)(2,1)S(1)}, bf16[144,512]{1,0:T(8,128)(2,1)S(1)}, u32[]{:S(2)}, u32[]{:S(2)}) collective-permute-start(bf16[144,512]{1,0:T(8,128)(2,1)S(1)} %shard_map.95.carry_ref.own_ref), channel_id=1, source_target_pairs={{0,4},{4,0},{8,12},{12,8},{16,20},{20,16},{24,28},{28,24},{1,5},{5... | collective-permute-start | bytes 442376 | tf_op jit(solution)/shard_map/ppermute | solution.py:71
  4.7 2.6 %shard_map.96 = (bf16[1024,1024]{1,0:T(8,128)(2,1)S(1)}, bf16[3,1024,128]{2,1,0:T(8,128)(2,1)S(1)}, f32[256,1024]{1,0:T(8,128)S(1)}, f32[256,768]{1,0:T(8,128)S(1)}, bf16[256,512]{1,0:T(8,128)(2,1)S(1)}) custom-call(bf16[144,512]{1,0:T(8,128)(2,1)S(1)} %shard_map.95.carry_ref.own_ref, bf16[256,1024]{1,0:T(8,128)(2,1)} %rhs_hbm.1, ...), custom_call_target="tpu_custom_call" | custom-call | flops 738197504 | bytes 8667136 | tf_op jit(solution)/shard_map/pallas_call | solution.py:53
  7.4 0.1 collective-permute-start
  7.5 1.1 %collective-permute-done.1.received_ref.refs_0_ = bf16[144,512]{1,0:T(8,128)(2,1)S(1)} collective-permute-done((bf16[144,512]{1,0:T(8,128)(2,1)S(1)}, bf16[144,512]{1,0:T(8,128)(2,1)S(1)}, u32[]{:S(2)}, u32[]{:S(2)}) %collective-permute-start.1) | collective-permute-done | bytes 147488 | tf_op jit(solution)/shard_map/ppermute | solution.py:71
  8.6 0.1 collective-permute-start.2
  8.7 1.9 %collective-permute-start.3 = (bf16[144,384]{1,0:T(8,128)(2,1)S(1)}, bf16[144,384]{1,0:T(8,128)(2,1)S(1)}, u32[]{:S(2)}, u32[]{:S(2)}) collective-permute-start(bf16[144,384]{1,0:T(8,128)(2,1)S(1)} %shard_map.97.refs_0_.own_ref), channel_id=1, source_target_pairs={{0,8},{4,12},{8,0},{12,4},{16,24},{20,28},{24,16},{28,20},{1,9},{5... | collective-permute-start | bytes 331784 | tf_op jit(solution)/shard_map/ppermute | solution.py:71
  10.6 1.4 %shard_map.99 = (f32[256,1024]{1,0:T(8,128)S(1)}, bf16[384,1024]{1,0:T(8,128)(2,1)S(1)}) custom-call(f32[256,1024]{1,0:T(8,128)S(1)} %get-tuple-element.17.solved_ref, bf16[3,1024,128]{2,1,0:T(8,128)(2,1)S(1)} %get-tuple-element.18.update_ref, bf16[1024,1024]{1,0:T(8,128)(2,1)S(1)} %get-tuple-element.19.inverse_ref), custom_call_target="tpu_custom_call" | custom-call | flops 1476395008 | bytes 5767168 | tf_op jit(solution)/shard_map/pallas_call | solution.py:53
  12.0 2.2 %collective-permute-done.3.refs_2_.received_ref = bf16[144,384]{1,0:T(8,128)(2,1)S(1)} collective-permute-done((bf16[144,384]{1,0:T(8,128)(2,1)S(1)}, bf16[144,384]{1,0:T(8,128)(2,1)S(1)}, u32[]{:S(2)}, u32[]{:S(2)}) %collective-permute-start.3) | collective-permute-done | bytes 110624 | tf_op jit(solution)/shard_map/ppermute | solution.py:71
  14.2 1.0 %collective-permute-done.received_ref = bf16[256,512]{1,0:T(8,128)(2,1)S(1)} collective-permute-done((bf16[256,512]{1,0:T(8,128)(2,1)S(1)}, bf16[256,512]{1,0:T(8,128)(2,1)S(1)}, u32[]{:S(2)}, u32[]{:S(2)}) %collective-permute-start) | collective-permute-done | bytes 262176 | tf_op jit(solution)/shard_map/ppermute | solution.py:71
  15.2 0.0 collective-permute-done.2.other_ref.refs_6_
  15.2 0.4 %shard_map.100 = (f32[256,256]{1,0:T(8,128)S(1)}, f32[256,512]{1,0:T(8,128)S(1)}, bf16[256,512]{1,0:T(8,128)(2,1)S(1)}) custom-call(f32[256,768]{1,0:T(8,128)S(1)} %get-tuple-element.15.own_ref, bf16[256,512]{1,0:T(8,128)(2,1)S(1)} %collective-permute-done.received_ref, bf16[144,512]{1,0:T(8,128)(2,1)S(1)} %shard_map.98.factor_ref.refs_5_, ...), custom_call_target="tpu_custom_call" | custom-call | flops 67108864 | bytes 3436544 | tf_op jit(solution)/shard_map/pallas_call | solution.py:53
  15.6 1.6 %collective-permute-start.4 = (bf16[256,512]{1,0:T(8,128)(2,1)S(1)}, bf16[256,512]{1,0:T(8,128)(2,1)S(1)}, u32[]{:S(2)}, u32[]{:S(2)}) collective-permute-start(bf16[256,512]{1,0:T(8,128)(2,1)S(1)} %get-tuple-element.22), channel_id=1, source_target_pairs={{0,8},{4,12},{8,0},{12,4},{16,24},{20,28},{24,16},{28,20},{1,9},{5... | collective-permute-start | bytes 786440 | tf_op jit(solution)/shard_map/ppermute | solution.py:71
  17.3 0.1 collective-permute-start.5
  17.4 4.5 %collective-permute-start.7 = (bf16[144,256]{1,0:T(8,128)(2,1)S(1)}, bf16[144,256]{1,0:T(8,128)(2,1)S(1)}, u32[]{:S(2)}, u32[]{:S(2)}) collective-permute-start(bf16[144,256]{1,0:T(8,128)(2,1)S(1)} %shard_map.101.refs_0_.own_ref), channel_id=1, source_target_pairs={{0,16},{4,20},{8,24},{12,28},{1,17},{5,21},{9,25},{13,29},{2,18},{... | collective-permute-start | bytes 221192 | tf_op jit(solution)/shard_map/ppermute | solution.py:71
  21.9 0.0 collective-permute-done.5.other_ref.refs_8_
  21.9 0.7 %collective-permute-done.4.received_ref = bf16[256,512]{1,0:T(8,128)(2,1)S(1)} collective-permute-done((bf16[256,512]{1,0:T(8,128)(2,1)S(1)}, bf16[256,512]{1,0:T(8,128)(2,1)S(1)}, u32[]{:S(2)}, u32[]{:S(2)}) %collective-permute-start.4) | collective-permute-done | bytes 262176 | tf_op jit(solution)/shard_map/ppermute | solution.py:71
  22.6 0.4 %shard_map.103 = (f32[256,256]{1,0:T(8,128)S(1)}, f32[256,256]{1,0:T(8,128)S(1)}, bf16[256,256]{1,0:T(8,128)(2,1)S(1)}) custom-call(f32[256,512]{1,0:T(8,128)S(1)} %get-tuple-element.21.own_ref, bf16[256,512]{1,0:T(8,128)(2,1)S(1)} %collective-permute-done.4.received_ref, bf16[144,384]{1,0:T(8,128)(2,1)S(1)} %shard_map.102.factor_ref.refs_7_, ...), custom_call_target="tpu_custom_call" | custom-call | flops 67108864 | bytes 1662976 | tf_op jit(solution)/shard_map/pallas_call | solution.py:53
  23.0 3.0 %collective-permute-start.6 = (bf16[256,256]{1,0:T(8,128)(2,1)S(1)}, bf16[256,256]{1,0:T(8,128)(2,1)S(1)}, u32[]{:S(2)}, u32[]{:S(2)}) collective-permute-start(bf16[256,256]{1,0:T(8,128)(2,1)S(1)} %get-tuple-element.24), channel_id=1, source_target_pairs={{0,16},{4,20},{8,24},{12,28},{16,0},{20,4},{24,8},{28,12},{1,17},{... | collective-permute-start | bytes 393224 | tf_op jit(solution)/shard_map/ppermute | solution.py:71
  26.0 0.0 collective-permute-done.7.received_ref
  26.0 0.1 collective-permute-start.8
  26.1 1.3 %collective-permute-done.8.refs_10_ = bf16[144,256]{1,0:T(8,128)(2,1)S(1)} collective-permute-done((bf16[144,256]{1,0:T(8,128)(2,1)S(1)}, bf16[144,256]{1,0:T(8,128)(2,1)S(1)}, u32[]{:S(2)}, u32[]{:S(2)}) %collective-permute-start.8) | collective-permute-done | bytes 73760 | tf_op jit(solution)/shard_map/ppermute | solution.py:71
  27.3 4.2 %collective-permute-done.6.refs_2_ = bf16[256,256]{1,0:T(8,128)(2,1)S(1)} collective-permute-done((bf16[256,256]{1,0:T(8,128)(2,1)S(1)}, bf16[256,256]{1,0:T(8,128)(2,1)S(1)}, u32[]{:S(2)}, u32[]{:S(2)}) %collective-permute-start.6) | collective-permute-done | bytes 131104 | tf_op jit(solution)/shard_map/ppermute | solution.py:71
  31.6 2.3 %shard_map.105 = (f32[256,1024]{1,0:T(8,128)}, f32[256,256]{1,0:T(8,128)}) custom-call(s32[1,3]{1,0:T(1,128)} %refs_0_.1, f32[256,256]{1,0:T(8,128)S(1)} %get-tuple-element.23.refs_1_, bf16[256,256]{1,0:T(8,128)(2,1)S(1)} %collective-permute-done.6.refs_2_, f32[256,1024]{1,0:T(8,128)S(1)} %get-tuple-element.25.refs_3_, ...), custom_call_target="tpu_custom_call" | custom-call | flops 738197504 | bytes 4726796 | tf_op jit(solution)/shard_map/pallas_call | solution.py:53
  (5 shorter events, 0.1 us)
Async XLA Ops:
  1.7 6.9 %collective-permute-start.1 = (bf16[144,512]{1,0:T(8,128)(2,1)S(1)}, bf16[144,512]{1,0:T(8,128)(2,1)S(1)}, u32[]{:S(2)}, u32[]{:S(2)}) collective-permute-start(bf16[144,512]{1,0:T(8,128)(2,1)S(1)} %shard_map.95.carry_ref.own_ref), channel_id=1, source_target_pairs={{0,4},{4,0},{8,12},{12,8},{16,20},{20,16},{24,28},{28,24},{1,5},{5... | collective-permute-start | bytes 442376 | tf_op jit(solution)/shard_map/ppermute | solution.py:71
  7.4 7.8 %collective-permute-start = (bf16[256,512]{1,0:T(8,128)(2,1)S(1)}, bf16[256,512]{1,0:T(8,128)(2,1)S(1)}, u32[]{:S(2)}, u32[]{:S(2)}) collective-permute-start(bf16[256,512]{1,0:T(8,128)(2,1)S(1)} %get-tuple-element.16), channel_id=1, source_target_pairs={{0,4},{4,0},{8,12},{12,8},{16,20},{20,16},{24,28},{28,24},{1,5},{5... | collective-permute-start | bytes 786440 | tf_op jit(solution)/shard_map/ppermute | solution.py:71
  8.6 6.6 %collective-permute-start.2 = (bf16[144,512]{1,0:T(8,128)(2,1)S(1)}, bf16[144,512]{1,0:T(8,128)(2,1)S(1)}, u32[]{:S(2)}, u32[]{:S(2)}) collective-permute-start(bf16[144,512]{1,0:T(8,128)(2,1)S(1)} %shard_map.98.factor_ref.refs_5_), channel_id=1, source_target_pairs={{0,1},{1,0},{2,3},{3,2},{4,5},{5,4},{6,7},{7,6},{8,9},{9,8},{10,11... | collective-permute-start | bytes 442376 | tf_op jit(solution)/shard_map/ppermute | solution.py:71
  8.7 5.5 %collective-permute-start.3 = (bf16[144,384]{1,0:T(8,128)(2,1)S(1)}, bf16[144,384]{1,0:T(8,128)(2,1)S(1)}, u32[]{:S(2)}, u32[]{:S(2)}) collective-permute-start(bf16[144,384]{1,0:T(8,128)(2,1)S(1)} %shard_map.97.refs_0_.own_ref), channel_id=1, source_target_pairs={{0,8},{4,12},{8,0},{12,4},{16,24},{20,28},{24,16},{28,20},{1,9},{5... | collective-permute-start | bytes 331784 | tf_op jit(solution)/shard_map/ppermute | solution.py:71
  15.6 7.0 %collective-permute-start.4 = (bf16[256,512]{1,0:T(8,128)(2,1)S(1)}, bf16[256,512]{1,0:T(8,128)(2,1)S(1)}, u32[]{:S(2)}, u32[]{:S(2)}) collective-permute-start(bf16[256,512]{1,0:T(8,128)(2,1)S(1)} %get-tuple-element.22), channel_id=1, source_target_pairs={{0,8},{4,12},{8,0},{12,4},{16,24},{20,28},{24,16},{28,20},{1,9},{5... | collective-permute-start | bytes 786440 | tf_op jit(solution)/shard_map/ppermute | solution.py:71
  17.3 4.6 %collective-permute-start.5 = (bf16[144,384]{1,0:T(8,128)(2,1)S(1)}, bf16[144,384]{1,0:T(8,128)(2,1)S(1)}, u32[]{:S(2)}, u32[]{:S(2)}) collective-permute-start(bf16[144,384]{1,0:T(8,128)(2,1)S(1)} %shard_map.102.factor_ref.refs_7_), channel_id=1, source_target_pairs={{0,1},{1,0},{2,3},{3,2},{4,5},{5,4},{6,7},{7,6},{8,9},{9,8},{10,11... | collective-permute-start | bytes 331784 | tf_op jit(solution)/shard_map/ppermute | solution.py:71
  17.4 8.6 %collective-permute-start.7 = (bf16[144,256]{1,0:T(8,128)(2,1)S(1)}, bf16[144,256]{1,0:T(8,128)(2,1)S(1)}, u32[]{:S(2)}, u32[]{:S(2)}) collective-permute-start(bf16[144,256]{1,0:T(8,128)(2,1)S(1)} %shard_map.101.refs_0_.own_ref), channel_id=1, source_target_pairs={{0,16},{4,20},{8,24},{12,28},{1,17},{5,21},{9,25},{13,29},{2,18},{... | collective-permute-start | bytes 221192 | tf_op jit(solution)/shard_map/ppermute | solution.py:71
  23.0 8.6 %collective-permute-start.6 = (bf16[256,256]{1,0:T(8,128)(2,1)S(1)}, bf16[256,256]{1,0:T(8,128)(2,1)S(1)}, u32[]{:S(2)}, u32[]{:S(2)}) collective-permute-start(bf16[256,256]{1,0:T(8,128)(2,1)S(1)} %get-tuple-element.24), channel_id=1, source_target_pairs={{0,16},{4,20},{8,24},{12,28},{16,0},{20,4},{24,8},{28,12},{1,17},{... | collective-permute-start | bytes 393224 | tf_op jit(solution)/shard_map/ppermute | solution.py:71
  26.0 1.3 %collective-permute-start.8 = (bf16[144,256]{1,0:T(8,128)(2,1)S(1)}, bf16[144,256]{1,0:T(8,128)(2,1)S(1)}, u32[]{:S(2)}, u32[]{:S(2)}) collective-permute-start(bf16[144,256]{1,0:T(8,128)(2,1)S(1)} %shard_map.104.refs_9_), channel_id=1, source_target_pairs={{0,1},{1,0},{2,3},{3,2},{4,5},{5,4},{6,7},{7,6},{8,9},{9,8},{10,11... | collective-permute-start | bytes 221192 | tf_op jit(solution)/shard_map/ppermute | solution.py:71

commit v7 on v6

--- a/solution.py
+++ b/solution.py
@@ -287,64 +287,76 @@
     step = min(256, size)
     for low in range(0, size, step):
         high = low + step
-        solved = solved_ref[:, low:]
-        coarse = solved.astype(bf16)
-        fine = (solved - coarse.astype(f32)).astype(bf16)
+        coarse, fine = two_parts(solved_ref[:, low:])
         block = inverse_ref[low:, low:high]
         base_ref[:, low:high] = dot(coarse, block) + dot(fine, block)
         for a in range(levels):
-            folded_ref[a * panel_rows : (a + 1) * panel_rows, low:high] = lax.dot_general(
-                update_ref[a, low:, :],
-                block,
-                (((0,), (0,)), ((), ())),
-                preferred_element_type=f32,
+            folded_ref[a * panel_rows : (a + 1) * panel_rows, low:high] = contract_rows(
+                update_ref[a, low:, :], block
             ).astype(bf16)
 
 
+def two_parts(value):
+    coarse = value.astype(bf16)
+    return coarse, (value - coarse.astype(f32)).astype(bf16)
+
+
+def contract_rows(a, b):
+    return lax.dot_general(a, b, (((0,), (0,)), ((), ())), preferred_element_type=f32)
+
+
+def fold_kernel(levels, panel_rows, *refs):
+    below = levels - 1
+    for now in range(below):
+        own_ref, other_ref, solved_ref = refs[3 * now : 3 * now + 3]
+        base_ref, folded_ref = refs[3 * below + 2 * now : 3 * below + 2 * now + 2]
+        factor = Factor(own_ref, other_ref, base_ref.shape[1], panel_rows)
+        inverse = factor.inverse()
+        coarse, fine = two_parts(solved_ref[...])
+        base_ref[...] = dot(coarse, inverse) + dot(fine, inverse)
+        folded_ref[...] = contract_rows(factor.updates(below - now), inverse).astype(bf16)
+
+
+def square_kernel(panel_rows, own_ref, other_ref, coarse_ref, fine_ref):
+    inverse = Factor(own_ref, other_ref, coarse_ref.shape[1], panel_rows).inverse()
+    coarse_ref[...], fine_ref[...] = two_parts(contract_rows(inverse, inverse))
+
+
 def down_kernel(levels, *refs):
-    panel_hbm, own_ref, received_ref, base_ref, folded_ref = refs[:5]
-    factor_refs = refs[5 : 5 + 2 * levels]
-    solved_refs = refs[5 + 2 * levels : 4 + 3 * levels]
-    leaf_out_hbm, sep_out_hbm, leaf_out_ref, sep_out_ref, panel_ref, sems = refs[4 + 3 * levels :]
-    copy = pltpu.make_async_copy(panel_hbm, panel_ref, sems.at[0])
-    copy.start()
-    k = lax.axis_index("leaf")
-    rows, sep_rows = own_ref.shape
+    carry_ref, own_ref, received_ref, base_ref, folded_ref, coarse_ref, fine_ref = refs[:7]
+    below = levels - 1
+    factor_refs = refs[7 : 7 + below]
+    folds = refs[7 + below : 7 + 3 * below]
+    leaf_out_hbm, sep_out_hbm, leaf_out_ref, sep_out_ref, sems = refs[7 + 3 * below :]
+    level = own_level(lax.axis_index("leaf"), levels)
+    sep_rows = own_ref.shape[1]
     panel_rows = folded_ref.shape[0] // levels
     count = sep_rows // panel_rows
-    level = own_level(k, levels)
-    factors = [
-        Factor(factor_refs[2 * now], factor_refs[2 * now + 1], sep_rows, panel_rows)
-        for now in range(levels)
-    ]
-
-    top = levels - 1
-    pending = sums_of(own_ref, parts_of(received_ref, sep_rows))
-    solved, _ = solve_up(pending, factors[top])
-    ancestors = {}
-    sep_out = jnp.zeros((rows, sep_rows), f32)
-    for now in reversed(range(levels)):
-        factor = factors[now]
-        residual = solved
-        if now < top:
-            blocks = [
-                picked(ancestors[a], factor.panel(a - now - 1), count).astype(bf16)
-                for a in range(now + 1, levels)
-            ]
-            residual = solved_refs[now][...] - dot_t(
-                jnp.concatenate(blocks, axis=1), factor.updates(top - now)
-            )
-        solution_now = dot(residual.astype(bf16), factor.inverse())
+
+    residual = (-(own_ref[...] + received_ref[...].astype(f32))).astype(bf16)
+    solution_now = dot(residual, coarse_ref[...]) + dot(residual, fine_ref[...])
+    ancestors = {below: solution_now.astype(bf16).astype(f32)}
+    sep_out = jnp.where(level == below, solution_now, 0.0)
+    for now in reversed(range(below)):
+        factor = Factor(factor_refs[now], None, sep_rows, panel_rows)
+        blocks = [
+            picked(ancestors[a], factor.panel(a - now - 1), count).astype(bf16)
+            for a in range(now + 1, levels)
+        ]
+        solution_now = folds[2 * now][...] - dot(
+            jnp.concatenate(blocks, axis=1), folds[2 * now + 1][...]
+        )
         ancestors[now] = solution_now.astype(bf16).astype(f32)
         sep_out = jnp.where(level == now, solution_now, sep_out)
     sep_out_ref[...] = sep_out
-    leaving = [pltpu.make_async_copy(sep_out_ref, sep_out_hbm, sems.at[1])]
+    leaving = [pltpu.make_async_copy(sep_out_ref, sep_out_hbm, sems.at[0])]
     leaving[0].start()
 
-    copy.wait()
-    blocks = jnp.concatenate(
-        [picked(ancestors[a], panel_ref[0, a], count).astype(bf16) for a in range(levels)], axis=1
-    )
+    blocks = [
+        picked(ancestors[a], leaf_panel(carry_ref, a, panel_rows), count).astype(bf16)
+        for a in range(levels)
+    ]
+    blocks = jnp.concatenate(blocks, axis=1)
     size = folded_ref.shape[1]
     step = min(256, size)
     for low in range(0, size, step):
@@ -355,7 +367,7 @@
             pltpu.make_async_copy(
                 leaf_out_ref.at[:, columns],
                 leaf_out_hbm.at[:, columns],
-                sems.at[len(leaving) + 1],
+                sems.at[len(leaving)],
             )
         )
         leaving[-1].start()
@@ -386,7 +398,7 @@
         hbm=range(4),
         scratch=[panel_smem, panel_smem, sems],
     )
-    arrived = exchange(carry, 1)
+    first_carry, arrived = carry, exchange(carry, 1)
     leaf_inverse, leaf_update, leaf_solved, sums, message = call(
         partial(leaf_up_kernel, levels),
         [
@@ -418,6 +430,8 @@
             )
             arrived = exchange(carry, 2 << now, upward=now + 2 == levels)
             pair += (carry,)
+        elif levels > 1:
+            pair += (message,)
         factors += call(partial(keep_kernel, now), [carry_shape(now)], pair)
         factors.append(exchange(factors[-1], 1, "rhs"))
         if now + 1 == levels:
@@ -436,16 +450,31 @@
         )
         solved.append(z)
         received = exchange(message, 2 << now)
+    below = levels - 1
+    triples, shapes = (), []
+    for now in range(below):
+        triples += (factors[2 * now], factors[2 * now + 1], solved[now])
+        shapes += [((scenarios, sep_rows), f32), (((below - now) * panel_rows, sep_rows), bf16)]
+    folds = call(
+        partial(fold_kernel, levels, panel_rows),
+        shapes,
+        triples,
+        flops=6 * below * scenarios * sep_rows * sep_rows,
+    )
+    square = call(
+        partial(square_kernel, panel_rows),
+        [((sep_rows, sep_rows), bf16)] * 2,
+        (factors[-2], factors[-1]),
+        flops=2 * sep_rows**3,
+    )
     return call(
         partial(down_kernel, levels),
         [((scenarios, size), f32), ((scenarios, sep_rows), f32)],
-        (leaf_panel, sums, received, base, folded, *factors, *solved),
-        hbm=(0,),
+        (first_carry, sums, received, base, folded, *square, *factors[: 2 * below : 2], *folds),
         hbm_outs=True,
         scratch=[
             pltpu.VMEM((scenarios, size), f32),
             pltpu.VMEM((scenarios, sep_rows), f32),
-            panel_smem,
             sems,
         ],
         flops=leaf_flops,

time: 34.1 us -> 33.7 us (0.988)
  waiting for transfers between devices: 10.5 us -> 9.87 us
    ppermute x9, waiting for transfers between devices: 10.5 us -> 9.87 us  [exchange(): lax.ppermute(block, axis, [pair for pair in route if not upward or pair[0...]
    pallas_call x11 -> x13, Pallas kernels: 8.3 us -> 8.54 us  [call(): pl.pallas_call(kernel, out_shape=outs, in_specs=[pl.BlockSpec(memory_spac...]
  transfers between devices with their start and end apart: 9 -> 9, of which waited for: 6 -> 6; matrix products, arithmetic and copies ran while one was open for 0% -> 0% of each run, Pallas kernels for 13% -> 15%
where the time goes in v7:
time: 33.7 us; the launch traced here: 33.5 us
  starting transfers between devices  14.3 us (42%)
  waiting for transfers between devices  9.87 us (29%)
  Pallas kernels  8.54 us (25%)
  between operations  0.76 us (2%)
    ppermute x9, starting transfers between devices, exchange(): lax.ppermute(block, axis, [pair for pair in route if not upward or pair[0...  14.3 us
    ppermute x9, waiting for transfers between devices, exchange(): lax.ppermute(block, axis, [pair for pair in route if not upward or pair[0...  9.87 us
    pallas_call x13, Pallas kernels, call(): pl.pallas_call(kernel, out_shape=outs, in_specs=[pl.BlockSpec(memory_spac...  8.54 us
  transfers between devices with their start and end apart: 9, of which 6 were waited for; matrix products, arithmetic and copies ran while one was open for 0% of the time, Pallas kernels for 15%

profile of v7, /device:TPU:0, one launch (start us, length us, event | category | flops | bytes accessed | tf_op | source)
XLA Modules:
  0.0 33.5 jit_solution(12966494875156887104)
XLA Ops:
  0.6 1.1 %shard_map.95.carry_ref.own_ref.refs_0_ = bf16[144,512]{1,0:T(8,128)(2,1)S(1)} custom-call(s32[1,3]{1,0:T(1,128)} %sep_panel_hbm.1, s32[1,3]{1,0:T(1,128)} %leaf_panel_hbm.1, bf16[256,256]{1,0:T(8,128)(2,1)} %sep_inverse_hbm.1, bf16[3,256,128]{2,1,0:T(8,128)(2,1)} %bitcast.3), custom_call_target="tpu_custom_call" | custom-call | bytes 475160 | tf_op jit(solution)/shard_map/pallas_call | solution.py:53
  1.7 3.0 %collective-permute-start.1 = (bf16[144,512]{1,0:T(8,128)(2,1)S(1)}, bf16[144,512]{1,0:T(8,128)(2,1)S(1)}, u32[]{:S(2)}, u32[]{:S(2)}) collective-permute-start(bf16[144,512]{1,0:T(8,128)(2,1)S(1)} %shard_map.95.carry_ref.own_ref.refs_0_), channel_id=1, source_target_pairs={{0,4},{4,0},{8,12},{12,8},{16,20},{20,16},{24,28},{28,24},{1,5},{5... | collective-permute-start | bytes 442376 | tf_op jit(solution)/shard_map/ppermute | solution.py:71
  4.7 2.6 %shard_map.96 = (bf16[1024,1024]{1,0:T(8,128)(2,1)S(1)}, bf16[3,1024,128]{2,1,0:T(8,128)(2,1)S(1)}, f32[256,1024]{1,0:T(8,128)S(1)}, f32[256,768]{1,0:T(8,128)S(1)}, bf16[256,512]{1,0:T(8,128)(2,1)S(1)}) custom-call(bf16[144,512]{1,0:T(8,128)(2,1)S(1)} %shard_map.95.carry_ref.own_ref.refs_0_, bf16[256,1024]{1,0:T(8,128)(2,1)} %rhs_hbm.1, ...), custom_call_target="tpu_custom_call" | custom-call | flops 738197504 | bytes 8667136 | tf_op jit(solution)/shard_map/pallas_call | solution.py:53
  7.4 0.1 collective-permute-start
  7.5 1.1 %collective-permute-done.1.received_ref.refs_0_ = bf16[144,512]{1,0:T(8,128)(2,1)S(1)} collective-permute-done((bf16[144,512]{1,0:T(8,128)(2,1)S(1)}, bf16[144,512]{1,0:T(8,128)(2,1)S(1)}, u32[]{:S(2)}, u32[]{:S(2)}) %collective-permute-start.1) | collective-permute-done | bytes 147488 | tf_op jit(solution)/shard_map/ppermute | solution.py:71
  8.6 0.1 collective-permute-start.2
  8.7 1.9 %collective-permute-start.3 = (bf16[144,384]{1,0:T(8,128)(2,1)S(1)}, bf16[144,384]{1,0:T(8,128)(2,1)S(1)}, u32[]{:S(2)}, u32[]{:S(2)}) collective-permute-start(bf16[144,384]{1,0:T(8,128)(2,1)S(1)} %shard_map.97.refs_0_.own_ref), channel_id=1, source_target_pairs={{0,8},{4,12},{8,0},{12,4},{16,24},{20,28},{24,16},{28,20},{1,9},{5... | collective-permute-start | bytes 331784 | tf_op jit(solution)/shard_map/ppermute | solution.py:71
  10.6 1.4 %shard_map.99 = (f32[256,1024]{1,0:T(8,128)S(1)}, bf16[384,1024]{1,0:T(8,128)(2,1)S(1)}) custom-call(f32[256,1024]{1,0:T(8,128)S(1)} %get-tuple-element.23.solved_ref, bf16[3,1024,128]{2,1,0:T(8,128)(2,1)S(1)} %get-tuple-element.24.update_ref, bf16[1024,1024]{1,0:T(8,128)(2,1)S(1)} %get-tuple-element.25.inverse_ref), custom_call_target="tpu_custom_call" | custom-call | flops 1476395008 | bytes 5767168 | tf_op jit(solution)/shard_map/pallas_call | solution.py:53
  12.0 2.2 %collective-permute-done.3.refs_2_.received_ref = bf16[144,384]{1,0:T(8,128)(2,1)S(1)} collective-permute-done((bf16[144,384]{1,0:T(8,128)(2,1)S(1)}, bf16[144,384]{1,0:T(8,128)(2,1)S(1)}, u32[]{:S(2)}, u32[]{:S(2)}) %collective-permute-start.3) | collective-permute-done | bytes 110624 | tf_op jit(solution)/shard_map/ppermute | solution.py:71
  14.2 1.0 %collective-permute-done.received_ref = bf16[256,512]{1,0:T(8,128)(2,1)S(1)} collective-permute-done((bf16[256,512]{1,0:T(8,128)(2,1)S(1)}, bf16[256,512]{1,0:T(8,128)(2,1)S(1)}, u32[]{:S(2)}, u32[]{:S(2)}) %collective-permute-start) | collective-permute-done | bytes 262176 | tf_op jit(solution)/shard_map/ppermute | solution.py:71
  15.2 0.0 collective-permute-done.2.other_ref.refs_1_
  15.2 0.4 %shard_map.100 = (f32[256,256]{1,0:T(8,128)S(1)}, f32[256,512]{1,0:T(8,128)S(1)}, bf16[256,512]{1,0:T(8,128)(2,1)S(1)}) custom-call(f32[256,768]{1,0:T(8,128)S(1)} %get-tuple-element.21.own_ref, bf16[256,512]{1,0:T(8,128)(2,1)S(1)} %collective-permute-done.received_ref, bf16[144,512]{1,0:T(8,128)(2,1)S(1)} %shard_map.98.factor_ref.refs_0_.refs_7_, ...), custom_call_target="tpu_custom_call" | custom-call | flops 67108864 | bytes 3436544 | tf_op jit(solution)/shard_map/pallas_call | solution.py:53
  15.6 1.6 %collective-permute-start.4 = (bf16[256,512]{1,0:T(8,128)(2,1)S(1)}, bf16[256,512]{1,0:T(8,128)(2,1)S(1)}, u32[]{:S(2)}, u32[]{:S(2)}) collective-permute-start(bf16[256,512]{1,0:T(8,128)(2,1)S(1)} %get-tuple-element.28), channel_id=1, source_target_pairs={{0,8},{4,12},{8,0},{12,4},{16,24},{20,28},{24,16},{28,20},{1,9},{5... | collective-permute-start | bytes 786440 | tf_op jit(solution)/shard_map/ppermute | solution.py:71
  17.3 0.1 collective-permute-start.5
  17.4 4.5 %collective-permute-start.7 = (bf16[144,256]{1,0:T(8,128)(2,1)S(1)}, bf16[144,256]{1,0:T(8,128)(2,1)S(1)}, u32[]{:S(2)}, u32[]{:S(2)}) collective-permute-start(bf16[144,256]{1,0:T(8,128)(2,1)S(1)} %shard_map.101.refs_0_.own_ref), channel_id=1, source_target_pairs={{0,16},{4,20},{8,24},{12,28},{1,17},{5,21},{9,25},{13,29},{2,18},{... | collective-permute-start | bytes 221192 | tf_op jit(solution)/shard_map/ppermute | solution.py:71
  21.9 0.0 collective-permute-done.5.other_ref.refs_4_
  21.9 0.7 %collective-permute-done.4.received_ref = bf16[256,512]{1,0:T(8,128)(2,1)S(1)} collective-permute-done((bf16[256,512]{1,0:T(8,128)(2,1)S(1)}, bf16[256,512]{1,0:T(8,128)(2,1)S(1)}, u32[]{:S(2)}, u32[]{:S(2)}) %collective-permute-start.4) | collective-permute-done | bytes 262176 | tf_op jit(solution)/shard_map/ppermute | solution.py:71
  22.6 0.4 %shard_map.103 = (f32[256,256]{1,0:T(8,128)S(1)}, f32[256,256]{1,0:T(8,128)S(1)}, bf16[256,256]{1,0:T(8,128)(2,1)S(1)}) custom-call(f32[256,512]{1,0:T(8,128)S(1)} %get-tuple-element.27.own_ref, bf16[256,512]{1,0:T(8,128)(2,1)S(1)} %collective-permute-done.4.received_ref, bf16[144,384]{1,0:T(8,128)(2,1)S(1)} %shard_map.102.factor_ref.refs_3_.refs_8_, ...), custom_call_target="tpu_custom_call" | custom-call | flops 67108864 | bytes 1662976 | tf_op jit(solution)/shard_map/pallas_call | solution.py:53
  23.0 3.0 %collective-permute-start.6 = (bf16[256,256]{1,0:T(8,128)(2,1)S(1)}, bf16[256,256]{1,0:T(8,128)(2,1)S(1)}, u32[]{:S(2)}, u32[]{:S(2)}) collective-permute-start(bf16[256,256]{1,0:T(8,128)(2,1)S(1)} %get-tuple-element.30.refs_0_), channel_id=1, source_target_pairs={{0,16},{4,20},{8,24},{12,28},{16,0},{20,4},{24,8},{28,12},{1,17},{... | collective-permute-start | bytes 393224 | tf_op jit(solution)/shard_map/ppermute | solution.py:71
  26.0 0.0 collective-permute-done.7.received_ref
  26.0 0.1 collective-permute-start.8
  26.1 0.4 %shard_map.106 = (f32[256,256]{1,0:T(8,128)S(1)}, bf16[256,256]{1,0:T(8,128)(2,1)S(1)}, f32[256,256]{1,0:T(8,128)S(1)}, bf16[128,256]{1,0:T(8,128)(2,1)S(1)}) custom-call(bf16[144,512]{1,0:T(8,128)(2,1)S(1)} %shard_map.98.factor_ref.refs_0_.refs_7_, bf16[144,512]{1,0:T(8,128)(2,1)S(1)} %collective-permute-done.2.other_ref.refs_1_, ...), custom_call_target="tpu_custom_call" | custom-call | flops 201326592 | bytes 1761280 | tf_op jit(solution)/shard_map/pallas_call | solution.py:53
  26.5 0.8 %collective-permute-done.8.other_ref = bf16[144,256]{1,0:T(8,128)(2,1)S(1)} collective-permute-done((bf16[144,256]{1,0:T(8,128)(2,1)S(1)}, bf16[144,256]{1,0:T(8,128)(2,1)S(1)}, u32[]{:S(2)}, u32[]{:S(2)}) %collective-permute-start.8) | collective-permute-done | bytes 73760 | tf_op jit(solution)/shard_map/ppermute | solution.py:71
  27.3 0.2 shard_map.105
  27.6 4.0 %collective-permute-done.6.refs_2_ = bf16[256,256]{1,0:T(8,128)(2,1)S(1)} collective-permute-done((bf16[256,256]{1,0:T(8,128)(2,1)S(1)}, bf16[256,256]{1,0:T(8,128)(2,1)S(1)}, u32[]{:S(2)}, u32[]{:S(2)}) %collective-permute-start.6) | collective-permute-done | bytes 131104 | tf_op jit(solution)/shard_map/ppermute | solution.py:71
  31.6 1.9 %shard_map.107 = (f32[256,1024]{1,0:T(8,128)}, f32[256,256]{1,0:T(8,128)}) custom-call(bf16[144,512]{1,0:T(8,128)(2,1)S(1)} %shard_map.95.carry_ref.own_ref.refs_0_, f32[256,256]{1,0:T(8,128)S(1)} %get-tuple-element.29.refs_1_, bf16[256,256]{1,0:T(8,128)(2,1)S(1)} %collective-permute-done.6.refs_2_, f32[256,1024]{1,0:T(8,128)S(1)} %get-tuple-element.31.refs_3_, ...), custom_call_target="tpu_custom_call" | custom-call | flops 738197504 | bytes 4927488 | tf_op jit(solution)/shard_map/pallas_call | solution.py:53
  (5 shorter events, 0.1 us)
Async XLA Ops:
  1.7 6.9 %collective-permute-start.1 = (bf16[144,512]{1,0:T(8,128)(2,1)S(1)}, bf16[144,512]{1,0:T(8,128)(2,1)S(1)}, u32[]{:S(2)}, u32[]{:S(2)}) collective-permute-start(bf16[144,512]{1,0:T(8,128)(2,1)S(1)} %shard_map.95.carry_ref.own_ref.refs_0_), channel_id=1, source_target_pairs={{0,4},{4,0},{8,12},{12,8},{16,20},{20,16},{24,28},{28,24},{1,5},{5... | collective-permute-start | bytes 442376 | tf_op jit(solution)/shard_map/ppermute | solution.py:71
  7.4 7.8 %collective-permute-start = (bf16[256,512]{1,0:T(8,128)(2,1)S(1)}, bf16[256,512]{1,0:T(8,128)(2,1)S(1)}, u32[]{:S(2)}, u32[]{:S(2)}) collective-permute-start(bf16[256,512]{1,0:T(8,128)(2,1)S(1)} %get-tuple-element.22), channel_id=1, source_target_pairs={{0,4},{4,0},{8,12},{12,8},{16,20},{20,16},{24,28},{28,24},{1,5},{5... | collective-permute-start | bytes 786440 | tf_op jit(solution)/shard_map/ppermute | solution.py:71
  8.6 6.6 %collective-permute-start.2 = (bf16[144,512]{1,0:T(8,128)(2,1)S(1)}, bf16[144,512]{1,0:T(8,128)(2,1)S(1)}, u32[]{:S(2)}, u32[]{:S(2)}) collective-permute-start(bf16[144,512]{1,0:T(8,128)(2,1)S(1)} %shard_map.98.factor_ref.refs_0_.refs_7_), channel_id=1, source_target_pairs={{0,1},{1,0},{2,3},{3,2},{4,5},{5,4},{6,7},{7,6},{8,9},{9,8},{10,11... | collective-permute-start | bytes 442376 | tf_op jit(solution)/shard_map/ppermute | solution.py:71
  8.7 5.5 %collective-permute-start.3 = (bf16[144,384]{1,0:T(8,128)(2,1)S(1)}, bf16[144,384]{1,0:T(8,128)(2,1)S(1)}, u32[]{:S(2)}, u32[]{:S(2)}) collective-permute-start(bf16[144,384]{1,0:T(8,128)(2,1)S(1)} %shard_map.97.refs_0_.own_ref), channel_id=1, source_target_pairs={{0,8},{4,12},{8,0},{12,4},{16,24},{20,28},{24,16},{28,20},{1,9},{5... | collective-permute-start | bytes 331784 | tf_op jit(solution)/shard_map/ppermute | solution.py:71
  15.6 7.0 %collective-permute-start.4 = (bf16[256,512]{1,0:T(8,128)(2,1)S(1)}, bf16[256,512]{1,0:T(8,128)(2,1)S(1)}, u32[]{:S(2)}, u32[]{:S(2)}) collective-permute-start(bf16[256,512]{1,0:T(8,128)(2,1)S(1)} %get-tuple-element.28), channel_id=1, source_target_pairs={{0,8},{4,12},{8,0},{12,4},{16,24},{20,28},{24,16},{28,20},{1,9},{5... | collective-permute-start | bytes 786440 | tf_op jit(solution)/shard_map/ppermute | solution.py:71
  17.3 4.6 %collective-permute-start.5 = (bf16[144,384]{1,0:T(8,128)(2,1)S(1)}, bf16[144,384]{1,0:T(8,128)(2,1)S(1)}, u32[]{:S(2)}, u32[]{:S(2)}) collective-permute-start(bf16[144,384]{1,0:T(8,128)(2,1)S(1)} %shard_map.102.factor_ref.refs_3_.refs_8_), channel_id=1, source_target_pairs={{0,1},{1,0},{2,3},{3,2},{4,5},{5,4},{6,7},{7,6},{8,9},{9,8},{10,11... | collective-permute-start | bytes 331784 | tf_op jit(solution)/shard_map/ppermute | solution.py:71
  17.4 8.6 %collective-permute-start.7 = (bf16[144,256]{1,0:T(8,128)(2,1)S(1)}, bf16[144,256]{1,0:T(8,128)(2,1)S(1)}, u32[]{:S(2)}, u32[]{:S(2)}) collective-permute-start(bf16[144,256]{1,0:T(8,128)(2,1)S(1)} %shard_map.101.refs_0_.own_ref), channel_id=1, source_target_pairs={{0,16},{4,20},{8,24},{12,28},{1,17},{5,21},{9,25},{13,29},{2,18},{... | collective-permute-start | bytes 221192 | tf_op jit(solution)/shard_map/ppermute | solution.py:71
  23.0 8.6 %collective-permute-start.6 = (bf16[256,256]{1,0:T(8,128)(2,1)S(1)}, bf16[256,256]{1,0:T(8,128)(2,1)S(1)}, u32[]{:S(2)}, u32[]{:S(2)}) collective-permute-start(bf16[256,256]{1,0:T(8,128)(2,1)S(1)} %get-tuple-element.30.refs_0_), channel_id=1, source_target_pairs={{0,16},{4,20},{8,24},{12,28},{16,0},{20,4},{24,8},{28,12},{1,17},{... | collective-permute-start | bytes 393224 | tf_op jit(solution)/shard_map/ppermute | solution.py:71
  26.0 1.3 %collective-permute-start.8 = (bf16[144,256]{1,0:T(8,128)(2,1)S(1)}, bf16[144,256]{1,0:T(8,128)(2,1)S(1)}, u32[]{:S(2)}, u32[]{:S(2)}) collective-permute-start(bf16[144,256]{1,0:T(8,128)(2,1)S(1)} %shard_map.104.own_ref), channel_id=1, source_target_pairs={{0,1},{1,0},{2,3},{3,2},{4,5},{5,4},{6,7},{7,6},{8,9},{9,8},{10,11... | collective-permute-start | bytes 221192 | tf_op jit(solution)/shard_map/ppermute | solution.py:71

commit v8 on v7

--- a/solution.py
+++ b/solution.py
@@ -66,9 +66,18 @@
     )(*args)
 
 
-def exchange(block, distance, axis="leaf", upward=False):
-    route = [(i, i ^ distance) for i in range(lax.axis_size(axis))]
-    return lax.ppermute(block, axis, [pair for pair in route if not upward or pair[0] < pair[1]])
+def exchange(block, distance, axis="leaf"):
+    return lax.ppermute(block, axis, [(i, i ^ distance) for i in range(lax.axis_size(axis))])
+
+
+def exchange_among(block, distance, members):
+    leaves, parts = lax.axis_size("leaf"), lax.axis_size("rhs")
+    route = []
+    for leaf in range(leaves):
+        for part in range(parts):
+            target = (leaf ^ distance, part) if leaf in members else (leaf, part ^ 1)
+            route.append((leaf * parts + part, target[0] * parts + target[1]))
+    return lax.ppermute(block, ("leaf", "rhs"), route)
 
 
 def upper_part():
@@ -204,6 +213,14 @@
     refs[-1][...] = jnp.where(lower, own_ref[...], received_ref[...])
 
 
+def keep_top_kernel(step, own_ref, received_ref, passed_ref, out_ref):
+    k = lax.axis_index("leaf")
+    lower = ((k >> step) & 1) == 0
+    near = ((k >> (step - 1)) & 1) == 0
+    upper = jnp.where(near, received_ref[...], passed_ref[...])
+    out_ref[...] = jnp.where(lower, own_ref[...], upper)
+
+
 class Factor:
     def __init__(self, own_ref, other_ref, sep_rows, panel_rows):
         self.refs = own_ref, other_ref
@@ -428,11 +445,17 @@
             (carry,) = call(
                 partial(hand_on_kernel, now, sep_rows), [carry_shape(now + 1)], pair
             )
-            arrived = exchange(carry, 2 << now, upward=now + 2 == levels)
+            if now + 2 < levels:
+                arrived = exchange(carry, 2 << now)
+            else:
+                quarter = 1 << now
+                arrived = exchange_among(carry, 3 * quarter, range(quarter, 3 * quarter))
+                passed = exchange_among(arrived, quarter, range(2 * quarter, 4 * quarter))
             pair += (carry,)
         elif levels > 1:
-            pair += (message,)
-        factors += call(partial(keep_kernel, now), [carry_shape(now)], pair)
+            pair += (passed,)
+        kernel = keep_kernel if now + 1 < levels or levels == 1 else keep_top_kernel
+        factors += call(partial(kernel, now), [carry_shape(now)], pair)
         factors.append(exchange(factors[-1], 1, "rhs"))
         if now + 1 == levels:
             break

time: 33.7 us -> 33.7 us (level)
  waiting for transfers between devices: 9.87 us -> 13.7 us
  starting transfers between devices: 14.3 us -> 10.5 us
    ppermute x9 -> x10, waiting for transfers between devices: 9.87 us -> 13.7 us  [the longest x8 12.8 us: exchange(): lax.ppermute(block, axis, [(i, i ^ distance) for i in range(lax.axis_size...]
    ppermute x9 -> x10, starting transfers between devices: 14.3 us -> 10.5 us  [the longest x8 9.62 us: exchange(): lax.ppermute(block, axis, [(i, i ^ distance) for i in range(lax.axis_size...]
  transfers between devices with their start and end apart: 9 -> 10, of which waited for: 6 -> 7; matrix products, arithmetic and copies ran while one was open for 0% -> 0% of each run, Pallas kernels for 15% -> 15%
where the time goes in v8:
time: 33.7 us; the launch traced here: 33.5 us
  waiting for transfers between devices  13.7 us (41%)
  starting transfers between devices  10.5 us (31%)
  Pallas kernels  8.55 us (25%)
  between operations  0.74 us (2%)
    ppermute x8, waiting for transfers between devices, exchange(): lax.ppermute(block, axis, [(i, i ^ distance) for i in range(lax.axis_size...  12.8 us
    ppermute x8, starting transfers between devices, exchange(): lax.ppermute(block, axis, [(i, i ^ distance) for i in range(lax.axis_size...  9.62 us
    pallas_call x13, Pallas kernels, call(): pl.pallas_call(kernel, out_shape=outs, in_specs=[pl.BlockSpec(memory_spac...  8.55 us
    ppermute x2, waiting for transfers between devices, exchange_among(): return lax.ppermute(block, ('leaf', 'rhs'), route)  0.92 us
    ppermute x2, starting transfers between devices, exchange_among(): return lax.ppermute(block, ('leaf', 'rhs'), route)  0.85 us
  transfers between devices with their start and end apart: 10, of which 7 were waited for; matrix products, arithmetic and copies ran while one was open for 0% of the time, Pallas kernels for 15%

profile of v8, /device:TPU:0, one launch (start us, length us, event | category | flops | bytes accessed | tf_op | source)
XLA Modules:
  0.0 33.5 jit_solution(18176747879435621525)
XLA Ops:
  0.6 1.1 %shard_map.95.carry_ref.own_ref.refs_0_ = bf16[144,512]{1,0:T(8,128)(2,1)S(1)} custom-call(s32[1,3]{1,0:T(1,128)} %sep_panel_hbm.1, s32[1,3]{1,0:T(1,128)} %leaf_panel_hbm.1, bf16[256,256]{1,0:T(8,128)(2,1)} %sep_inverse_hbm.1, bf16[3,256,128]{2,1,0:T(8,128)(2,1)} %bitcast.3), custom_call_target="tpu_custom_call" | custom-call | bytes 475160 | tf_op jit(solution)/shard_map/pallas_call | solution.py:53
  1.7 3.0 %collective-permute-start.1 = (bf16[144,512]{1,0:T(8,128)(2,1)S(1)}, bf16[144,512]{1,0:T(8,128)(2,1)S(1)}, u32[]{:S(2)}, u32[]{:S(2)}) collective-permute-start(bf16[144,512]{1,0:T(8,128)(2,1)S(1)} %shard_map.95.carry_ref.own_ref.refs_0_), channel_id=1, source_target_pairs={{0,4},{4,0},{8,12},{12,8},{16,20},{20,16},{24,28},{28,24},{1,5},{5... | collective-permute-start | bytes 442376 | tf_op jit(solution)/shard_map/ppermute | solution.py:70
  4.7 2.6 %shard_map.96 = (bf16[1024,1024]{1,0:T(8,128)(2,1)S(1)}, bf16[3,1024,128]{2,1,0:T(8,128)(2,1)S(1)}, f32[256,1024]{1,0:T(8,128)S(1)}, f32[256,768]{1,0:T(8,128)S(1)}, bf16[256,512]{1,0:T(8,128)(2,1)S(1)}) custom-call(bf16[144,512]{1,0:T(8,128)(2,1)S(1)} %shard_map.95.carry_ref.own_ref.refs_0_, bf16[256,1024]{1,0:T(8,128)(2,1)} %rhs_hbm.1, ...), custom_call_target="tpu_custom_call" | custom-call | flops 738197504 | bytes 8667136 | tf_op jit(solution)/shard_map/pallas_call | solution.py:53
  7.4 0.1 collective-permute-start
  7.5 1.1 %collective-permute-done.1.received_ref.refs_0_ = bf16[144,512]{1,0:T(8,128)(2,1)S(1)} collective-permute-done((bf16[144,512]{1,0:T(8,128)(2,1)S(1)}, bf16[144,512]{1,0:T(8,128)(2,1)S(1)}, u32[]{:S(2)}, u32[]{:S(2)}) %collective-permute-start.1) | collective-permute-done | bytes 147488 | tf_op jit(solution)/shard_map/ppermute | solution.py:70
  8.6 0.1 collective-permute-start.2
  8.7 1.9 %collective-permute-start.3 = (bf16[144,384]{1,0:T(8,128)(2,1)S(1)}, bf16[144,384]{1,0:T(8,128)(2,1)S(1)}, u32[]{:S(2)}, u32[]{:S(2)}) collective-permute-start(bf16[144,384]{1,0:T(8,128)(2,1)S(1)} %shard_map.97.refs_0_.own_ref), channel_id=1, source_target_pairs={{0,8},{4,12},{8,0},{12,4},{16,24},{20,28},{24,16},{28,20},{1,9},{5... | collective-permute-start | bytes 331784 | tf_op jit(solution)/shard_map/ppermute | solution.py:70
  10.6 1.4 %shard_map.99 = (f32[256,1024]{1,0:T(8,128)S(1)}, bf16[384,1024]{1,0:T(8,128)(2,1)S(1)}) custom-call(f32[256,1024]{1,0:T(8,128)S(1)} %get-tuple-element.23.solved_ref, bf16[3,1024,128]{2,1,0:T(8,128)(2,1)S(1)} %get-tuple-element.24.update_ref, bf16[1024,1024]{1,0:T(8,128)(2,1)S(1)} %get-tuple-element.25.inverse_ref), custom_call_target="tpu_custom_call" | custom-call | flops 1476395008 | bytes 5767168 | tf_op jit(solution)/shard_map/pallas_call | solution.py:53
  12.0 2.2 %collective-permute-done.3.refs_2_.received_ref = bf16[144,384]{1,0:T(8,128)(2,1)S(1)} collective-permute-done((bf16[144,384]{1,0:T(8,128)(2,1)S(1)}, bf16[144,384]{1,0:T(8,128)(2,1)S(1)}, u32[]{:S(2)}, u32[]{:S(2)}) %collective-permute-start.3) | collective-permute-done | bytes 110624 | tf_op jit(solution)/shard_map/ppermute | solution.py:70
  14.2 1.0 %collective-permute-done.received_ref = bf16[256,512]{1,0:T(8,128)(2,1)S(1)} collective-permute-done((bf16[256,512]{1,0:T(8,128)(2,1)S(1)}, bf16[256,512]{1,0:T(8,128)(2,1)S(1)}, u32[]{:S(2)}, u32[]{:S(2)}) %collective-permute-start) | collective-permute-done | bytes 262176 | tf_op jit(solution)/shard_map/ppermute | solution.py:70
  15.2 0.0 collective-permute-done.2.other_ref.refs_1_
  15.2 0.4 %shard_map.100 = (f32[256,256]{1,0:T(8,128)S(1)}, f32[256,512]{1,0:T(8,128)S(1)}, bf16[256,512]{1,0:T(8,128)(2,1)S(1)}) custom-call(f32[256,768]{1,0:T(8,128)S(1)} %get-tuple-element.21.own_ref, bf16[256,512]{1,0:T(8,128)(2,1)S(1)} %collective-permute-done.received_ref, bf16[144,512]{1,0:T(8,128)(2,1)S(1)} %shard_map.98.factor_ref.refs_0_.refs_7_, ...), custom_call_target="tpu_custom_call" | custom-call | flops 67108864 | bytes 3436544 | tf_op jit(solution)/shard_map/pallas_call | solution.py:53
  15.6 1.6 %collective-permute-start.4 = (bf16[256,512]{1,0:T(8,128)(2,1)S(1)}, bf16[256,512]{1,0:T(8,128)(2,1)S(1)}, u32[]{:S(2)}, u32[]{:S(2)}) collective-permute-start(bf16[256,512]{1,0:T(8,128)(2,1)S(1)} %get-tuple-element.28), channel_id=1, source_target_pairs={{0,8},{4,12},{8,0},{12,4},{16,24},{20,28},{24,16},{28,20},{1,9},{5... | collective-permute-start | bytes 786440 | tf_op jit(solution)/shard_map/ppermute | solution.py:70
  17.3 0.1 collective-permute-start.5
  17.4 0.5 %collective-permute-start.7 = (bf16[144,256]{1,0:T(8,128)(2,1)S(1)}, bf16[144,256]{1,0:T(8,128)(2,1)S(1)}, u32[]{:S(2)}, u32[]{:S(2)}) collective-permute-start(bf16[144,256]{1,0:T(8,128)(2,1)S(1)} %shard_map.101.refs_0_.own_ref), channel_id=1, source_target_pairs={{0,1},{1,0},{2,3},{3,2},{4,5},{5,4},{6,7},{7,6},{8,16},{9,17},{10,... | collective-permute-start | bytes 221192 | tf_op jit(solution)/shard_map/ppermute | solution.py:80
  17.9 0.9 %collective-permute-done.7.received_ref = bf16[144,256]{1,0:T(8,128)(2,1)S(1)} collective-permute-done((bf16[144,256]{1,0:T(8,128)(2,1)S(1)}, bf16[144,256]{1,0:T(8,128)(2,1)S(1)}, u32[]{:S(2)}, u32[]{:S(2)}) %collective-permute-start.7) | collective-permute-done | bytes 73760 | tf_op jit(solution)/shard_map/ppermute | solution.py:80
  18.8 0.4 %collective-permute-start.8 = (bf16[144,256]{1,0:T(8,128)(2,1)S(1)}, bf16[144,256]{1,0:T(8,128)(2,1)S(1)}, u32[]{:S(2)}, u32[]{:S(2)}) collective-permute-start(bf16[144,256]{1,0:T(8,128)(2,1)S(1)} %collective-permute-done.7.received_ref), channel_id=1, source_target_pairs={{0,1},{1,0},{2,3},{3,2},{4,5},{5,4},{6,7},{7,6},{8,9},{9,8},{10,11... | collective-permute-start | bytes 221192 | tf_op jit(solution)/shard_map/ppermute | solution.py:80
  19.1 0.0 collective-permute-done.5.other_ref.refs_4_
  19.1 3.5 %collective-permute-done.4.received_ref = bf16[256,512]{1,0:T(8,128)(2,1)S(1)} collective-permute-done((bf16[256,512]{1,0:T(8,128)(2,1)S(1)}, bf16[256,512]{1,0:T(8,128)(2,1)S(1)}, u32[]{:S(2)}, u32[]{:S(2)}) %collective-permute-start.4) | collective-permute-done | bytes 262176 | tf_op jit(solution)/shard_map/ppermute | solution.py:70
  22.6 0.4 %shard_map.103 = (f32[256,256]{1,0:T(8,128)S(1)}, f32[256,256]{1,0:T(8,128)S(1)}, bf16[256,256]{1,0:T(8,128)(2,1)S(1)}) custom-call(f32[256,512]{1,0:T(8,128)S(1)} %get-tuple-element.27.own_ref, bf16[256,512]{1,0:T(8,128)(2,1)S(1)} %collective-permute-done.4.received_ref, bf16[144,384]{1,0:T(8,128)(2,1)S(1)} %shard_map.102.factor_ref.refs_3_.refs_8_, ...), custom_call_target="tpu_custom_call" | custom-call | flops 67108864 | bytes 1662976 | tf_op jit(solution)/shard_map/pallas_call | solution.py:53
  23.0 2.8 %collective-permute-start.6 = (bf16[256,256]{1,0:T(8,128)(2,1)S(1)}, bf16[256,256]{1,0:T(8,128)(2,1)S(1)}, u32[]{:S(2)}, u32[]{:S(2)}) collective-permute-start(bf16[256,256]{1,0:T(8,128)(2,1)S(1)} %get-tuple-element.30), channel_id=1, source_target_pairs={{0,16},{4,20},{8,24},{12,28},{16,0},{20,4},{24,8},{28,12},{1,17},{... | collective-permute-start | bytes 393224 | tf_op jit(solution)/shard_map/ppermute | solution.py:70
  25.8 0.0 collective-permute-done.8.passed_ref
  25.8 0.1 collective-permute-start.9
  25.9 1.3 %collective-permute-done.9.other_ref = bf16[144,256]{1,0:T(8,128)(2,1)S(1)} collective-permute-done((bf16[144,256]{1,0:T(8,128)(2,1)S(1)}, bf16[144,256]{1,0:T(8,128)(2,1)S(1)}, u32[]{:S(2)}, u32[]{:S(2)}) %collective-permute-start.9) | collective-permute-done | bytes 73760 | tf_op jit(solution)/shard_map/ppermute | solution.py:70
  27.2 0.2 shard_map.105
  27.4 0.4 %shard_map.106 = (f32[256,256]{1,0:T(8,128)S(1)}, bf16[256,256]{1,0:T(8,128)(2,1)S(1)}, f32[256,256]{1,0:T(8,128)S(1)}, bf16[128,256]{1,0:T(8,128)(2,1)S(1)}) custom-call(bf16[144,512]{1,0:T(8,128)(2,1)S(1)} %shard_map.98.factor_ref.refs_0_.refs_7_, bf16[144,512]{1,0:T(8,128)(2,1)S(1)} %collective-permute-done.2.other_ref.refs_1_, ...), custom_call_target="tpu_custom_call" | custom-call | flops 201326592 | bytes 1761280 | tf_op jit(solution)/shard_map/pallas_call | solution.py:53
  27.8 3.8 %collective-permute-done.6.refs_2_ = bf16[256,256]{1,0:T(8,128)(2,1)S(1)} collective-permute-done((bf16[256,256]{1,0:T(8,128)(2,1)S(1)}, bf16[256,256]{1,0:T(8,128)(2,1)S(1)}, u32[]{:S(2)}, u32[]{:S(2)}) %collective-permute-start.6) | collective-permute-done | bytes 131104 | tf_op jit(solution)/shard_map/ppermute | solution.py:70
  31.6 1.9 %shard_map.107 = (f32[256,1024]{1,0:T(8,128)}, f32[256,256]{1,0:T(8,128)}) custom-call(bf16[144,512]{1,0:T(8,128)(2,1)S(1)} %shard_map.95.carry_ref.own_ref.refs_0_, f32[256,256]{1,0:T(8,128)S(1)} %get-tuple-element.29.refs_1_, bf16[256,256]{1,0:T(8,128)(2,1)S(1)} %collective-permute-done.6.refs_2_, f32[256,1024]{1,0:T(8,128)S(1)} %get-tuple-element.31.refs_3_, ...), custom_call_target="tpu_custom_call" | custom-call | flops 738197504 | bytes 4927488 | tf_op jit(solution)/shard_map/pallas_call | solution.py:53
  (5 shorter events, 0.1 us)
Async XLA Ops:
  1.7 6.9 %collective-permute-start.1 = (bf16[144,512]{1,0:T(8,128)(2,1)S(1)}, bf16[144,512]{1,0:T(8,128)(2,1)S(1)}, u32[]{:S(2)}, u32[]{:S(2)}) collective-permute-start(bf16[144,512]{1,0:T(8,128)(2,1)S(1)} %shard_map.95.carry_ref.own_ref.refs_0_), channel_id=1, source_target_pairs={{0,4},{4,0},{8,12},{12,8},{16,20},{20,16},{24,28},{28,24},{1,5},{5... | collective-permute-start | bytes 442376 | tf_op jit(solution)/shard_map/ppermute | solution.py:70
  7.4 7.8 %collective-permute-start = (bf16[256,512]{1,0:T(8,128)(2,1)S(1)}, bf16[256,512]{1,0:T(8,128)(2,1)S(1)}, u32[]{:S(2)}, u32[]{:S(2)}) collective-permute-start(bf16[256,512]{1,0:T(8,128)(2,1)S(1)} %get-tuple-element.22), channel_id=1, source_target_pairs={{0,4},{4,0},{8,12},{12,8},{16,20},{20,16},{24,28},{28,24},{1,5},{5... | collective-permute-start | bytes 786440 | tf_op jit(solution)/shard_map/ppermute | solution.py:70
  8.6 6.6 %collective-permute-start.2 = (bf16[144,512]{1,0:T(8,128)(2,1)S(1)}, bf16[144,512]{1,0:T(8,128)(2,1)S(1)}, u32[]{:S(2)}, u32[]{:S(2)}) collective-permute-start(bf16[144,512]{1,0:T(8,128)(2,1)S(1)} %shard_map.98.factor_ref.refs_0_.refs_7_), channel_id=1, source_target_pairs={{0,1},{1,0},{2,3},{3,2},{4,5},{5,4},{6,7},{7,6},{8,9},{9,8},{10,11... | collective-permute-start | bytes 442376 | tf_op jit(solution)/shard_map/ppermute | solution.py:70
  8.7 5.5 %collective-permute-start.3 = (bf16[144,384]{1,0:T(8,128)(2,1)S(1)}, bf16[144,384]{1,0:T(8,128)(2,1)S(1)}, u32[]{:S(2)}, u32[]{:S(2)}) collective-permute-start(bf16[144,384]{1,0:T(8,128)(2,1)S(1)} %shard_map.97.refs_0_.own_ref), channel_id=1, source_target_pairs={{0,8},{4,12},{8,0},{12,4},{16,24},{20,28},{24,16},{28,20},{1,9},{5... | collective-permute-start | bytes 331784 | tf_op jit(solution)/shard_map/ppermute | solution.py:70
  15.6 7.0 %collective-permute-start.4 = (bf16[256,512]{1,0:T(8,128)(2,1)S(1)}, bf16[256,512]{1,0:T(8,128)(2,1)S(1)}, u32[]{:S(2)}, u32[]{:S(2)}) collective-permute-start(bf16[256,512]{1,0:T(8,128)(2,1)S(1)} %get-tuple-element.28), channel_id=1, source_target_pairs={{0,8},{4,12},{8,0},{12,4},{16,24},{20,28},{24,16},{28,20},{1,9},{5... | collective-permute-start | bytes 786440 | tf_op jit(solution)/shard_map/ppermute | solution.py:70
  17.3 1.8 %collective-permute-start.5 = (bf16[144,384]{1,0:T(8,128)(2,1)S(1)}, bf16[144,384]{1,0:T(8,128)(2,1)S(1)}, u32[]{:S(2)}, u32[]{:S(2)}) collective-permute-start(bf16[144,384]{1,0:T(8,128)(2,1)S(1)} %shard_map.102.factor_ref.refs_3_.refs_8_), channel_id=1, source_target_pairs={{0,1},{1,0},{2,3},{3,2},{4,5},{5,4},{6,7},{7,6},{8,9},{9,8},{10,11... | collective-permute-start | bytes 331784 | tf_op jit(solution)/shard_map/ppermute | solution.py:70
  17.4 1.4 %collective-permute-start.7 = (bf16[144,256]{1,0:T(8,128)(2,1)S(1)}, bf16[144,256]{1,0:T(8,128)(2,1)S(1)}, u32[]{:S(2)}, u32[]{:S(2)}) collective-permute-start(bf16[144,256]{1,0:T(8,128)(2,1)S(1)} %shard_map.101.refs_0_.own_ref), channel_id=1, source_target_pairs={{0,1},{1,0},{2,3},{3,2},{4,5},{5,4},{6,7},{7,6},{8,16},{9,17},{10,... | collective-permute-start | bytes 221192 | tf_op jit(solution)/shard_map/ppermute | solution.py:80
  18.8 7.0 %collective-permute-start.8 = (bf16[144,256]{1,0:T(8,128)(2,1)S(1)}, bf16[144,256]{1,0:T(8,128)(2,1)S(1)}, u32[]{:S(2)}, u32[]{:S(2)}) collective-permute-start(bf16[144,256]{1,0:T(8,128)(2,1)S(1)} %collective-permute-done.7.received_ref), channel_id=1, source_target_pairs={{0,1},{1,0},{2,3},{3,2},{4,5},{5,4},{6,7},{7,6},{8,9},{9,8},{10,11... | collective-permute-start | bytes 221192 | tf_op jit(solution)/shard_map/ppermute | solution.py:80
  23.0 8.6 %collective-permute-start.6 = (bf16[256,256]{1,0:T(8,128)(2,1)S(1)}, bf16[256,256]{1,0:T(8,128)(2,1)S(1)}, u32[]{:S(2)}, u32[]{:S(2)}) collective-permute-start(bf16[256,256]{1,0:T(8,128)(2,1)S(1)} %get-tuple-element.30), channel_id=1, source_target_pairs={{0,16},{4,20},{8,24},{12,28},{16,0},{20,4},{24,8},{28,12},{1,17},{... | collective-permute-start | bytes 393224 | tf_op jit(solution)/shard_map/ppermute | solution.py:70
  25.8 1.3 %collective-permute-start.9 = (bf16[144,256]{1,0:T(8,128)(2,1)S(1)}, bf16[144,256]{1,0:T(8,128)(2,1)S(1)}, u32[]{:S(2)}, u32[]{:S(2)}) collective-permute-start(bf16[144,256]{1,0:T(8,128)(2,1)S(1)} %shard_map.104.own_ref), channel_id=1, source_target_pairs={{0,1},{1,0},{2,3},{3,2},{4,5},{5,4},{6,7},{7,6},{8,9},{9,8},{10,11... | collective-permute-start | bytes 221192 | tf_op jit(solution)/shard_map/ppermute | solution.py:70

commit v9 on v8

--- a/solution.py
+++ b/solution.py
@@ -472,7 +472,7 @@
             flops=2 * scenarios * sep_rows * sep_rows * 2,
         )
         solved.append(z)
-        received = exchange(message, 2 << now)
+        received = exchange(message, (3 if now + 2 == levels else 2) << now)
     below = levels - 1
     triples, shapes = (), []
     for now in range(below):

time: 33.7 us -> 32.9 us (0.976)
  waiting for transfers between devices: 13.7 us -> 11.9 us
  starting transfers between devices: 10.5 us -> 11.5 us
    ppermute x8, waiting for transfers between devices: 12.8 us -> 11 us  [exchange(): lax.ppermute(block, axis, [(i, i ^ distance) for i in range(lax.axis_size...]
    ppermute x8, starting transfers between devices: 9.62 us -> 10.6 us  [exchange(): lax.ppermute(block, axis, [(i, i ^ distance) for i in range(lax.axis_size...]
  transfers between devices with their start and end apart: 10 -> 10, of which waited for: 7 -> 7; matrix products, arithmetic and copies ran while one was open for 0% -> 0% of each run, Pallas kernels for 15% -> 16%
where the time goes in v9:
time: 32.9 us; the launch traced here: 32.7 us
  waiting for transfers between devices  11.9 us (36%)
  starting transfers between devices  11.5 us (35%)
  Pallas kernels  8.56 us (26%)
  between operations  0.74 us (2%)
    ppermute x8, waiting for transfers between devices, exchange(): lax.ppermute(block, axis, [(i, i ^ distance) for i in range(lax.axis_size...  11 us
    ppermute x8, starting transfers between devices, exchange(): lax.ppermute(block, axis, [(i, i ^ distance) for i in range(lax.axis_size...  10.6 us
    pallas_call x13, Pallas kernels, call(): pl.pallas_call(kernel, out_shape=outs, in_specs=[pl.BlockSpec(memory_spac...  8.56 us
    ppermute x2, waiting for transfers between devices, exchange_among(): return lax.ppermute(block, ('leaf', 'rhs'), route)  0.92 us
    ppermute x2, starting transfers between devices, exchange_among(): return lax.ppermute(block, ('leaf', 'rhs'), route)  0.85 us
  transfers between devices with their start and end apart: 10, of which 7 were waited for; matrix products, arithmetic and copies ran while one was open for 0% of the time, Pallas kernels for 16%

profile of v9, /device:TPU:0, one launch (start us, length us, event | category | flops | bytes accessed | tf_op | source)
XLA Modules:
  0.0 32.7 jit_solution(16403776439604043924)
XLA Ops:
  0.6 1.1 %shard_map.95.carry_ref.own_ref.refs_0_ = bf16[144,512]{1,0:T(8,128)(2,1)S(1)} custom-call(s32[1,3]{1,0:T(1,128)} %sep_panel_hbm.1, s32[1,3]{1,0:T(1,128)} %leaf_panel_hbm.1, bf16[256,256]{1,0:T(8,128)(2,1)} %sep_inverse_hbm.1, bf16[3,256,128]{2,1,0:T(8,128)(2,1)} %bitcast.3), custom_call_target="tpu_custom_call" | custom-call | bytes 475160 | tf_op jit(solution)/shard_map/pallas_call | solution.py:53
  1.7 3.0 %collective-permute-start.1 = (bf16[144,512]{1,0:T(8,128)(2,1)S(1)}, bf16[144,512]{1,0:T(8,128)(2,1)S(1)}, u32[]{:S(2)}, u32[]{:S(2)}) collective-permute-start(bf16[144,512]{1,0:T(8,128)(2,1)S(1)} %shard_map.95.carry_ref.own_ref.refs_0_), channel_id=1, source_target_pairs={{0,4},{4,0},{8,12},{12,8},{16,20},{20,16},{24,28},{28,24},{1,5},{5... | collective-permute-start | bytes 442376 | tf_op jit(solution)/shard_map/ppermute | solution.py:70
  4.7 2.6 %shard_map.96 = (bf16[1024,1024]{1,0:T(8,128)(2,1)S(1)}, bf16[3,1024,128]{2,1,0:T(8,128)(2,1)S(1)}, f32[256,1024]{1,0:T(8,128)S(1)}, f32[256,768]{1,0:T(8,128)S(1)}, bf16[256,512]{1,0:T(8,128)(2,1)S(1)}) custom-call(bf16[144,512]{1,0:T(8,128)(2,1)S(1)} %shard_map.95.carry_ref.own_ref.refs_0_, bf16[256,1024]{1,0:T(8,128)(2,1)} %rhs_hbm.1, ...), custom_call_target="tpu_custom_call" | custom-call | flops 738197504 | bytes 8667136 | tf_op jit(solution)/shard_map/pallas_call | solution.py:53
  7.4 0.1 collective-permute-start
  7.5 1.1 %collective-permute-done.1.received_ref.refs_0_ = bf16[144,512]{1,0:T(8,128)(2,1)S(1)} collective-permute-done((bf16[144,512]{1,0:T(8,128)(2,1)S(1)}, bf16[144,512]{1,0:T(8,128)(2,1)S(1)}, u32[]{:S(2)}, u32[]{:S(2)}) %collective-permute-start.1) | collective-permute-done | bytes 147488 | tf_op jit(solution)/shard_map/ppermute | solution.py:70
  8.6 0.1 collective-permute-start.2
  8.7 1.9 %collective-permute-start.3 = (bf16[144,384]{1,0:T(8,128)(2,1)S(1)}, bf16[144,384]{1,0:T(8,128)(2,1)S(1)}, u32[]{:S(2)}, u32[]{:S(2)}) collective-permute-start(bf16[144,384]{1,0:T(8,128)(2,1)S(1)} %shard_map.97.refs_0_.own_ref), channel_id=1, source_target_pairs={{0,8},{4,12},{8,0},{12,4},{16,24},{20,28},{24,16},{28,20},{1,9},{5... | collective-permute-start | bytes 331784 | tf_op jit(solution)/shard_map/ppermute | solution.py:70
  10.6 1.4 %shard_map.99 = (f32[256,1024]{1,0:T(8,128)S(1)}, bf16[384,1024]{1,0:T(8,128)(2,1)S(1)}) custom-call(f32[256,1024]{1,0:T(8,128)S(1)} %get-tuple-element.23.solved_ref, bf16[3,1024,128]{2,1,0:T(8,128)(2,1)S(1)} %get-tuple-element.24.update_ref, bf16[1024,1024]{1,0:T(8,128)(2,1)S(1)} %get-tuple-element.25.inverse_ref), custom_call_target="tpu_custom_call" | custom-call | flops 1476395008 | bytes 5767168 | tf_op jit(solution)/shard_map/pallas_call | solution.py:53
  12.0 2.2 %collective-permute-done.3.refs_2_.received_ref = bf16[144,384]{1,0:T(8,128)(2,1)S(1)} collective-permute-done((bf16[144,384]{1,0:T(8,128)(2,1)S(1)}, bf16[144,384]{1,0:T(8,128)(2,1)S(1)}, u32[]{:S(2)}, u32[]{:S(2)}) %collective-permute-start.3) | collective-permute-done | bytes 110624 | tf_op jit(solution)/shard_map/ppermute | solution.py:70
  14.2 1.0 %collective-permute-done.received_ref = bf16[256,512]{1,0:T(8,128)(2,1)S(1)} collective-permute-done((bf16[256,512]{1,0:T(8,128)(2,1)S(1)}, bf16[256,512]{1,0:T(8,128)(2,1)S(1)}, u32[]{:S(2)}, u32[]{:S(2)}) %collective-permute-start) | collective-permute-done | bytes 262176 | tf_op jit(solution)/shard_map/ppermute | solution.py:70
  15.2 0.0 collective-permute-done.2.other_ref.refs_1_
  15.2 0.4 %shard_map.100 = (f32[256,256]{1,0:T(8,128)S(1)}, f32[256,512]{1,0:T(8,128)S(1)}, bf16[256,512]{1,0:T(8,128)(2,1)S(1)}) custom-call(f32[256,768]{1,0:T(8,128)S(1)} %get-tuple-element.21.own_ref, bf16[256,512]{1,0:T(8,128)(2,1)S(1)} %collective-permute-done.received_ref, bf16[144,512]{1,0:T(8,128)(2,1)S(1)} %shard_map.98.factor_ref.refs_0_.refs_7_, ...), custom_call_target="tpu_custom_call" | custom-call | flops 67108864 | bytes 3436544 | tf_op jit(solution)/shard_map/pallas_call | solution.py:53
  15.6 1.6 %collective-permute-start.4 = (bf16[256,512]{1,0:T(8,128)(2,1)S(1)}, bf16[256,512]{1,0:T(8,128)(2,1)S(1)}, u32[]{:S(2)}, u32[]{:S(2)}) collective-permute-start(bf16[256,512]{1,0:T(8,128)(2,1)S(1)} %get-tuple-element.28), channel_id=1, source_target_pairs={{0,8},{4,12},{8,0},{12,4},{16,24},{20,28},{24,16},{28,20},{1,9},{5... | collective-permute-start | bytes 786440 | tf_op jit(solution)/shard_map/ppermute | solution.py:70
  17.3 0.1 collective-permute-start.5
  17.4 0.5 %collective-permute-start.7 = (bf16[144,256]{1,0:T(8,128)(2,1)S(1)}, bf16[144,256]{1,0:T(8,128)(2,1)S(1)}, u32[]{:S(2)}, u32[]{:S(2)}) collective-permute-start(bf16[144,256]{1,0:T(8,128)(2,1)S(1)} %shard_map.101.refs_0_.own_ref), channel_id=1, source_target_pairs={{0,1},{1,0},{2,3},{3,2},{4,5},{5,4},{6,7},{7,6},{8,16},{9,17},{10,... | collective-permute-start | bytes 221192 | tf_op jit(solution)/shard_map/ppermute | solution.py:80
  17.9 0.9 %collective-permute-done.7.received_ref = bf16[144,256]{1,0:T(8,128)(2,1)S(1)} collective-permute-done((bf16[144,256]{1,0:T(8,128)(2,1)S(1)}, bf16[144,256]{1,0:T(8,128)(2,1)S(1)}, u32[]{:S(2)}, u32[]{:S(2)}) %collective-permute-start.7) | collective-permute-done | bytes 73760 | tf_op jit(solution)/shard_map/ppermute | solution.py:80
  18.8 0.4 %collective-permute-start.8 = (bf16[144,256]{1,0:T(8,128)(2,1)S(1)}, bf16[144,256]{1,0:T(8,128)(2,1)S(1)}, u32[]{:S(2)}, u32[]{:S(2)}) collective-permute-start(bf16[144,256]{1,0:T(8,128)(2,1)S(1)} %collective-permute-done.7.received_ref), channel_id=1, source_target_pairs={{0,1},{1,0},{2,3},{3,2},{4,5},{5,4},{6,7},{7,6},{8,9},{9,8},{10,11... | collective-permute-start | bytes 221192 | tf_op jit(solution)/shard_map/ppermute | solution.py:80
  19.1 0.0 collective-permute-done.5.other_ref.refs_4_
  19.1 3.5 %collective-permute-done.4.received_ref = bf16[256,512]{1,0:T(8,128)(2,1)S(1)} collective-permute-done((bf16[256,512]{1,0:T(8,128)(2,1)S(1)}, bf16[256,512]{1,0:T(8,128)(2,1)S(1)}, u32[]{:S(2)}, u32[]{:S(2)}) %collective-permute-start.4) | collective-permute-done | bytes 262176 | tf_op jit(solution)/shard_map/ppermute | solution.py:70
  22.6 0.4 %shard_map.103 = (f32[256,256]{1,0:T(8,128)S(1)}, f32[256,256]{1,0:T(8,128)S(1)}, bf16[256,256]{1,0:T(8,128)(2,1)S(1)}) custom-call(f32[256,512]{1,0:T(8,128)S(1)} %get-tuple-element.27.own_ref, bf16[256,512]{1,0:T(8,128)(2,1)S(1)} %collective-permute-done.4.received_ref, bf16[144,384]{1,0:T(8,128)(2,1)S(1)} %shard_map.102.factor_ref.refs_3_.refs_8_, ...), custom_call_target="tpu_custom_call" | custom-call | flops 67108864 | bytes 1662976 | tf_op jit(solution)/shard_map/pallas_call | solution.py:53
  23.0 3.8 %collective-permute-start.6 = (bf16[256,256]{1,0:T(8,128)(2,1)S(1)}, bf16[256,256]{1,0:T(8,128)(2,1)S(1)}, u32[]{:S(2)}, u32[]{:S(2)}) collective-permute-start(bf16[256,256]{1,0:T(8,128)(2,1)S(1)} %get-tuple-element.30), channel_id=1, source_target_pairs={{0,24},{4,28},{8,16},{12,20},{16,8},{20,12},{24,0},{28,4},{1,25},{... | collective-permute-start | bytes 393224 | tf_op jit(solution)/shard_map/ppermute | solution.py:70
  26.8 0.0 collective-permute-done.8.passed_ref
  26.8 0.1 collective-permute-start.9
  26.9 1.3 %collective-permute-done.9.other_ref = bf16[144,256]{1,0:T(8,128)(2,1)S(1)} collective-permute-done((bf16[144,256]{1,0:T(8,128)(2,1)S(1)}, bf16[144,256]{1,0:T(8,128)(2,1)S(1)}, u32[]{:S(2)}, u32[]{:S(2)}) %collective-permute-start.9) | collective-permute-done | bytes 73760 | tf_op jit(solution)/shard_map/ppermute | solution.py:70
  28.2 0.2 shard_map.105
  28.4 0.4 %shard_map.106 = (f32[256,256]{1,0:T(8,128)S(1)}, bf16[256,256]{1,0:T(8,128)(2,1)S(1)}, f32[256,256]{1,0:T(8,128)S(1)}, bf16[128,256]{1,0:T(8,128)(2,1)S(1)}) custom-call(bf16[144,512]{1,0:T(8,128)(2,1)S(1)} %shard_map.98.factor_ref.refs_0_.refs_7_, bf16[144,512]{1,0:T(8,128)(2,1)S(1)} %collective-permute-done.2.other_ref.refs_1_, ...), custom_call_target="tpu_custom_call" | custom-call | flops 201326592 | bytes 1761280 | tf_op jit(solution)/shard_map/pallas_call | solution.py:53
  28.8 1.9 %collective-permute-done.6.refs_2_ = bf16[256,256]{1,0:T(8,128)(2,1)S(1)} collective-permute-done((bf16[256,256]{1,0:T(8,128)(2,1)S(1)}, bf16[256,256]{1,0:T(8,128)(2,1)S(1)}, u32[]{:S(2)}, u32[]{:S(2)}) %collective-permute-start.6) | collective-permute-done | bytes 131104 | tf_op jit(solution)/shard_map/ppermute | solution.py:70
  30.8 1.9 %shard_map.107 = (f32[256,1024]{1,0:T(8,128)}, f32[256,256]{1,0:T(8,128)}) custom-call(bf16[144,512]{1,0:T(8,128)(2,1)S(1)} %shard_map.95.carry_ref.own_ref.refs_0_, f32[256,256]{1,0:T(8,128)S(1)} %get-tuple-element.29.refs_1_, bf16[256,256]{1,0:T(8,128)(2,1)S(1)} %collective-permute-done.6.refs_2_, f32[256,1024]{1,0:T(8,128)S(1)} %get-tuple-element.31.refs_3_, ...), custom_call_target="tpu_custom_call" | custom-call | flops 738197504 | bytes 4927488 | tf_op jit(solution)/shard_map/pallas_call | solution.py:53
  (5 shorter events, 0.1 us)
Async XLA Ops:
  1.7 6.9 %collective-permute-start.1 = (bf16[144,512]{1,0:T(8,128)(2,1)S(1)}, bf16[144,512]{1,0:T(8,128)(2,1)S(1)}, u32[]{:S(2)}, u32[]{:S(2)}) collective-permute-start(bf16[144,512]{1,0:T(8,128)(2,1)S(1)} %shard_map.95.carry_ref.own_ref.refs_0_), channel_id=1, source_target_pairs={{0,4},{4,0},{8,12},{12,8},{16,20},{20,16},{24,28},{28,24},{1,5},{5... | collective-permute-start | bytes 442376 | tf_op jit(solution)/shard_map/ppermute | solution.py:70
  7.4 7.8 %collective-permute-start = (bf16[256,512]{1,0:T(8,128)(2,1)S(1)}, bf16[256,512]{1,0:T(8,128)(2,1)S(1)}, u32[]{:S(2)}, u32[]{:S(2)}) collective-permute-start(bf16[256,512]{1,0:T(8,128)(2,1)S(1)} %get-tuple-element.22), channel_id=1, source_target_pairs={{0,4},{4,0},{8,12},{12,8},{16,20},{20,16},{24,28},{28,24},{1,5},{5... | collective-permute-start | bytes 786440 | tf_op jit(solution)/shard_map/ppermute | solution.py:70
  8.6 6.6 %collective-permute-start.2 = (bf16[144,512]{1,0:T(8,128)(2,1)S(1)}, bf16[144,512]{1,0:T(8,128)(2,1)S(1)}, u32[]{:S(2)}, u32[]{:S(2)}) collective-permute-start(bf16[144,512]{1,0:T(8,128)(2,1)S(1)} %shard_map.98.factor_ref.refs_0_.refs_7_), channel_id=1, source_target_pairs={{0,1},{1,0},{2,3},{3,2},{4,5},{5,4},{6,7},{7,6},{8,9},{9,8},{10,11... | collective-permute-start | bytes 442376 | tf_op jit(solution)/shard_map/ppermute | solution.py:70
  8.7 5.5 %collective-permute-start.3 = (bf16[144,384]{1,0:T(8,128)(2,1)S(1)}, bf16[144,384]{1,0:T(8,128)(2,1)S(1)}, u32[]{:S(2)}, u32[]{:S(2)}) collective-permute-start(bf16[144,384]{1,0:T(8,128)(2,1)S(1)} %shard_map.97.refs_0_.own_ref), channel_id=1, source_target_pairs={{0,8},{4,12},{8,0},{12,4},{16,24},{20,28},{24,16},{28,20},{1,9},{5... | collective-permute-start | bytes 331784 | tf_op jit(solution)/shard_map/ppermute | solution.py:70
  15.6 7.0 %collective-permute-start.4 = (bf16[256,512]{1,0:T(8,128)(2,1)S(1)}, bf16[256,512]{1,0:T(8,128)(2,1)S(1)}, u32[]{:S(2)}, u32[]{:S(2)}) collective-permute-start(bf16[256,512]{1,0:T(8,128)(2,1)S(1)} %get-tuple-element.28), channel_id=1, source_target_pairs={{0,8},{4,12},{8,0},{12,4},{16,24},{20,28},{24,16},{28,20},{1,9},{5... | collective-permute-start | bytes 786440 | tf_op jit(solution)/shard_map/ppermute | solution.py:70
  17.3 1.8 %collective-permute-start.5 = (bf16[144,384]{1,0:T(8,128)(2,1)S(1)}, bf16[144,384]{1,0:T(8,128)(2,1)S(1)}, u32[]{:S(2)}, u32[]{:S(2)}) collective-permute-start(bf16[144,384]{1,0:T(8,128)(2,1)S(1)} %shard_map.102.factor_ref.refs_3_.refs_8_), channel_id=1, source_target_pairs={{0,1},{1,0},{2,3},{3,2},{4,5},{5,4},{6,7},{7,6},{8,9},{9,8},{10,11... | collective-permute-start | bytes 331784 | tf_op jit(solution)/shard_map/ppermute | solution.py:70
  17.4 1.4 %collective-permute-start.7 = (bf16[144,256]{1,0:T(8,128)(2,1)S(1)}, bf16[144,256]{1,0:T(8,128)(2,1)S(1)}, u32[]{:S(2)}, u32[]{:S(2)}) collective-permute-start(bf16[144,256]{1,0:T(8,128)(2,1)S(1)} %shard_map.101.refs_0_.own_ref), channel_id=1, source_target_pairs={{0,1},{1,0},{2,3},{3,2},{4,5},{5,4},{6,7},{7,6},{8,16},{9,17},{10,... | collective-permute-start | bytes 221192 | tf_op jit(solution)/shard_map/ppermute | solution.py:80
  18.8 8.0 %collective-permute-start.8 = (bf16[144,256]{1,0:T(8,128)(2,1)S(1)}, bf16[144,256]{1,0:T(8,128)(2,1)S(1)}, u32[]{:S(2)}, u32[]{:S(2)}) collective-permute-start(bf16[144,256]{1,0:T(8,128)(2,1)S(1)} %collective-permute-done.7.received_ref), channel_id=1, source_target_pairs={{0,1},{1,0},{2,3},{3,2},{4,5},{5,4},{6,7},{7,6},{8,9},{9,8},{10,11... | collective-permute-start | bytes 221192 | tf_op jit(solution)/shard_map/ppermute | solution.py:80
  23.0 7.8 %collective-permute-start.6 = (bf16[256,256]{1,0:T(8,128)(2,1)S(1)}, bf16[256,256]{1,0:T(8,128)(2,1)S(1)}, u32[]{:S(2)}, u32[]{:S(2)}) collective-permute-start(bf16[256,256]{1,0:T(8,128)(2,1)S(1)} %get-tuple-element.30), channel_id=1, source_target_pairs={{0,24},{4,28},{8,16},{12,20},{16,8},{20,12},{24,0},{28,4},{1,25},{... | collective-permute-start | bytes 393224 | tf_op jit(solution)/shard_map/ppermute | solution.py:70
  26.8 1.3 %collective-permute-start.9 = (bf16[144,256]{1,0:T(8,128)(2,1)S(1)}, bf16[144,256]{1,0:T(8,128)(2,1)S(1)}, u32[]{:S(2)}, u32[]{:S(2)}) collective-permute-start(bf16[144,256]{1,0:T(8,128)(2,1)S(1)} %shard_map.104.own_ref), channel_id=1, source_target_pairs={{0,1},{1,0},{2,3},{3,2},{4,5},{5,4},{6,7},{7,6},{8,9},{9,8},{10,11... | collective-permute-start | bytes 221192 | tf_op jit(solution)/shard_map/ppermute | solution.py:70
